TPU v7x, 32 devices: a whole 2x2x4 slice. The times are simulated.
32 devices in a mesh: freq: 4 (over y, core), tm: 8 (over z, x).
Axes of the slice: x: 2, y: 2, z: 4, core: 2. Of those that a mesh axis runs over, the one named last changes fastest.
Arguments:
- patches: bfloat16 [12, 832, 256], P('freq', 'tm')
- column_mask: int32 [832], replicated, may hold values from 0 to 1, as said below
- labels: int32 [8, 527], replicated, may hold values 0 or 1
- clip_weights: int32 [8], replicated, may hold values from 1 to 3
- wide_weights: float32 [2, 768, 6144], P(None, 'tm')
- down_weights: float32 [2, 3072, 768], P(None, 'tm'), may hold values from -0.109375 to 0.109375
- embedding: float32 [1504, 768], P(None, 'tm')
- classifier: float32 [768, 527], P('tm'), may hold values from -0.21875 to 0.21875
- vectors: float32 [29, 768], P(None, 'tm')
- class_bias: float32 [527], replicated, may hold values from -3 to 3
- wide_first: float32 [2, 768, 6144], P(None, 'tm'), may hold values from -0.00390625 to 0.00390625
- down_first: float32 [2, 3072, 768], P(None, 'tm'), may hold values from -0.00390625 to 0.00390625
- embedding_first: float32 [1504, 768], P(None, 'tm'), may hold values from -0.00390625 to 0.00390625
- classifier_first: float32 [768, 527], P('tm'), may hold values from -0.00390625 to 0.00390625
- vectors_first: float32 [29, 768], P(None, 'tm'), may hold values from -0.03125 to 0.03125
- bias_first: float32 [527], replicated, may hold values from -0.03125 to 0.03125
- wide_second: float32 [2, 768, 6144], P(None, 'tm'), may hold values from 6.353893e-08 to 2.541557e-07
- down_second: float32 [2, 3072, 768], P(None, 'tm'), may hold values from 6.353893e-08 to 2.541557e-07
- embedding_second: float32 [1504, 768], P(None, 'tm'), may hold values from 6.353893e-08 to 2.541557e-07
- classifier_second: float32 [768, 527], P('tm'), may hold values from 6.353893e-08 to 2.541557e-07
- vectors_second: float32 [29, 768], P(None, 'tm'), may hold values from 4.0664913e-06 to 1.6265965e-05
- bias_second: float32 [527], replicated, may hold values from 4.0664913e-06 to 1.6265965e-05
Outputs:
- wide_new: float32 [2, 768, 6144], P(None, 'tm')
- down_new: float32 [2, 3072, 768], P(None, 'tm')
- embedding_new: float32 [1504, 768], P(None, 'tm')
- classifier_new: float32 [768, 527], P('tm')
- vectors_new: float32 [29, 768], P(None, 'tm')
- bias_new: float32 [527], replicated
- wide_first_new: float32 [2, 768, 6144], P(None, 'tm')
- down_first_new: float32 [2, 3072, 768], P(None, 'tm')
- embedding_first_new: float32 [1504, 768], P(None, 'tm')
- classifier_first_new: float32 [768, 527], P('tm')
- vectors_first_new: float32 [29, 768], P(None, 'tm')
- bias_first_new: float32 [527], replicated
- wide_second_new: float32 [2, 768, 6144], P(None, 'tm')
- down_second_new: float32 [2, 3072, 768], P(None, 'tm')
- embedding_second_new: float32 [1504, 768], P(None, 'tm')
- classifier_second_new: float32 [768, 527], P('tm')
- vectors_second_new: float32 [29, 768], P(None, 'tm')
- bias_second_new: float32 [527], replicated
- wide_copy: bfloat16 [2, 768, 6144], P(None, 'tm')
- down_copy: bfloat16 [2, 3072, 768], P(None, 'tm')
- embedding_copy: bfloat16 [1504, 768], P(None, 'tm')
- classifier_copy: bfloat16 [768, 527], P('tm')
- grad_norm: float32 [], replicated
- loss_sum: float32 [], replicated
- weight_total: float32 [], replicated
Inputs may be any that keep to these rules, and one draw needn't show every extreme that they name: `column_mask`: each clip's columns are live for its first columns and dead after them, with 64 to 101 live columns; in every draw some clip has exactly 101.
All inputs are finite; a program needn't handle non-finite values.
Results may differ from a plain program's by a relative error of at most 0.0055.
The roundings to bfloat16 on the way count: a program that leaves them out, or rounds other values in their place, can miss the bound.
Values may be sent and summed in bfloat16 or wider, within the bound.
A program may use at most 320 MiB of HBM per device.

v0:
```python
import jax
import jax.numpy as jnp
from jax import lax
from jax.sharding import PartitionSpec as P

D = 768
HEADS = 12
FF = 3072
L = 2
FROWS = 12
HALF = 52
PATCH = 256
STEP = 5
CPD = 2


DECAY_FIRST = 0.5
DECAY_SECOND = 0.5
LEARN_RATE = 0.03
WEIGHT_DECAY = 0.05
EPSILON = 1e-08


def swapped(block, axis, distance):
    count = lax.axis_size(axis)
    route = []
    for low in range(count):
        high = low | 1 << distance
        if high != low and high < count:
            route += [(low, high), (high, low)]
    return lax.ppermute(block, axis, route)


def norm_rows(x):
    center = jnp.mean(x, -1, keepdims=True)
    shifted = x - center
    scale = lax.rsqrt(jnp.mean(shifted * shifted, -1, keepdims=True) + 1e-06)
    return (shifted * scale, scale)


def norm_back(dnorm, normed, scale):
    return scale * (
        dnorm
        - jnp.mean(dnorm, -1, keepdims=True)
        - normed * jnp.mean(dnorm * normed, -1, keepdims=True)
    )


def gelu_parts(before):
    lower = 0.5 * (1.0 + lax.erf(before * 0.7071067811865476))
    return (before * lower, lower + before * jnp.exp(-0.5 * before * before) * 0.3989422804014327)


def matmul(left, right):
    return jnp.dot(left, right, preferred_element_type=jnp.float32)


def row_total(value):
    return jnp.sum(value.astype(jnp.float32), (0, 1))


def split_heads(query, allkv):
    clips, rows, width = query.shape
    depth = width // HEADS
    query_heads = query.reshape(clips, rows, HEADS, depth)
    key_heads = allkv[..., :width].reshape(clips, -1, HEADS, depth)
    value_heads = allkv[..., width:].reshape(clips, -1, HEADS, depth)
    return (query_heads, key_heads, value_heads, depth ** (-0.5))


def scores_of(query_heads, key_heads, keymask, scale):
    scores = (
        jnp.einsum("cqhd,ckhd->chqk", query_heads, key_heads, preferred_element_type=jnp.float32)
        * scale
    )
    return jnp.where(keymask[:, None, None, :], scores, -1e30)


def attend(query, allkv, keymask):
    query_heads, key_heads, value_heads, scale = split_heads(query, allkv)
    scores = scores_of(query_heads, key_heads, keymask, scale)
    top = jnp.max(scores, -1, keepdims=True)
    expo = jnp.exp(scores - top)
    total = jnp.sum(expo, -1, keepdims=True)
    probs = (expo / total).astype(jnp.bfloat16)
    mixed = jnp.einsum("chqk,ckhd->cqhd", probs, value_heads, preferred_element_type=jnp.float32)
    return (mixed.reshape(query.shape).astype(jnp.bfloat16), top + jnp.log(total))


def attend_back(dmixed, query, allkv, keymask, logsum):
    query_heads, key_heads, value_heads, scale = split_heads(query, allkv)
    probs = jnp.exp(scores_of(query_heads, key_heads, keymask, scale) - logsum)
    dout_heads = dmixed.reshape(query_heads.shape)
    dprob = jnp.einsum(
        "cqhd,ckhd->chqk", dout_heads, value_heads, preferred_element_type=jnp.float32
    )
    dscore = (probs * (dprob - jnp.sum(probs * dprob, -1, keepdims=True))).astype(jnp.bfloat16)
    dquery = (
        jnp.einsum("chqk,ckhd->cqhd", dscore, key_heads, preferred_element_type=jnp.float32) * scale
    )
    dkey = (
        jnp.einsum("chqk,cqhd->ckhd", dscore, query_heads, preferred_element_type=jnp.float32)
        * scale
    )
    dvalue = jnp.einsum(
        "chqk,cqhd->ckhd",
        probs.astype(jnp.bfloat16),
        dout_heads,
        preferred_element_type=jnp.float32,
    )
    width = query.shape[-1]
    dkeyval = jnp.concatenate(
        [dkey.reshape(dkey.shape[0], -1, width), dvalue.reshape(dvalue.shape[0], -1, width)], -1
    )
    return (dquery.reshape(query.shape), dkeyval)


def layer_forward(x, wide, downward, rows, up_bias, keymask):
    width = x.shape[-1]
    normed_one, scale_one = norm_rows(x)
    act_one = (normed_one * rows[0] + rows[1]).astype(jnp.bfloat16)
    joined = matmul(act_one, wide[:, : 3 * width])
    query = (joined[..., :width] + rows[4]).astype(jnp.bfloat16)
    keyval = jnp.concatenate(
        [joined[..., width : 2 * width], joined[..., 2 * width :] + rows[5]], -1
    ).astype(jnp.bfloat16)
    gathered = lax.all_gather(keyval, "freq", axis=1, tiled=True)
    partner = swapped(gathered, "tm", 0)
    allkv = jnp.concatenate([gathered, partner], 1)
    mixed, logsum = attend(query, allkv, keymask)
    resid = x + matmul(mixed, wide[:, 3 * width : 4 * width]) + rows[6]
    normed_two, scale_two = norm_rows(resid)
    act_two = (normed_two * rows[2] + rows[3]).astype(jnp.bfloat16)
    before = matmul(act_two, wide[:, 4 * width :]) + up_bias
    hidden = gelu_parts(before)[0].astype(jnp.bfloat16)
    out = resid + matmul(hidden, downward) + rows[7]
    return (
        out,
        (
            normed_one,
            scale_one,
            act_one,
            query,
            allkv,
            logsum,
            mixed,
            normed_two,
            scale_two,
            act_two,
            before,
            hidden,
        ),
    )


def layer_backward(dout, kept, wide, downward, rows, keymask):
    (
        normed_one,
        scale_one,
        act_one,
        query,
        allkv,
        logsum,
        mixed,
        normed_two,
        scale_two,
        act_two,
        before,
        hidden,
    ) = kept
    width = dout.shape[-1]
    dout_low = dout.astype(jnp.bfloat16)
    grad_down = jnp.einsum("crf,crd->fd", hidden, dout_low, preferred_element_type=jnp.float32)
    dhidden = jnp.einsum("crd,fd->crf", dout_low, downward, preferred_element_type=jnp.float32)
    dbefore = dhidden * gelu_parts(before)[1]
    dbefore_low = dbefore.astype(jnp.bfloat16)
    grad_up = jnp.einsum("crd,crf->df", act_two, dbefore_low, preferred_element_type=jnp.float32)
    dact_two = jnp.einsum(
        "crf,df->crd", dbefore_low, wide[:, 4 * width :], preferred_element_type=jnp.float32
    )
    dresid = dout + norm_back(dact_two * rows[2], normed_two, scale_two)
    dresid_low = dresid.astype(jnp.bfloat16)
    grad_out = jnp.einsum("crd,cre->de", mixed, dresid_low, preferred_element_type=jnp.float32)
    dmixed = jnp.einsum(
        "cre,de->crd",
        dresid_low,
        wide[:, 3 * width : 4 * width],
        preferred_element_type=jnp.float32,
    ).astype(jnp.bfloat16)
    dquery, dkeyval = attend_back(dmixed, query, allkv, keymask, logsum)
    middle = dkeyval.shape[1] // 2
    returned = swapped(dkeyval[:, middle:], "tm", 0)
    dlocal = lax.psum_scatter(
        dkeyval[:, :middle] + returned, "freq", scatter_dimension=1, tiled=True
    )
    dfused = jnp.concatenate([dquery, dlocal], -1).astype(jnp.bfloat16)
    grad_joined = jnp.einsum("crd,cre->de", act_one, dfused, preferred_element_type=jnp.float32)
    dact_one = jnp.einsum(
        "cre,de->crd", dfused, wide[:, : 3 * width], preferred_element_type=jnp.float32
    )
    dinput = dresid + norm_back(dact_one * rows[0], normed_one, scale_one)
    grad_rows = jnp.stack(
        [
            row_total(dact_one * normed_one),
            row_total(dact_one),
            row_total(dact_two * normed_two),
            row_total(dact_two),
            row_total(dfused[..., :width]),
            row_total(dfused[..., 2 * width :]),
            row_total(dresid),
            row_total(dout),
        ]
    )
    grad_wide = jnp.concatenate([grad_joined, grad_out, grad_up], -1)
    return (dinput, grad_wide, grad_down, grad_rows, row_total(dbefore))


def adam(weight, first, second, grad):
    first = DECAY_FIRST * first + (1.0 - DECAY_FIRST) * grad
    second = DECAY_SECOND * second + (1.0 - DECAY_SECOND) * grad * grad
    fix_one = 1.0 - DECAY_FIRST**STEP
    fix_two = 1.0 - DECAY_SECOND**STEP
    weight = weight - LEARN_RATE * (
        first / fix_one / (jnp.sqrt(second / fix_two) + EPSILON) + WEIGHT_DECAY * weight
    )
    return (weight, first, second)


def local(
    patches,
    column_mask,
    labels,
    clip_weights,
    wide_weights,
    down_weights,
    embedding,
    classifier,
    vectors,
    class_bias,
    wide_first,
    down_first,
    embedding_first,
    classifier_first,
    vectors_first,
    bias_first,
    wide_second,
    down_second,
    embedding_second,
    classifier_second,
    vectors_second,
    bias_second,
):
    freq_count = lax.axis_size("freq")
    time_count = lax.axis_size("tm")
    freq_index = lax.axis_index("freq")
    time_index = lax.axis_index("tm")
    half = time_index % 2
    pair = time_index // 2
    rows_dev = FROWS // freq_count
    spread_rows = FF // D
    glob = L * 8 + L * spread_rows
    ngrid = FROWS * 2 * HALF
    columns = column_mask.reshape(time_count, CPD, HALF) > 0

    def half_columns(index):
        return lax.dynamic_index_in_dim(columns, index, 0, keepdims=False)

    mine_columns = half_columns(time_index)
    other_columns = half_columns(time_index + 1 - 2 * half)
    pixels = patches.astype(jnp.float32).reshape(rows_dev, CPD, HALF, PATCH).transpose(1, 0, 2, 3)
    live = mine_columns.astype(jnp.float32)[:, None, :, None]
    total, squares, count = lax.psum(
        (
            jnp.sum(pixels * live),
            jnp.sum(pixels * pixels * live),
            jnp.sum(live) * (rows_dev * PATCH),
        ),
        ("freq", "tm"),
    )
    center = total / count
    mel_scale = lax.rsqrt(squares / count - center * center + 1e-05)
    pnorm = (
        ((pixels - center) * mel_scale).astype(jnp.bfloat16).reshape(CPD, rows_dev * HALF, PATCH)
    )
    wide_all, down_all, embed_all, class_all, vec_all = (
        lax.all_gather(wide_weights.astype(jnp.bfloat16), "tm", axis=1, tiled=True),
        lax.all_gather(down_weights.astype(jnp.bfloat16), "tm", axis=1, tiled=True),
        lax.all_gather(embedding.astype(jnp.bfloat16), "tm", axis=1, tiled=True),
        lax.all_gather(classifier.astype(jnp.bfloat16), "tm", axis=0, tiled=True),
        lax.all_gather(vectors.astype(jnp.bfloat16), "tm", axis=1, tiled=True),
    )

    def slot_valid(freq_source, own_half, cols):
        special = jnp.logical_and(freq_source == 0, own_half)
        return jnp.concatenate(
            [jnp.broadcast_to(special, (CPD, 2)), jnp.tile(cols, (1, rows_dev))], 1
        )

    keymask = jnp.concatenate(
        [slot_valid(f, half == 0, mine_columns) for f in range(freq_count)]
        + [slot_valid(f, half == 1, other_columns) for f in range(freq_count)],
        1,
    )
    positions = lax.dynamic_slice(
        embed_all[:ngrid].reshape(FROWS, 2 * HALF, D),
        (freq_index * rows_dev, half * HALF, 0),
        (rows_dev, HALF, D),
    ).reshape(rows_dev * HALF, D)
    grid = matmul(pnorm, embed_all[ngrid:]) + vec_all[glob] + positions
    special = jnp.broadcast_to(vec_all[glob + 1 : glob + 3].astype(jnp.float32), (CPD, 2, D))
    x = jnp.concatenate([special, grid], 1)
    saved = []
    for layer in range(L):
        up_bias = vec_all[L * 8 + layer * spread_rows : L * 8 + (layer + 1) * spread_rows].reshape(
            FF
        )
        x, kept = layer_forward(
            x,
            wide_all[layer],
            down_all[layer],
            vec_all[layer * 8 : layer * 8 + 8],
            up_bias,
            keymask,
        )
        saved.append(kept)
    owner = jnp.logical_and(freq_index == 0, half == 0).astype(jnp.float32)
    normed_end, scale_end = norm_rows(x[:, :2])
    feature = jnp.mean(normed_end * vec_all[glob + 3] + vec_all[glob + 4], 1).astype(jnp.bfloat16)
    logits = matmul(feature, class_all) + class_bias
    clip_start = pair * CPD
    flags = lax.dynamic_slice_in_dim(labels, clip_start, CPD, 0).astype(jnp.float32)
    weights = lax.dynamic_slice_in_dim(clip_weights, clip_start, CPD, 0).astype(jnp.float32)[
        :, None
    ]
    weight_total = jnp.sum(clip_weights).astype(jnp.float32)
    loss_part = owner * jnp.sum(weights * (jax.nn.softplus(logits) - flags * logits))
    dlogits = owner * weights * (jax.nn.sigmoid(logits) - flags) / weight_total
    dlogits_low = dlogits.astype(jnp.bfloat16)
    grad_class = jnp.einsum("cd,ck->dk", feature, dlogits_low, preferred_element_type=jnp.float32)
    dfinal = jnp.broadcast_to(
        0.5
        * jnp.einsum("ck,dk->cd", dlogits_low, class_all, preferred_element_type=jnp.float32)[
            :, None, :
        ],
        (CPD, 2, D),
    )
    end_rows = [row_total(dfinal * normed_end), row_total(dfinal)]
    dspecial = norm_back(dfinal * vec_all[glob + 3], normed_end, scale_end)
    dx = jnp.concatenate([dspecial, jnp.zeros((CPD, x.shape[1] - 2, D), jnp.float32)], 1)
    layer_wide = [None] * L
    layer_down = [None] * L
    layer_rows = [None] * L
    layer_up = [None] * L
    for layer in reversed(range(L)):
        dx, grad_wide, grad_down, grad_rows, grad_up_bias = layer_backward(
            dx,
            saved[layer],
            wide_all[layer],
            down_all[layer],
            vec_all[layer * 8 : layer * 8 + 8],
            keymask,
        )
        layer_wide[layer] = grad_wide
        layer_down[layer] = grad_down
        layer_rows[layer] = grad_rows
        layer_up[layer] = grad_up_bias.reshape(spread_rows, D)
    dgrid = dx[:, 2:]
    grad_patch = jnp.einsum(
        "crp,crd->pd", pnorm, dgrid.astype(jnp.bfloat16), preferred_element_type=jnp.float32
    )
    dpositions = jnp.sum(dgrid, 0).reshape(rows_dev, HALF, D)
    grad_pos = lax.dynamic_update_slice(
        jnp.zeros((FROWS, 2 * HALF, D), jnp.float32),
        dpositions,
        (freq_index * rows_dev, half * HALF, 0),
    ).reshape(ngrid, D)
    grad_embed = jnp.concatenate([grad_pos, grad_patch], 0)
    global_rows = jnp.stack(
        [row_total(dgrid), jnp.sum(dx[:, 0], 0), jnp.sum(dx[:, 1], 0)] + end_rows
    )
    grad_vectors = jnp.concatenate(
        [jnp.concatenate(layer_rows, 0), jnp.concatenate(layer_up, 0), global_rows], 0
    )
    grad_wide = jnp.stack(layer_wide)
    grad_down = jnp.stack(layer_down)
    params = (wide_weights, down_weights, embedding, classifier, vectors, class_bias)
    firsts = (wide_first, down_first, embedding_first, classifier_first, vectors_first, bias_first)
    seconds = (
        wide_second,
        down_second,
        embedding_second,
        classifier_second,
        vectors_second,
        bias_second,
    )
    grad_wide, grad_down, grad_embed, grad_class, grad_vectors = (
        lax.psum_scatter(grad_wide, "tm", scatter_dimension=1, tiled=True),
        lax.psum_scatter(grad_down, "tm", scatter_dimension=1, tiled=True),
        lax.psum_scatter(grad_embed, "tm", scatter_dimension=1, tiled=True),
        lax.psum_scatter(grad_class, "tm", scatter_dimension=0, tiled=True),
        lax.psum_scatter(grad_vectors, "tm", scatter_dimension=1, tiled=True),
    )
    grad_wide, grad_down, grad_embed, grad_class, grad_vectors = lax.psum(
        (grad_wide, grad_down, grad_embed, grad_class, grad_vectors), "freq"
    )
    owned_all = (grad_wide, grad_down, grad_embed, grad_class, grad_vectors)
    local_squares = jnp.where(freq_index == 0, sum((jnp.sum(g * g) for g in owned_all)), 0.0)
    owned = (grad_wide, grad_down, grad_embed, grad_class, grad_vectors)
    square_total, grad_bias, loss_sum = lax.psum(
        (local_squares, jnp.sum(dlogits, 0), loss_part), ("freq", "tm")
    )
    grad_norm = jnp.sqrt(square_total + jnp.sum(grad_bias * grad_bias))
    coef = jnp.minimum(1.0, 1.0 / (grad_norm + 1e-06))
    grads = owned + (grad_bias,)
    news = [adam(w, m, v, g * coef) for w, m, v, g in zip(params, firsts, seconds, grads)]
    masters = [n[0] for n in news]
    first_new = [n[1] for n in news]
    second_new = [n[2] for n in news]
    return (
        masters[0],
        masters[1],
        masters[2],
        masters[3],
        masters[4],
        masters[5],
        first_new[0],
        first_new[1],
        first_new[2],
        first_new[3],
        first_new[4],
        first_new[5],
        second_new[0],
        second_new[1],
        second_new[2],
        second_new[3],
        second_new[4],
        second_new[5],
        masters[0].astype(jnp.bfloat16),
        masters[1].astype(jnp.bfloat16),
        masters[2].astype(jnp.bfloat16),
        masters[3].astype(jnp.bfloat16),
        grad_norm,
        loss_sum,
        weight_total,
    )


def solution(mesh):
    placed = (
        P("freq", "tm", None),
        P(),
        P(),
        P(),
        P(None, "tm", None),
        P(None, "tm", None),
        P(None, "tm"),
        P("tm", None),
        P(None, "tm"),
        P(),
        P(None, "tm", None),
        P(None, "tm", None),
        P(None, "tm"),
        P("tm", None),
        P(None, "tm"),
        P(),
        P(None, "tm", None),
        P(None, "tm", None),
        P(None, "tm"),
        P("tm", None),
        P(None, "tm"),
        P(),
    )
    return jax.shard_map(
        local,
        mesh=mesh,
        in_specs=placed,
        out_specs=(
            P(None, "tm", None),
            P(None, "tm", None),
            P(None, "tm"),
            P("tm", None),
            P(None, "tm"),
            P(),
            P(None, "tm", None),
            P(None, "tm", None),
            P(None, "tm"),
            P("tm", None),
            P(None, "tm"),
            P(),
            P(None, "tm", None),
            P(None, "tm", None),
            P(None, "tm"),
            P("tm", None),
            P(None, "tm"),
            P(),
            P(None, "tm", None),
            P(None, "tm", None),
            P(None, "tm"),
            P("tm", None),
            P(),
            P(),
            P(),
        ),
        check_vma=False,
    )
```

profile of v0, /device:TPU:0, one launch (start us, length us, event | category | flops | bytes accessed | tf_op | source)
XLA Modules:
  0.0 3055.8 jit_solution(14375252656341726927)
XLA Ops:
  15.6 43.3 %all-reduce.4 = (f32[]{:T(128)}, f32[]{:T(128)}, f32[]{:T(128)}) all-reduce(f32[]{:T(128)} %get-tuple-element.146, f32[]{:T(128)S(6)} %mul.609, f32[]{:T(128)} %get-tuple-element.145), channel_id=1, replica_groups=mesh['freq'=4,'tm'=8] {'freq','tm'}, use_global_device_ids=true, to_apply=%region_5.6 | all-reduce | flops 3 | bytes 24 | tf_op jit(solution)/shard_map/psum | solution.py:272
  61.8 51.4 %all-gather = bf16[8,96,29]{1,2,0:T(8,128)(2,1)S(1)} all-gather(bf16[1,96,29]{1,2,0:T(8,128)(2,1)S(1)} %convert_bitcast_fusion), channel_id=1, replica_groups=mesh['freq'=4,'tm'=8] {'tm'}, dimensions={0}, use_global_device_ids=true | all-gather | bytes 50112 | tf_op jit(solution)/shard_map/all_gather | solution.py:290
  121.1 309.1 %all-gather.9.cloned.1.call-done = bf16[2,768,6144]{2,1,0:T(8,128)(2,1)} async-done(((bf16[2,96,6144]{2,1,0:T(8,128)(2,1)}), bf16[2,768,6144]{2,1,0:T(8,128)(2,1)}) %all-gather.9.cloned.1.call-update) | async-done | bytes 18874384 | tf_op jit(solution)/shard_map/all_gather | solution.py:286
  430.1 11.5 slice_bitcast_fusion.1
  450.0 31.4 %all-gather.11.cloned.1.call-done = bf16[2,632,1536]{2,0,1:T(2,128)(2,1)} async-done(((bf16[2,158,1536]{2,0,1:T(2,128)(2,1)}), bf16[2,632,1536]{2,0,1:T(2,128)(2,1)}) %all-gather.11.cloned.1.call-update) | async-done | bytes 3883024 | tf_op jit(solution)/shard_map/all_gather | solution.py:127
  481.4 4.6 copy.233
  488.1 10.9 copy.234
  499.0 125.3 %collective-permute-done = bf16[2,632,1536]{2,1,0:T(8,128)(2,1)} collective-permute-done((bf16[2,632,1536]{2,1,0:T(8,128)(2,1)}, bf16[2,632,1536]{2,1,0:T(8,128)(2,1)}, u32[]{:S(2)}, u32[]{:S(2)}) %collective-permute-start) | collective-permute-done | bytes 3883040 | tf_op jit(solution)/shard_map/ppermute | solution.py:31
  624.4 6.2 copy.235
  630.6 7.4 fusion.28
  644.4 4.5 copy-done
  648.9 8.6 fusion.37
  660.2 5.9 multiply_convert_fusion.3
  666.2 4.7 fusion.123
  677.0 33.6 %all-gather.15.cloned.1.call-done = bf16[2,632,1536]{2,0,1:T(2,128)(2,1)} async-done(((bf16[2,158,1536]{2,0,1:T(2,128)(2,1)}), bf16[2,632,1536]{2,0,1:T(2,128)(2,1)}) %all-gather.15.cloned.1.call-update) | async-done | bytes 3883024 | tf_op jit(solution)/shard_map/all_gather | solution.py:127
  710.6 4.6 copy.239
  718.1 111.8 %all_gather.27 = bf16[768,527]{1,0:T(8,128)(2,1)S(1)} all-gather(bf16[96,527]{1,0:T(8,128)(2,1)S(1)} %convert_element_type.465), channel_id=1, replica_groups=mesh['freq'=4,'tm'=8] {'tm'}, dimensions={0}, use_global_device_ids=true | all-gather | bytes 910656 | tf_op jit(solution)/shard_map/all_gather | solution.py:289
  830.1 10.7 copy.240
  840.8 6.2 copy.241
  847.1 7.4 pad_maximum_fusion.5
  865.5 8.6 fusion.36
  895.8 14.9 multiply_reduce_fusion.1
  910.7 10.4 fusion.4
  921.1 13.3 multiply_convert_fusion.1
  934.4 5.0 convolution_multiply_fusion.1
  940.4 12.7 copy.245
  953.1 12.7 copy.246
  965.8 8.3 pad_maximum_fusion.3
  976.3 8.3 multiply_convert_fusion.5
  984.8 153.5 %collective-permute-done.2 = f32[2,632,1536]{2,0,1:T(2,128)} collective-permute-done((f32[2,632,1536]{2,0,1:T(2,128)}, f32[2,632,1536]{2,0,1:T(2,128)}, u32[]{:S(2)}, u32[]{:S(2)}) %collective-permute-start.2) | collective-permute-done | bytes 7766048 | tf_op jit(solution)/shard_map/ppermute | solution.py:31
  1138.3 9.9 fusion.15
  1148.2 136.3 %all-reduce.11 = bf16[2,632,1536]{2,0,1:T(2,128)(2,1)} all-reduce(f32[2,632,1536]{2,0,1:T(2,128)} %fusion.15), channel_id=2, replica_groups=mesh['freq'=4,'tm'=8] {'freq'}, use_global_device_ids=true, to_apply=%region_27.28.clone | all-reduce | flops 1941504 | bytes 11649024
  1286.5 4.6 multiply_reduce_fusion.5
  1292.1 5.4 fusion.126
  1302.0 13.9 multiply_reduce_fusion
  1315.8 10.4 fusion.6
  1326.2 13.6 multiply_convert_fusion
  1339.8 5.1 convolution_multiply_fusion
  1346.0 12.7 copy.250
  1358.7 12.7 copy.251
  1371.4 7.9 pad_maximum_fusion.2
  1381.9 8.3 multiply_convert_fusion.4
  1390.6 171.6 %collective-permute-done.3 = f32[2,632,1536]{2,0,1:T(2,128)} collective-permute-done((f32[2,632,1536]{2,0,1:T(2,128)}, f32[2,632,1536]{2,0,1:T(2,128)}, u32[]{:S(2)}, u32[]{:S(2)}) %collective-permute-start.3) | collective-permute-done | bytes 7766048 | tf_op jit(solution)/shard_map/ppermute | solution.py:31
  1562.1 9.9 fusion.13
  1572.0 136.0 %all-reduce.12 = bf16[2,632,1536]{2,0,1:T(2,128)(2,1)} all-reduce(f32[2,632,1536]{2,0,1:T(2,128)} %fusion.13), channel_id=3, replica_groups=mesh['freq'=4,'tm'=8] {'freq'}, use_global_device_ids=true, to_apply=%region_33.34.clone | all-reduce | flops 1941504 | bytes 11649024
  1710.1 4.6 multiply_reduce_fusion.7
  1725.5 4.6 pad_maximum_fusion.4
  1730.1 6.0 copy.268
  1743.1 6.6 pad_maximum_fusion.1
  1751.9 8.4 convolution_bitcast_fusion.2
  1761.2 5.1 convolution_bitcast_fusion.3
  1766.3 5.4 convolution_bitcast_fusion.4
  1771.8 7.2 maximum_bitcast_fusion.1
  1781.3 11.0 maximum_bitcast_fusion
  1792.2 20.8 pad_maximum_fusion
  1826.0 4.7 reduce-scatter.16.cloned.1.call-done
  1830.7 316.9 %reduce-scatter.12.cloned.1.call-done = f32[2,384,768]{2,1,0:T(8,128)} async-done(((f32[2,3072,768]{2,1,0:T(8,128)}), f32[2,384,768]{2,1,0:T(8,128)}) %reduce-scatter.12.cloned.1.call-update) | async-done | bytes 2359312 | tf_op jit(solution)/shard_map/reduce_scatter | solution.py:398
  2147.6 608.8 %reduce-scatter.10.cloned.1.call-done = f32[2,96,6144]{2,1,0:T(8,128)} async-done(((f32[2,768,6144]{2,1,0:T(8,128)}), f32[2,96,6144]{2,1,0:T(8,128)}) %reduce-scatter.10.cloned.1.call-update) | async-done | bytes 4718608 | tf_op jit(solution)/shard_map/reduce_scatter | solution.py:397
  2757.0 63.6 %reduce-scatter.18.cloned.1.call-done = f32[96,29]{1,0:T(8,128)} async-done(((f32[768,29]{1,0:T(8,128)}), f32[96,29]{1,0:T(8,128)}) %reduce-scatter.18.cloned.1.call-update) | async-done | bytes 11152
  2821.5 10.6 psum.84
  2832.7 136.2 %all-reduce.10.cloned.1.call-done = (f32[2,96,6144]{2,1,0:T(8,128)}, f32[2,384,768]{2,1,0:T(8,128)}, f32[1504,96]{0,1:T(8,128)}, f32[96,527]{1,0:T(8,128)}) async-done(((f32[2,96,6144]{2,1,0:T(8,128)}, f32[2,384,768]{2,1,0:T(8,128)}, f32[1504,96]{0,1:T(8,128)}, f32[96,527]{1,0:T(8,128)}), (f32[2,96,6144]{2,1,0:T(8,128)}, f32[2,384,768]{2,1,0:T(8,128)}, f32[1504,96]{0,1:T(8,128)}, ...) | async-done | bytes 7857808 | tf_op jit(solution)/shard_map/psum | solution.py:403
  2979.1 39.8 %all-reduce.3 = (f32[]{:T(128)}, f32[527]{0:T(1024)}, f32[]{:T(128)}) all-reduce(f32[]{:T(128)S(6)} %select_n.56, f32[527]{0:T(1024)} %get-tuple-element.202, f32[]{:T(128)S(6)} %mul.777), channel_id=1, replica_groups=mesh['freq'=4,'tm'=8] {'freq','tm'}, use_global_device_ids=true, to_apply=%region_75.76 | all-reduce | flops 529 | bytes 4232 | tf_op jit(solution)/shard_map/psum | solution.py:409
  3030.6 7.3 fusion.107
  3037.9 8.9 fusion.109
  (445 shorter events, 146.2 us)
Async XLA Ops:
  7.2 106.9 %all-gather.7.cloned.1.call-start = ((), (), s32[]{:S(2)}) async-start(), calls=%async_computation.5 | async-start | bytes 2654208 | tf_op jit(solution)/shard_map/all_gather | solution.py:288
  9.1 52.7 %copy-start.52 = (f32[29,96]{1,0:T(8,128)S(1)}, f32[29,96]{1,0:T(8,128)}, u32[]{:S(2)}) copy-start(f32[29,96]{1,0:T(8,128)} %param.30) | copy-start | bytes 33412
  9.1 421.0 %all-gather.9.cloned.1.call-start = ((), (), s32[]{:S(2)}) async-start(), calls=%async_computation.6 | async-start | bytes 21233664 | tf_op jit(solution)/shard_map/all_gather | solution.py:286
  13.3 468.1 %all-gather.11.cloned.1.call-start = ((), (), s32[]{:S(2)}) async-start(), calls=%async_computation.7 | async-start | bytes 4853760 | tf_op jit(solution)/shard_map/all_gather | solution.py:127
  61.8 57.2 %copy-start.40 = (bf16[2,3,52,256]{3,0,2,1:T(2,128)(2,1)}, bf16[2,3,52,256]{3,0,2,1:T(2,128)(2,1)S(1)}, u32[]{:S(2)}) copy-start(bf16[2,3,52,256]{3,0,2,1:T(2,128)(2,1)S(1)} %copy.228) | copy-start | bytes 479236
  114.0 327.6 %copy-start.75 = (f32[768]{0:T(1024)}, f32[768]{0:T(1024)S(1)}, u32[]{:S(2)}) copy-start(f32[768]{0:T(1024)S(1)} %get-tuple-element.164) | copy-start | bytes 9220
  114.0 327.6 %copy-start.92 = (f32[768]{0:T(1024)}, f32[768]{0:T(1024)S(1)}, u32[]{:S(2)}) copy-start(f32[768]{0:T(1024)S(1)} %get-tuple-element.163) | copy-start | bytes 9220
  114.1 546.1 %copy-start.78 = (f32[768]{0:T(1024)}, f32[768]{0:T(1024)S(1)}, u32[]{:S(2)}) copy-start(f32[768]{0:T(1024)S(1)} %get-tuple-element.159) | copy-start | bytes 9220
  114.1 546.1 %copy-start.94 = (f32[768]{0:T(1024)}, f32[768]{0:T(1024)S(1)}, u32[]{:S(2)}) copy-start(f32[768]{0:T(1024)S(1)} %get-tuple-element.158) | copy-start | bytes 9220
  114.1 557.2 %copy-start.80 = (f32[768]{0:T(1024)}, f32[768]{0:T(1024)S(1)}, u32[]{:S(2)}) copy-start(f32[768]{0:T(1024)S(1)} %get-tuple-element.156) | copy-start | bytes 9220
  114.1 779.0 %copy-start.68 = (f32[768]{0:T(1024)}, f32[768]{0:T(1024)S(1)}, u32[]{:S(2)}) copy-start(f32[768]{0:T(1024)S(1)} %get-tuple-element.151) | copy-start | bytes 9220
  120.5 537.1 %copy-start.6 = (f32[2,156,768]{2,1,0:T(8,128)}, f32[2,156,768]{2,1,0:T(8,128)S(1)}, u32[]{:S(2)}) copy-start(f32[2,156,768]{2,1,0:T(8,128)S(1)} %fusion.40) | copy-start | bytes 2875396
  120.5 537.1 %copy-start.49 = (f32[2,2,768]{2,1,0:T(2,128)}, f32[2,2,768]{2,1,0:T(2,128)S(1)}, u32[]{:S(2)}) copy-start(f32[2,2,768]{2,1,0:T(2,128)S(1)} %broadcast_in_dim.34) | copy-start | bytes 36868
  120.7 321.0 %copy-start.59 = (f32[2,158]{1,0:T(2,128)}, f32[2,158]{1,0:T(2,128)S(1)}, u32[]{:S(2)}) copy-start(f32[2,158]{1,0:T(2,128)S(1)} %broadcast_multiply_fusion.11) | copy-start | bytes 3796
  121.0 320.6 %copy-start.83 = (f32[2,158]{1,0:T(2,128)}, f32[2,158]{1,0:T(2,128)S(1)}, u32[]{:S(2)}) copy-start(f32[2,158]{1,0:T(2,128)S(1)} %add_rsqrt_fusion.3) | copy-start | bytes 3796
  448.6 217.6 %all-gather.13.cloned.1.call-start = ((), (), s32[]{:S(2)}) async-start(), calls=%async_computation.8 | async-start | bytes 10616832 | tf_op jit(solution)/shard_map/all_gather | solution.py:287
  449.8 38.1 %copy-start.39 = (bf16[2,158,768]{2,1,0:T(8,128)(2,1)S(1)}, bf16[2,158,768]{2,1,0:T(8,128)(2,1)}, u32[]{:S(2)}) copy-start(bf16[2,158,768]{2,1,0:T(8,128)(2,1)} %get-tuple-element.224) | copy-start | bytes 1456132
  449.8 260.8 %all-gather.15.cloned.1.call-start = ((), (), s32[]{:S(2)}) async-start(), calls=%async_computation.9 | async-start | bytes 4853760 | tf_op jit(solution)/shard_map/all_gather | solution.py:127
  486.0 138.3 %collective-permute-start = (bf16[2,632,1536]{2,1,0:T(8,128)(2,1)}, bf16[2,632,1536]{2,1,0:T(8,128)(2,1)}, u32[]{:S(2)}, u32[]{:S(2)}) collective-permute-start(bf16[2,632,1536]{2,1,0:T(8,128)(2,1)} %copy.233), channel_id=1, source_target_pairs={{0,1},{1,0},{2,3},{3,2},{4,5},{5,4},{6,7},{7,6},{8,9},{9,8},{10,11... | collective-permute-start | bytes 11649032 | tf_op jit(solution)/shard_map/ppermute | solution.py:31
  488.1 149.8 %copy-start.11 = (bf16[2,158,768]{1,2,0:T(8,128)(2,1)}, bf16[2,158,768]{1,2,0:T(8,128)(2,1)S(1)}, u32[]{:S(2)}) copy-start(bf16[2,158,768]{1,2,0:T(8,128)(2,1)S(1)} %copy.236) | copy-start | bytes 1456132
  670.9 620.1 %copy-start.19 = (f32[2,158,768]{2,1,0:T(8,128)}, f32[2,158,768]{2,1,0:T(8,128)S(1)}, u32[]{:S(2)}) copy-start(f32[2,158,768]{2,1,0:T(8,128)S(1)} %get-tuple-element.238) | copy-start | bytes 2912260
  671.0 620.1 %copy-start.63 = (f32[2,158]{1,0:T(2,128)}, f32[2,158]{1,0:T(2,128)S(1)}, u32[]{:S(2)}) copy-start(f32[2,158]{1,0:T(2,128)S(1)} %broadcast_multiply_fusion.9) | copy-start | bytes 3796
  677.0 39.7 %copy-start.41 = (f32[96,527]{1,0:T(8,128)S(1)}, f32[96,527]{1,0:T(8,128)}, u32[]{:S(2)}) copy-start(f32[96,527]{1,0:T(8,128)} %param.29) | copy-start | bytes 607108
  677.0 39.8 %copy-start.102 = (s32[8]{0:T(128)S(1)}, s32[8]{0:T(128)}, u32[]{:S(2)}) copy-start(s32[8]{0:T(128)} %param.25) | copy-start | bytes 100
  677.0 1149.0 %reduce-scatter.14.cloned.1.call-start = ((), (), s32[]{:S(2)}) async-start(), calls=%async_computation.12 | async-start | bytes 2211840 | tf_op jit(solution)/shard_map/reduce_scatter | solution.py:400
  715.2 125.6 %collective-permute-start.1 = (bf16[2,632,1536]{2,1,0:T(8,128)(2,1)}, bf16[2,632,1536]{2,1,0:T(8,128)(2,1)}, u32[]{:S(2)}, u32[]{:S(2)}) collective-permute-start(bf16[2,632,1536]{2,1,0:T(8,128)(2,1)} %copy.239), channel_id=1, source_target_pairs={{0,1},{1,0},{2,3},{3,2},{4,5},{5,4},{6,7},{7,6},{8,9},{9,8},{10,11... | collective-permute-start | bytes 11649032 | tf_op jit(solution)/shard_map/ppermute | solution.py:31
  876.5 16.6 copy-start.17
  876.5 16.6 copy-start.65
  876.8 16.3 copy-start.90
  881.0 9.4 slice-start.4
  881.0 9.4 slice-start.5
  895.8 14.9 copy-start.25
  974.1 164.2 %collective-permute-start.2 = (f32[2,632,1536]{2,0,1:T(2,128)}, f32[2,632,1536]{2,0,1:T(2,128)}, u32[]{:S(2)}, u32[]{:S(2)}) collective-permute-start(f32[2,632,1536]{2,0,1:T(2,128)} %pad_maximum_fusion.3), channel_id=1, source_target_pairs={{0,1},{1,0},{2,3},{3,2},{4,5},{5,4},{6,7},{7,6},{8,9},{9,8},{10,11... | collective-permute-start | bytes 23298056 | tf_op jit(solution)/shard_map/ppermute | solution.py:31
  984.5 163.6 %copy-start.21 = (bf16[2,12,64,158]{3,2,1,0:T(8,128)(2,1)}, bf16[2,12,64,158]{3,2,1,0:T(8,128)(2,1)S(1)}, u32[]{:S(2)}) copy-start(bf16[2,12,64,158]{3,2,1,0:T(8,128)(2,1)S(1)} %multiply_convert_fusion.5) | copy-start | bytes 1456132
  984.8 301.6 %copy-start.45 = (bf16[2,158,768]{2,1,0:T(8,128)(2,1)}, bf16[2,158,768]{2,1,0:T(8,128)(2,1)S(1)}, u32[]{:S(2)}) copy-start(bf16[2,158,768]{2,1,0:T(8,128)(2,1)S(1)} %copy.248) | copy-start | bytes 1456132
  1148.2 138.3 %copy-start.81 = (f32[768]{0:T(1024)S(1)}, f32[768]{0:T(1024)}, u32[]{:S(2)}) copy-start(f32[768]{0:T(1024)} %copy-done.80) | copy-start | bytes 9220
  1148.2 138.3 %copy-start.89 = (f32[2,158]{1,0:T(2,128)S(1)}, f32[2,158]{1,0:T(2,128)}, u32[]{:S(2)}) copy-start(f32[2,158]{1,0:T(2,128)} %copy-done.88) | copy-start | bytes 3796
  1286.5 11.0 slice-start.7
  1286.5 11.0 slice-start.8
  1326.2 13.6 copy-start.12
  1379.3 182.8 %collective-permute-start.3 = (f32[2,632,1536]{2,0,1:T(2,128)}, f32[2,632,1536]{2,0,1:T(2,128)}, u32[]{:S(2)}, u32[]{:S(2)}) collective-permute-start(f32[2,632,1536]{2,0,1:T(2,128)} %pad_maximum_fusion.2), channel_id=1, source_target_pairs={{0,1},{1,0},{2,3},{3,2},{4,5},{5,4},{6,7},{7,6},{8,9},{9,8},{10,11... | collective-permute-start | bytes 23298056 | tf_op jit(solution)/shard_map/ppermute | solution.py:31
  1381.9 448.8 %reduce-scatter.16.cloned.1.call-start = ((), (), s32[]{:S(2)}) async-start(), calls=%async_computation.13 | async-start | bytes 5308416
  1390.3 171.8 %copy-start.23 = (bf16[2,12,64,158]{3,2,1,0:T(8,128)(2,1)}, bf16[2,12,64,158]{3,2,1,0:T(8,128)(2,1)S(1)}, u32[]{:S(2)}) copy-start(bf16[2,12,64,158]{3,2,1,0:T(8,128)(2,1)S(1)} %multiply_convert_fusion.4) | copy-start | bytes 1456132
  1390.5 319.5 %copy-start.47 = (bf16[2,158,768]{2,1,0:T(8,128)(2,1)}, bf16[2,158,768]{2,1,0:T(8,128)(2,1)S(1)}, u32[]{:S(2)}) copy-start(bf16[2,158,768]{2,1,0:T(8,128)(2,1)S(1)} %copy.253) | copy-start | bytes 1456132
  1572.0 138.1 %copy-start.7 = (f32[2,156,768]{2,1,0:T(8,128)S(1)}, f32[2,156,768]{2,1,0:T(8,128)}, u32[]{:S(2)}) copy-start(f32[2,156,768]{2,1,0:T(8,128)} %copy-done.6) | copy-start | bytes 2875396
  1572.0 138.1 %copy-start.50 = (f32[2,2,768]{2,1,0:T(2,128)S(1)}, f32[2,2,768]{2,1,0:T(2,128)}, u32[]{:S(2)}) copy-start(f32[2,2,768]{2,1,0:T(2,128)} %copy-done.49) | copy-start | bytes 36868
  1572.0 138.1 %copy-start.60 = (f32[2,158]{1,0:T(2,128)S(1)}, f32[2,158]{1,0:T(2,128)}, u32[]{:S(2)}) copy-start(f32[2,158]{1,0:T(2,128)} %copy-done.59) | copy-start | bytes 3796
  1572.0 138.1 %copy-start.76 = (f32[768]{0:T(1024)S(1)}, f32[768]{0:T(1024)}, u32[]{:S(2)}) copy-start(f32[768]{0:T(1024)} %copy-done.75) | copy-start | bytes 9220
  1572.0 138.1 %copy-start.84 = (f32[2,158]{1,0:T(2,128)S(1)}, f32[2,158]{1,0:T(2,128)}, u32[]{:S(2)}) copy-start(f32[2,158]{1,0:T(2,128)} %copy-done.83) | copy-start | bytes 3796
  1736.2 411.4 %reduce-scatter.12.cloned.1.call-start = ((), (), s32[]{:S(2)}) async-start(), calls=%async_computation.11 | async-start | bytes 21233664 | tf_op jit(solution)/shard_map/reduce_scatter | solution.py:398
  1749.8 1006.6 %reduce-scatter.10.cloned.1.call-start = ((), (), s32[]{:S(2)}) async-start(), calls=%async_computation.10 | async-start | bytes 42467328 | tf_op jit(solution)/shard_map/reduce_scatter | solution.py:397
  1751.8 9.3 copy-start.20
  1751.8 9.3 copy-start.35
  1751.8 9.3 copy-start.46
  1751.9 9.3 copy-start.64
  1751.9 9.3 copy-start.97
  1813.0 9.3 copy-start.72
  1813.1 1007.6 %reduce-scatter.18.cloned.1.call-start = ((), (), s32[]{:S(2)}) async-start(), calls=%async_computation.14 | async-start | bytes 442368
  1825.9 1143.0 %all-reduce.10.cloned.1.call-start = ((), (), s32[]{:S(2)}) async-start(), calls=%async_computation.15 | async-start | bytes 15826944 | tf_op jit(solution)/shard_map/psum | solution.py:403
  2968.9 58.0 %copy-start.32 = (f32[1504,96]{0,1:T(8,128)S(1)}, f32[1504,96]{0,1:T(8,128)}, u32[]{:S(2)}) copy-start(f32[1504,96]{0,1:T(8,128)} %param.28) | copy-start | bytes 1732612
  2973.2 57.3 %copy-start.14 = (f32[2,384,768]{2,1,0:T(8,128)S(1)}, f32[2,384,768]{2,1,0:T(8,128)}, u32[]{:S(2)}) copy-start(f32[2,384,768]{2,1,0:T(8,128)} %param.27) | copy-start | bytes 7077892
  3024.5 13.4 slice-start
  3024.5 13.4 slice-start.11
  3026.9 10.9 slice-start.2
  (77 other events, 395.6 us)
Sparse Core Ops, SparseCore 0:
  10.8 55.0 all-gather.6
  68.0 362.0 all-gather.8
  448.7 32.6 all-gather.10
  484.0 181.0 all-gather.12
  677.1 33.4 all-gather.14
  1382.0 74.8 reduce-scatter.13
  1736.3 94.3 reduce-scatter.15
  1835.1 312.4 reduce-scatter.11
  2151.9 604.4 reduce-scatter.9
  2760.1 60.5 reduce-scatter.17
  2823.4 145.4 all-reduce.9
where the time goes:
time: 3070 us; the launch traced here: 3060 us
  waiting for transfers between devices  1950 us (64%)
  blocking collectives  529 us (17%)
  other arithmetic  189 us (6%)
  matrix products  188 us (6%)
  local copies, waits for them, and re-layouts  160 us (5%)
    reduce_scatter x1, waiting for transfers between devices, local(): lax.psum_scatter(grad_wide, 'tm', scatter_dimension=1, tiled=True)  609 us
    ppermute x4, waiting for transfers between devices, swapped(): return lax.ppermute(block, axis, route)  450 us
    reduce_scatter x1, waiting for transfers between devices, local(): lax.psum_scatter(grad_down, 'tm', scatter_dimension=1, tiled=True)  317 us
    all_gather x1, waiting for transfers between devices, local(): lax.all_gather(wide_weights.astype(jnp.bfloat16), 'tm', axis=1, tiled=True)  309 us
    unnamed x2, blocking collectives  272 us
    psum x1, waiting for transfers between devices, local(): lax.psum((grad_wide, grad_down, grad_embed, grad_class, grad_vectors), 'f...  136 us
    all_gather x1, blocking collectives, local(): lax.all_gather(classifier.astype(jnp.bfloat16), 'tm', axis=0, tiled=True)  112 us
    unnamed x13, waiting for transfers between devices  68.5 us
  transfers between devices with their start and end apart: 15, of which 11 were waited for; matrix products, arithmetic and copies ran while one was open for 7% of the time, Pallas kernels for 0%

commit v1 on v0

v1 whole, which is shorter than its diff:
```python
import functools

import jax
import jax.numpy as jnp
from jax import lax
from jax.experimental import pallas as pl
from jax.experimental.pallas import tpu as pltpu
from jax.sharding import PartitionSpec as P

D = 768
HEADS = 12
HDIM = 64
FF = 3072
L = 2
FROWS = 12
HALF = 52
PATCH = 256
STEP = 5
CPD = 2
NGRID = FROWS * 2 * HALF
CLASSES = 527
VROWS = 29
GLOB = L * 8 + L * (FF // D)

TOK = 320
PER = 3
NF = 4

DECAY_FIRST = 0.5
DECAY_SECOND = 0.5
LEARN_RATE = 0.03
WEIGHT_DECAY = 0.05
EPSILON = 1e-08

MESH = pl.DeviceIdType.MESH
BF = jnp.bfloat16
F32 = jnp.float32
VLIM = 60 * 1024 * 1024
VM = pltpu.VMEM


def nn(a, b):
    return lax.dot_general(a, b, (((1,), (0,)), ((), ())), preferred_element_type=F32)


def nt(a, b):
    return lax.dot_general(a, b, (((1,), (1,)), ((), ())), preferred_element_type=F32)


def tn(a, b):
    return lax.dot_general(a, b, (((0,), (0,)), ((), ())), preferred_element_type=F32)


def norm_rows(x):
    center = jnp.mean(x, -1, keepdims=True)
    shifted = x - center
    scale = lax.rsqrt(jnp.mean(shifted * shifted, -1, keepdims=True) + 1e-06)
    return (shifted * scale, scale)


def norm_back(dnorm, normed, scale):
    return scale * (
        dnorm
        - jnp.mean(dnorm, -1, keepdims=True)
        - normed * jnp.mean(dnorm * normed, -1, keepdims=True)
    )


def vspec():
    return pl.BlockSpec(memory_space=VM)


def aspec():
    return pl.BlockSpec(memory_space=pl.ANY)


def place():
    f, t = lax.axis_index("freq"), lax.axis_index("tm")
    return f, t, f // 2, f % 2, t // 2, t % 2


def remote(src, dst, ssem, rsem, dev):
    return pltpu.make_async_remote_copy(
        src_ref=src, dst_ref=dst, send_sem=ssem, recv_sem=rsem, device_id=dev, device_id_type=MESH
    )


def greet_all(times):
    f, t = lax.axis_index("freq"), lax.axis_index("tm")
    n = NF * times
    me = f * times + t
    barrier = pltpu.get_barrier_semaphore()

    def hello(i, carry):
        other = (me + i) % n
        pl.semaphore_signal(
            barrier, inc=1, device_id=(other // times, other % times), device_id_type=MESH
        )
        return carry

    lax.fori_loop(1, n, hello, 0)
    pl.semaphore_wait(barrier, n - 1)


def spread_small(times, small, gathered, ssem, rsem):
    f, t = lax.axis_index("freq"), lax.axis_index("tm")
    n = NF * times
    me = f * times + t

    def send(i, carry):
        other = (me + i) % n
        remote(
            small, gathered.at[me], ssem, rsem, (other // times, other % times)
        ).start()
        return carry

    lax.fori_loop(1, n, send, 0)
    gathered[me] = small[...]


def wait_small(times, gathered, ssem, rsem):
    n = NF * times
    many = gathered.at[pl.ds(0, n - 1)]
    pltpu.make_async_copy(many, many, rsem).wait()
    pltpu.make_async_copy(many, many, ssem).wait()


GROUPS = (("c", 4), ("c", 0), ("c", 1), ("d", 0), ("c", 2), ("c", 3), ("d", 1))
SUBS = tuple((kind, idx, h) for kind, idx in GROUPS for h in (0, 1))


def gather_kernel(
    times, ucol, udown, stats, psend, ocol, odown, sall, precv,
    zs, zr, own, s1, r1, s2, r2, s3, r3, ss, sr, ps, pr,
):
    f, t, y, c, g, x = place()
    count = times // 2
    greet_all(times)
    spread_small(times, stats, sall, ss, sr)
    swap = remote(psend, precv, ps, pr, (f, g * 2 + 1 - x))
    swap.start()
    every = slice(None)

    def source(s):
        kind, idx, h = SUBS[s]
        if kind == "c":
            return ucol.at[idx, y, c, :, pl.ds(h * 384, 384)]
        return udown.at[idx, y, pl.ds(h * 96, 96), pl.ds(pl.multiple_of(c * 384, 128), 384)]

    def view(s, yy, zz, xx):
        kind, idx, h = SUBS[s]
        if kind == "c":
            return ocol.at[idx, yy, c, zz, xx, :, pl.ds(h * 384, 384)]
        return odown.at[
            idx, zz, xx, yy, pl.ds(h * 96, 96), pl.ds(pl.multiple_of(c * 384, 128), 384)
        ]

    def along(s, dz):
        return remote(
            source(s), view(s, y, g, x), zs.at[s, dz - 1], zr.at[s, dz - 1],
            (f, ((g + dz) % count) * 2 + x),
        )

    def keep(s):
        return pltpu.make_async_copy(source(s), view(s, y, g, x), own.at[s])

    over_x = (f, g * 2 + 1 - x)
    over_y = ((1 - y) * 2 + c, t)
    over_c = (y * 2 + 1 - c, t)

    def first(s):
        block = view(s, y, every, x)
        return remote(block, block, s1.at[s], r1.at[s], over_x if s % 2 == 0 else over_y)

    def second(s):
        block = view(s, y, every, every) if s % 2 == 0 else view(s, every, every, x)
        return remote(block, block, s2.at[s], r2.at[s], over_y if s % 2 == 0 else over_x)

    def third(s):
        block = view(s, every, every, every)
        return remote(block, block, s3.at[s], r3.at[s], over_c)

    total = len(SUBS)
    for s in range(total):
        keep(s).start()
        for dz in range(1, count):
            along(s, dz).start()
    for step in range(total + 3):
        if step < total:
            for dz in range(1, count):
                along(step, dz).wait_recv()
            keep(step).wait()
            first(step).start()
        if 0 <= step - 1 < total:
            first(step - 1).wait_recv()
            second(step - 1).start()
        if 0 <= step - 2 < total:
            second(step - 2).wait_recv()
            third(step - 2).start()
        if 0 <= step - 3 < total:
            third(step - 3).wait_recv()
    for s in range(total):
        for dz in range(1, count):
            along(s, dz).wait_send()
        first(s).wait_send()
        second(s).wait_send()
        third(s).wait_send()
    swap.wait()
    wait_small(times, sall, ss, sr)


def gather_weights(times, ucol, udown, stats, psend):
    count = times // 2
    total = len(SUBS)
    dma = pltpu.SemaphoreType.DMA
    return pl.pallas_call(
        functools.partial(gather_kernel, times),
        out_shape=(
            jax.ShapeDtypeStruct((2 * L + 1, 2, 2, count, 2, 96, D), BF),
            jax.ShapeDtypeStruct((L, count, 2, 2, 192, D), BF),
            jax.ShapeDtypeStruct((NF * times, 8, 128), F32),
            jax.ShapeDtypeStruct(psend.shape, BF),
        ),
        in_specs=[vspec()] * 4,
        out_specs=(aspec(), aspec(), vspec(), vspec()),
        scratch_shapes=[
            dma((total, count - 1)), dma((total, count - 1)), dma((total,)),
            dma((total,)), dma((total,)), dma((total,)), dma((total,)), dma((total,)), dma((total,)),
            dma, dma, dma, dma,
        ],
        compiler_params=pltpu.CompilerParams(
            collective_id=1, has_side_effects=True, vmem_limit_bytes=32 * 1024 * 1024
        ),
        name="gather_weights",
    )(ucol, udown, stats, psend)


QROWS = TOK + TOK // 2


def greet_clip():
    f, t = lax.axis_index("freq"), lax.axis_index("tm")
    barrier = pltpu.get_barrier_semaphore()
    for i in range(1, NF):
        pl.semaphore_signal(barrier, inc=1, device_id=((f + i) % NF, t), device_id_type=MESH)
    pl.semaphore_wait(barrier, NF - 1)


def pack_half(v):
    return jnp.concatenate([v[: TOK // 2], v[TOK // 2 :]], 1)


def open_half(v):
    return jnp.concatenate([v[:, :HDIM], v[:, HDIM:]], 0)


def forward_kernel(
    layer, x_ref, rows_ref, upb_ref, mask_ref, wcol, wdown,
    xo_ref, x1_ref, fa_ref, gp_ref, qk_ref,
    wbuf, dbuf, qsend, osend, orecv, kall, vall, acc, wsem, qs, qr, os, orr,
):
    f, t = lax.axis_index("freq"), lax.axis_index("tm")
    loads = [
        pltpu.make_async_copy(wcol.at[2 * layer], wbuf.at[0], wsem.at[0]),
        pltpu.make_async_copy(wcol.at[2 * layer + 1], wbuf.at[1], wsem.at[1]),
        pltpu.make_async_copy(wdown.at[layer], dbuf, wsem.at[2]),
    ]
    for load in loads:
        load.start()
    x = x_ref[...]
    normed, _ = norm_rows(x)
    act = (normed * rows_ref[0:1, :] + rows_ref[1:2, :]).astype(BF)
    fa_ref[0] = act
    greet_clip()
    loads[0].wait()

    def to_clip(j, i):
        other = (f + i) % NF
        return remote(qsend.at[j, other], qk_ref.at[j, f], qs.at[j, i - 1], qr.at[j, i - 1], (other, t))

    def back_clip(j, i):
        other = (f + i) % NF
        return remote(osend.at[j, other], orecv.at[j, f], os.at[j, i - 1], orr.at[j, i - 1], (other, t))

    for j in range(PER):
        cols = slice(256 * j, 256 * (j + 1))
        query = (nn(act, wbuf[0, 0, :, cols]) + rows_ref[4:5, cols]).astype(BF)
        key = nn(act, wbuf[0, 1, :, cols]).astype(BF)
        value = (nn(act, wbuf[0, 2, :, cols]) + rows_ref[5:6, cols]).astype(BF)
        for h in range(NF):
            part = slice(HDIM * h, HDIM * (h + 1))
            qsend[j, h, :TOK] = jnp.concatenate([query[:, part], key[:, part]], 1)
            qsend[j, h, TOK:] = pack_half(value[:, part])
        for i in range(1, NF):
            to_clip(j, i).start()
        qk_ref[j, f] = qsend[j, f]
    mask = mask_ref[...]
    for j in range(PER):
        for i in range(1, NF):
            to_clip(j, i).wait_recv()
        for s in range(NF):
            kall[s * TOK : (s + 1) * TOK] = qk_ref[j, s, :TOK, HDIM:]
            vall[s * TOK : (s + 1) * TOK] = open_half(qk_ref[j, s, TOK:])

        def attend(i, carry):
            s = (f + i) % NF
            halves = []
            for h in range(2):
                lo = h * (TOK // 2)
                q = qk_ref[j, s, lo : lo + TOK // 2, :HDIM]
                scores = nt(q, kall[...]) * (HDIM ** (-0.5)) + mask
                top = jnp.max(scores, -1, keepdims=True)
                expo = jnp.exp(scores - top)
                total = jnp.sum(expo, -1, keepdims=True)
                probs = (expo * (1.0 / total)).astype(BF)
                halves.append(nn(probs, vall[...]).astype(BF))
            osend[j, s] = jnp.concatenate(halves, 1)

            @pl.when(i > 0)
            def _():
                remote(
                    osend.at[j, s], orecv.at[j, f], os.at[j, i - 1], orr.at[j, i - 1], (s, t)
                ).start()

            return carry

        lax.fori_loop(1, NF, attend, 0)
        lax.fori_loop(0, 1, attend, 0)
        orecv[j, f] = osend[j, f]
    for load in loads[1:]:
        load.wait()
    parts = []
    for j in range(PER):
        for i in range(1, NF):
            back_clip(j, i).wait_recv()
        for h in range(NF):
            parts.append(open_half(orecv[j, h]))
    mixed = jnp.concatenate(parts, 1)
    fa_ref[1] = mixed
    resid = x_ref[...] + nn(mixed, wbuf[0, 3]) + rows_ref[6:7, :]
    x1_ref[...] = resid
    normed, _ = norm_rows(resid)
    act = (normed * rows_ref[2:3, :] + rows_ref[3:4, :]).astype(BF)
    fa_ref[2] = act
    acc[...] = resid + rows_ref[7:8, :]

    def mlp(k, carry):
        before = nn(fa_ref[2], wbuf[1, k]) + upb_ref[k]
        lower = 0.5 * (1.0 + lax.erf(before * 0.7071067811865476))
        gp_ref[k] = lower + before * jnp.exp(-0.5 * before * before) * 0.3989422804014327
        hidden = (before * lower).astype(BF)
        fa_ref[3 + k] = hidden
        acc[...] += nn(hidden, dbuf[pl.ds(pl.multiple_of(k * D, D), D)])
        return carry

    lax.fori_loop(0, FF // D, mlp, 0)
    xo_ref[...] = acc[...]
    for j in range(PER):
        for i in range(1, NF):
            to_clip(j, i).wait_send()
            back_clip(j, i).wait_send()


def forward_layer(layer, x, rows, up_bias, mask, wcol, wdown):
    dma = pltpu.SemaphoreType.DMA
    return pl.pallas_call(
        functools.partial(forward_kernel, layer),
        out_shape=(
            jax.ShapeDtypeStruct((TOK, D), F32),
            jax.ShapeDtypeStruct((TOK, D), F32),
            jax.ShapeDtypeStruct((7, TOK, D), BF),
            jax.ShapeDtypeStruct((FF // D, TOK, D), F32),
            jax.ShapeDtypeStruct((PER, NF, QROWS, 128), BF),
        ),
        in_specs=[vspec()] * 4 + [aspec()] * 2,
        out_specs=(vspec(),) * 5,
        scratch_shapes=[
            VM((2, 4, D, D), BF),
            VM((FF, D), BF),
            VM((PER, NF, QROWS, 128), BF),
            VM((PER, NF, TOK // 2, 128), BF),
            VM((PER, NF, TOK // 2, 128), BF),
            VM((NF * TOK, HDIM), BF),
            VM((NF * TOK, HDIM), BF),
            VM((TOK, D), F32),
            dma((3,)),
            dma((PER, NF - 1)), dma((PER, NF - 1)), dma((PER, NF - 1)), dma((PER, NF - 1)),
        ],
        compiler_params=pltpu.CompilerParams(
            collective_id=2 + layer, has_side_effects=True, vmem_limit_bytes=VLIM
        ),
        name="forward_layer",
    )(x, rows, up_bias, mask, wcol, wdown)


def backward_kernel(
    layer, dout_ref, x_ref, x1_ref, gp_ref, qk_ref, rows_ref, mask_ref, wcol, wdown,
    dx_ref, ba_ref, rowg_ref, upg_ref,
    wbuf, dbuf, dsend, drecv, gsend, grecv, kall, vall, dkall, dvall, dqall, acc,
    wsem, ds_, dr_, gs_, gr_,
):
    f, t = lax.axis_index("freq"), lax.axis_index("tm")
    loads = [
        pltpu.make_async_copy(wdown.at[layer], dbuf, wsem.at[0]),
        pltpu.make_async_copy(wcol.at[2 * layer + 1], wbuf.at[1], wsem.at[1]),
        pltpu.make_async_copy(wcol.at[2 * layer], wbuf.at[0], wsem.at[2]),
    ]
    for load in loads:
        load.start()
    dout = dout_ref[...]
    ba_ref[8] = dout.astype(BF)
    rowg_ref[7:8, :] = jnp.sum(dout, 0, keepdims=True)
    acc[...] = jnp.zeros_like(acc)
    greet_clip()
    loads[0].wait()
    loads[1].wait()

    def mlp(k, carry):
        dhidden = nt(ba_ref[8], dbuf[pl.ds(pl.multiple_of(k * D, D), D)])
        dbefore = dhidden * gp_ref[k]
        upg_ref[k] = jnp.sum(dbefore, 0, keepdims=True)
        low = dbefore.astype(BF)
        ba_ref[4 + k] = low
        acc[...] += nt(low, wbuf[1, k])
        return carry

    lax.fori_loop(0, FF // D, mlp, 0)
    normed, scale = norm_rows(x1_ref[...])
    dact = acc[...]
    rowg_ref[2:3, :] = jnp.sum(dact * normed, 0, keepdims=True)
    rowg_ref[3:4, :] = jnp.sum(dact, 0, keepdims=True)
    dresid = dout_ref[...] + norm_back(dact * rows_ref[2:3, :], normed, scale)
    rowg_ref[6:7, :] = jnp.sum(dresid, 0, keepdims=True)
    acc[...] = dresid
    low = dresid.astype(BF)
    ba_ref[3] = low
    loads[2].wait()
    dmixed = nt(low, wbuf[0, 3]).astype(BF)

    def to_clip(j, i):
        other = (f + i) % NF
        return remote(dsend.at[j, other], drecv.at[j, f], ds_.at[j, i - 1], dr_.at[j, i - 1], (other, t))

    def back_clip(j, i):
        other = (f + i) % NF
        return remote(gsend.at[j, other], grecv.at[j, f], gs_.at[j, i - 1], gr_.at[j, i - 1], (other, t))

    for j in range(PER):
        for h in range(NF):
            lo = 256 * j + HDIM * h
            dsend[j, h] = pack_half(dmixed[:, lo : lo + HDIM])
        for i in range(1, NF):
            to_clip(j, i).start()
        drecv[j, f] = dsend[j, f]
    mask = mask_ref[...]
    root = HDIM ** (-0.5)
    for j in range(PER):
        for s in range(NF):
            kall[s * TOK : (s + 1) * TOK] = qk_ref[j, s, :TOK, HDIM:]
            vall[s * TOK : (s + 1) * TOK] = open_half(qk_ref[j, s, TOK:])
        dkall[...] = jnp.zeros_like(dkall)
        dvall[...] = jnp.zeros_like(dvall)
        for i in range(1, NF):
            to_clip(j, i).wait_recv()

        def attend(s, carry):
            q = qk_ref[j, s, :TOK, :HDIM]
            dmix = open_half(drecv[j, s])
            scores = nt(kall[...], q) * root + mask
            top = jnp.max(scores, 0, keepdims=True)
            expo = jnp.exp(scores - top)
            probs = expo * (1.0 / jnp.sum(expo, 0, keepdims=True))
            dprob = nt(vall[...], dmix)
            inner = jnp.sum(probs * dprob, 0, keepdims=True)
            dscore = (probs * (dprob - inner)).astype(BF)
            dvall[...] += nn(probs.astype(BF), dmix)
            dkall[...] += nn(dscore, q)
            dqall[s] = (tn(dscore, kall[...]) * root).astype(BF)
            return carry

        lax.fori_loop(0, NF, attend, 0)
        for s in range(NF):
            span = slice(s * TOK, (s + 1) * TOK)
            gsend[j, s, :TOK] = jnp.concatenate(
                [dqall[s], (dkall[span] * root).astype(BF)], 1
            )
            gsend[j, s, TOK:] = pack_half(dvall[span].astype(BF))
        for i in range(1, NF):
            back_clip(j, i).start()
        grecv[j, f] = gsend[j, f]
    for j in range(PER):
        for i in range(1, NF):
            back_clip(j, i).wait_recv()
        cols = slice(256 * j, 256 * (j + 1))
        ba_ref[0, :, cols] = jnp.concatenate([grecv[j, h, :TOK, :HDIM] for h in range(NF)], 1)
        ba_ref[1, :, cols] = jnp.concatenate([grecv[j, h, :TOK, HDIM:] for h in range(NF)], 1)
        ba_ref[2, :, cols] = jnp.concatenate([open_half(grecv[j, h, TOK:]) for h in range(NF)], 1)
    rowg_ref[4:5, :] = jnp.sum(ba_ref[0].astype(F32), 0, keepdims=True)
    rowg_ref[5:6, :] = jnp.sum(ba_ref[2].astype(F32), 0, keepdims=True)
    dact = nt(ba_ref[0], wbuf[0, 0]) + nt(ba_ref[1], wbuf[0, 1]) + nt(ba_ref[2], wbuf[0, 2])
    normed, scale = norm_rows(x_ref[...])
    rowg_ref[0:1, :] = jnp.sum(dact * normed, 0, keepdims=True)
    rowg_ref[1:2, :] = jnp.sum(dact, 0, keepdims=True)
    dx_ref[...] = acc[...] + norm_back(dact * rows_ref[0:1, :], normed, scale)
    for j in range(PER):
        for i in range(1, NF):
            to_clip(j, i).wait_send()
            back_clip(j, i).wait_send()


def backward_layer(layer, dout, x, x1, gp, qk, rows, mask, wcol, wdown):
    dma = pltpu.SemaphoreType.DMA
    return pl.pallas_call(
        functools.partial(backward_kernel, layer),
        out_shape=(
            jax.ShapeDtypeStruct((TOK, D), F32),
            jax.ShapeDtypeStruct((9, TOK, D), BF),
            jax.ShapeDtypeStruct((8, D), F32),
            jax.ShapeDtypeStruct((FF // D, 1, D), F32),
        ),
        in_specs=[vspec()] * 7 + [aspec()] * 2,
        out_specs=(vspec(),) * 4,
        scratch_shapes=[
            VM((2, 4, D, D), BF),
            VM((FF, D), BF),
            VM((PER, NF, TOK // 2, 128), BF),
            VM((PER, NF, TOK // 2, 128), BF),
            VM((PER, NF, QROWS, 128), BF),
            VM((PER, NF, QROWS, 128), BF),
            VM((NF * TOK, HDIM), BF),
            VM((NF * TOK, HDIM), BF),
            VM((NF * TOK, HDIM), F32),
            VM((NF * TOK, HDIM), F32),
            VM((NF, TOK, HDIM), BF),
            VM((TOK, D), F32),
            dma((3,)),
            dma((PER, NF - 1)), dma((PER, NF - 1)), dma((PER, NF - 1)), dma((PER, NF - 1)),
        ],
        compiler_params=pltpu.CompilerParams(
            collective_id=2 + L + layer, has_side_effects=True, vmem_limit_bytes=VLIM
        ),
        name="backward_layer",
    )(dout, x, x1, gp, qk, rows, mask, wcol, wdown)


RGROUPS = (("d", 1), ("u", 1), ("q", 1), ("d", 0), ("u", 0), ("q", 0), ("m", 0))


def reduce_kernel(
    times, fa0, fa1, ba0, ba1, ma, small,
    gcol, gdown, small_all, square_all, rfa0, rfa1, rba0, rba1, rma,
    lbuf, rbuf, full, low, recv1, mid_own, mid_low, recv2, zlow, zown, zrecv, sq,
    ls, cs, cr, s1, r1, s2, r2, zs, zr, fs, fr, ks, kr, ss, sr, qs, qr,
):
    f, t, y, c, g, x = place()
    count = times // 2
    over_x = (f, g * 2 + 1 - x)
    over_y = ((1 - y) * 2 + c, t)
    over_c = (y * 2 + 1 - c, t)
    total = len(RGROUPS)
    fas, rfas = (fa0, fa1), (rfa0, rfa1)
    bas, rbas = (ba0, ba1), (rba0, rba1)
    greet_all(times)

    def operands(gi, core):
        kind, l = RGROUPS[gi]
        out = []
        if kind == "d":
            for k in range(4):
                out.append((fas[l], rfas[l], 3 + k, None, lbuf, k))
            out.append((bas[l], rbas[l], 8, pl.ds(pl.multiple_of(core * 384, 128), 384), rbuf, 0))
            return out
        for role in range(2):
            yy = y if role == 0 else 1 - y
            if kind == "u":
                if role == 0:
                    out.append((fas[l], rfas[l], 2, None, lbuf, 0))
                out.append((bas[l], rbas[l], 4 + 2 * yy + core, None, rbuf, role))
            elif kind == "q":
                out.append((fas[l], rfas[l], yy * core, None, lbuf, role))
                out.append((bas[l], rbas[l], 2 * yy + core, None, rbuf, role))
            else:
                out.append((ma, rma, 3 * yy, None, lbuf, role))
                out.append((ma, rma, 1 + core + 3 * yy, None, rbuf, role))
        return out

    def swaps(gi):
        kind, l = RGROUPS[gi]
        co = 1 - c
        if kind == "d":
            pairs = [(fas[l], rfas[l], pl.ds(3, 4), None)]
            pairs.append((bas[l], rbas[l], 8, pl.ds(pl.multiple_of(co * 384, 128), 384)))
        elif kind == "u":
            pairs = [(fas[l], rfas[l], 2, None)]
            pairs += [(bas[l], rbas[l], 4 + 2 * yy + co, None) for yy in range(2)]
        elif kind == "q":
            pairs = [(fas[l], rfas[l], pl.ds(0, 2), None)]
            pairs += [(bas[l], rbas[l], 2 * yy + co, None) for yy in range(2)]
        else:
            pairs = [(ma, rma, 3 * yy, None) for yy in range(2)]
            pairs += [(ma, rma, 1 + co + 3 * yy, None) for yy in range(2)]
        out = []
        for n, (src, dst, idx, cols) in enumerate(pairs):
            if cols is None:
                a, b = src.at[idx], dst.at[idx]
            else:
                a, b = src.at[idx, :, cols], dst.at[idx, :, cols]
            out.append(remote(a, b, cs.at[gi, n], cr.at[gi, n], over_c))
        return out

    def loads(gi, received):
        slot = gi % 2
        out = []
        for n, (mine, other, idx, cols, buf, where) in enumerate(operands(gi, c)):
            src = other if received else mine
            rows = pl.ds(TOK, TOK) if received else pl.ds(0, TOK)
            if cols is None:
                a, b = src.at[idx], buf.at[slot, where, rows]
            else:
                a, b = src.at[idx, :, cols], buf.at[slot, where, rows, pl.ds(0, 384)]
            out.append(pltpu.make_async_copy(a, b, ls.at[slot, 1 if received else 0, n]))
        return out

    def step1(gi, h):
        slot = gi % 2
        block = low.at[slot, 0, 1] if h == 0 else low.at[slot, 1, :, 1 - x]
        return remote(
            block, recv1.at[gi, h], s1.at[gi, h], r1.at[gi, h], over_y if h == 0 else over_x
        )

    def step2(gi, h):
        slot = gi % 2
        return remote(
            mid_low.at[slot, h], recv2.at[gi, h], s2.at[gi, h], r2.at[gi, h],
            over_x if h == 0 else over_y,
        )

    def along(gi, dz):
        slot = gi % 2
        return remote(
            zlow.at[slot, (g + dz) % count], zrecv.at[gi, dz - 1], zs.at[gi, dz - 1], zr.at[gi, dz - 1],
            (f, ((g + dz) % count) * 2 + x),
        )

    def result(gi, yy):
        kind, l = RGROUPS[gi]
        if kind == "d":
            return gdown.at[l, yy, :, pl.ds(pl.multiple_of(c * 384, 128), 384)]
        idx = 4 if kind == "m" else 2 * l + (1 if kind == "u" else 0)
        return gcol.at[idx, yy, c]

    def spread_y(gi):
        block = result(gi, y)
        return remote(block, block, fs.at[gi], fr.at[gi], over_y)

    def spread_c(gi):
        block = result(gi, slice(None))
        return remote(block, block, ks.at[gi], kr.at[gi], over_c)

    def compute(gi):
        kind, _ = RGROUPS[gi]
        slot = gi % 2
        if kind == "d":
            def one(z, carry):
                prod = tn(lbuf[slot, z], rbuf[slot, 0, :, :384])
                prod = prod.reshape(2, 2, 2, 96, 384)
                for xx in range(2):
                    for yy in range(2):
                        role = (yy + y) % 2
                        for h in range(2):
                            full[slot, h, role, xx, z] = prod[xx, yy, h]
                            low[slot, h, role, xx, z] = prod[xx, yy, h].astype(BF)
                return carry

            lax.fori_loop(0, count, one, 0)
            return

        def role_loop(role, carry):
            lrole = role * 0 if kind == "u" else role
            for h in range(2):
                prod = tn(lbuf[slot, lrole], rbuf[slot, role, :, h * 384 : (h + 1) * 384])
                prod = prod.reshape(count, 2, 96, 384)
                for xx in range(2):
                    full[slot, h, role, xx] = prod[:, xx]
                    low[slot, h, role, xx] = prod[:, xx].astype(BF)
            return carry

        lax.fori_loop(0, 2, role_loop, 0)

    spread_small(times, small, small_all, ss, sr)
    for gi in range(total):
        for copy in swaps(gi):
            copy.start()
    sq[...] = jnp.zeros_like(sq)

    def begin_loads(gi):
        for copy in loads(gi, False):
            copy.start()
        for copy in swaps(gi):
            copy.wait_recv()
        for copy in loads(gi, True):
            copy.start()

    begin_loads(0)
    for step in range(total + 5):
        gi = step
        if gi < total:
            slot = gi % 2
            for copy in loads(gi, False) + loads(gi, True):
                copy.wait()
            if gi + 1 < total:
                begin_loads(gi + 1)
            if gi >= 2:
                for h in range(2):
                    step1(gi - 2, h).wait_send()
            compute(gi)
            for h in range(2):
                step1(gi, h).start()
        gi = step - 1
        if 0 <= gi < total:
            slot = gi % 2
            if gi >= 2:
                for h in range(2):
                    step2(gi - 2, h).wait_send()
            step1(gi, 0).wait_recv()
            mid_low[slot, 0] = (full[slot, 0, 0, 1 - x] + recv1[gi, 0, 1 - x].astype(F32)).astype(BF)
            step2(gi, 0).start()
            mid_own[slot, 0] = full[slot, 0, 0, x] + recv1[gi, 0, x].astype(F32)
            step1(gi, 1).wait_recv()
            mid_low[slot, 1] = (full[slot, 1, 1, x] + recv1[gi, 1, 1].astype(F32)).astype(BF)
            step2(gi, 1).start()
            mid_own[slot, 1] = full[slot, 1, 0, x] + recv1[gi, 1, 0].astype(F32)
        gi = step - 2
        if 0 <= gi < total:
            slot = gi % 2
            if gi >= 2:
                for dz in range(1, count):
                    along(gi - 2, dz).wait_send()
            for h in range(2):
                step2(gi, h).wait_recv()
                summed = mid_own[slot, h] + recv2[gi, h].astype(F32)
                zlow[slot, :, h] = summed.astype(BF)
                mid_own[slot, h] = summed
            for dz in range(1, count):
                along(gi, dz).start()
            for h in range(2):
                zown[slot, h] = mid_own[slot, h, g]
        gi = step - 3
        if 0 <= gi < total:
            slot = gi % 2
            for dz in range(1, count):
                along(gi, dz).wait_recv()
            for h in range(2):
                value = zown[slot, h]
                for dz in range(1, count):
                    value = value + zrecv[gi, dz - 1, h].astype(F32)
                sq[...] += jnp.sum((value * value).reshape(12, 8, 384), 0)
                kind, l = RGROUPS[gi]
                if kind == "d":
                    spot = pl.ds(pl.multiple_of(c * 384, 128), 384)
                    gdown[l, y, h * 96 : (h + 1) * 96, spot] = value.astype(BF)
                else:
                    idx = 4 if kind == "m" else 2 * l + (1 if kind == "u" else 0)
                    gcol[idx, y, c, :, h * 384 : (h + 1) * 384] = value.astype(BF)
            spread_y(gi).start()
        gi = step - 4
        if 0 <= gi < total:
            spread_y(gi).wait_recv()
            spread_c(gi).start()
        if step == total + 2:
            value = sq[...]
            sq[:, :128] = value[:, :128] + value[:, 128:256] + value[:, 256:]
            part = sq.at[:, pl.ds(0, 128)]
            n = NF * times
            me = f * times + t

            def send(i, carry):
                other = (me + i) % n
                remote(part, square_all.at[me], qs, qr, (other // times, other % times)).start()
                return carry

            lax.fori_loop(1, n, send, 0)
            square_all[me] = sq[:, :128]
    for gi in range(total):
        spread_c(gi).wait_recv()
        for copy in swaps(gi):
            copy.wait_send()
        spread_y(gi).wait_send()
        spread_c(gi).wait_send()
    for gi in range(total - 2, total):
        for h in range(2):
            step1(gi, h).wait_send()
            step2(gi, h).wait_send()
        for dz in range(1, count):
            along(gi, dz).wait_send()
    wait_small(times, small_all, ss, sr)
    wait_small(times, square_all, qs, qr)


def reduce_grads(times, fa, ba, ma, small):
    count = times // 2
    n = NF * times
    total = len(RGROUPS)
    dma = pltpu.SemaphoreType.DMA
    return pl.pallas_call(
        functools.partial(reduce_kernel, times),
        out_shape=(
            jax.ShapeDtypeStruct((2 * L + 1, 2, 2, 96, D), BF),
            jax.ShapeDtypeStruct((L, 2, 192, D), BF),
            jax.ShapeDtypeStruct((n, 8, 128), F32),
            jax.ShapeDtypeStruct((n, 8, 128), F32),
            jax.ShapeDtypeStruct(fa[0].shape, BF),
            jax.ShapeDtypeStruct(fa[1].shape, BF),
            jax.ShapeDtypeStruct(ba[0].shape, BF),
            jax.ShapeDtypeStruct(ba[1].shape, BF),
            jax.ShapeDtypeStruct(ma.shape, BF),
        ),
        in_specs=[aspec()] * 5 + [vspec()],
        out_specs=(vspec(),) * 4 + (aspec(),) * 5,
        scratch_shapes=[
            VM((2, 4, 2 * TOK, D), BF),
            VM((2, 2, 2 * TOK, D), BF),
            VM((2, 2, 2, 2, count, 96, 384), F32),
            VM((2, 2, 2, 2, count, 96, 384), BF),
            VM((total, 2, 2, count, 96, 384), BF),
            VM((2, 2, count, 96, 384), F32),
            VM((2, 2, count, 96, 384), BF),
            VM((total, 2, count, 96, 384), BF),
            VM((2, count, 2, 96, 384), BF),
            VM((2, 2, 96, 384), F32),
            VM((total, count - 1, 2, 96, 384), BF),
            VM((8, 384), F32),
            dma((2, 2, 8)),
            dma((total, 4)), dma((total, 4)),
            dma((total, 2)), dma((total, 2)), dma((total, 2)), dma((total, 2)),
            dma((total, count - 1)), dma((total, count - 1)),
            dma((total,)), dma((total,)), dma((total,)), dma((total,)),
            dma, dma, dma, dma,
        ],
        compiler_params=pltpu.CompilerParams(
            collective_id=2 + 2 * L, has_side_effects=True, vmem_limit_bytes=VLIM
        ),
        name="reduce_grads",
    )(fa[0], fa[1], ba[0], ba[1], ma, small)[:4]


def adam(weight, first, second, grad):
    first = DECAY_FIRST * first + (1.0 - DECAY_FIRST) * grad
    second = DECAY_SECOND * second + (1.0 - DECAY_SECOND) * grad * grad
    fix_one = 1.0 - DECAY_FIRST**STEP
    fix_two = 1.0 - DECAY_SECOND**STEP
    weight = weight - LEARN_RATE * (
        first / fix_one / (jnp.sqrt(second / fix_two) + EPSILON) + WEIGHT_DECAY * weight
    )
    return (weight, first, second)


def pad_to(v, axis, size):
    pads = [(0, 0)] * v.ndim
    pads[axis] = (0, size - v.shape[axis])
    return jnp.pad(v, pads)


def local(
    patches, column_mask, labels, clip_weights, wide_weights, down_weights, embedding, classifier,
    vectors, class_bias, wide_first, down_first, embedding_first, classifier_first, vectors_first,
    bias_first, wide_second, down_second, embedding_second, classifier_second, vectors_second,
    bias_second,
):
    times = lax.axis_size("tm")
    f, t = lax.axis_index("freq"), lax.axis_index("tm")
    half = t % 2
    pair = t // 2
    rows_dev = FROWS // NF
    kernels = D // times == 96
    shard = D // times
    columns = column_mask.reshape(times, CPD, HALF) > 0
    mine_columns = lax.dynamic_index_in_dim(columns, t, 0, keepdims=False)
    raw = patches.reshape(rows_dev, CPD, HALF, PATCH)

    pixels = raw.astype(F32)
    live = mine_columns.astype(F32)[None, :, :, None]
    sums = jnp.stack(
        [
            jnp.sum(pixels * live),
            jnp.sum(pixels * pixels * live),
            jnp.sum(live) * (rows_dev * PATCH),
        ]
    )
    keep_block = lax.dynamic_index_in_dim(raw, half, 1, keepdims=False)
    give_block = lax.dynamic_index_in_dim(raw, 1 - half, 1, keepdims=False)
    give_block = pad_to(give_block.reshape(rows_dev * HALF, PATCH), 0, 160)

    wide_low = wide_weights.astype(BF)
    down_low = down_weights.astype(BF)
    embed_t = pad_to(embedding.astype(BF).T, 1, 2 * D)
    class_vec = jnp.concatenate([classifier.astype(BF), vectors.astype(BF).T], 1)
    class_vec = pad_to(class_vec, 1, D)
    if kernels:
        units = jnp.concatenate(
            [
                wide_low.reshape(L, shard, 2, 4, D).transpose(0, 2, 3, 1, 4).reshape(2 * L, 4, shard, D),
                jnp.stack([embed_t[:, :D], embed_t[:, D:], class_vec, jnp.zeros_like(class_vec)])[None],
            ],
            0,
        ).reshape(2 * L + 1, 2, 2, shard, D)
        wcol, wdown, sall, take_block = gather_weights(
            times, units, down_low.reshape(L, 2, 192, D), jnp.broadcast_to(pad_to(sums, 0, 128), (8, 128)), give_block
        )
        wcol = wcol.reshape(2 * L + 1, 4, D, D)
        wdown = wdown.reshape(L, FF, D)
        embed_all = jnp.concatenate([wcol[4, 0], wcol[4, 1]], 1)
        class_vec_all = wcol[4, 2]
        sums = jnp.sum(sall[:, 0, :3], 0)
    else:
        wide_all = lax.all_gather(wide_low, "tm", axis=1, tiled=True)
        wcol = wide_all.reshape(L, D, 2, 4, D).transpose(0, 2, 3, 1, 4).reshape(2 * L, 4, D, D)
        wdown = lax.all_gather(down_low, "tm", axis=1, tiled=True)
        embed_all = lax.all_gather(embed_t, "tm", axis=0, tiled=True)
        class_vec_all = lax.all_gather(class_vec, "tm", axis=0, tiled=True)
        sums = lax.psum(sums, ("freq", "tm"))
        take_block = lax.ppermute(
            give_block, "tm", [(i, i + 1 - 2 * (i % 2)) for i in range(times)]
        )
    class_all = class_vec_all[:, :CLASSES]
    vec_all = class_vec_all[:, CLASSES : CLASSES + VROWS].T.astype(F32)
    take_block = take_block[: rows_dev * HALF].reshape(rows_dev, HALF, PATCH)
    clip_pixels = jnp.where(
        half == 0,
        jnp.stack([keep_block, take_block], 1),
        jnp.stack([take_block, keep_block], 1),
    ).reshape(rows_dev * 2 * HALF, PATCH)

    center = sums[0] / sums[2]
    mel_scale = lax.rsqrt(sums[1] / sums[2] - center * center + 1e-05)
    pnorm = ((clip_pixels.astype(F32) - center) * mel_scale).astype(BF)
    grid_rows = rows_dev * 2 * HALF
    positions = lax.dynamic_slice(embed_all, (0, f * grid_rows), (D, grid_rows)).T.astype(F32)
    grid = (
        jnp.einsum("rp,dp->rd", pnorm, embed_all[:, NGRID : NGRID + PATCH], preferred_element_type=F32)
        + vec_all[GLOB]
        + positions
    )
    x = jnp.concatenate(
        [grid, vec_all[GLOB + 1 : GLOB + 3], jnp.zeros((TOK - grid_rows - 2, D), F32)], 0
    )

    clip_columns = lax.dynamic_slice(columns, (pair * 2, half, 0), (2, 1, HALF)).reshape(2 * HALF)
    slots = jnp.concatenate(
        [
            jnp.broadcast_to(jnp.tile(clip_columns, rows_dev), (NF, grid_rows)),
            jnp.broadcast_to((jnp.arange(NF) == 0)[:, None], (NF, 2)),
            jnp.zeros((NF, TOK - grid_rows - 2), bool),
        ],
        1,
    ).reshape(NF * TOK)
    mask = jnp.where(slots, 0.0, -1e30).astype(F32)

    saved = []
    fa = []
    for layer in range(L):
        rows = vec_all[layer * 8 : layer * 8 + 8]
        up_bias = vec_all[L * 8 + layer * 4 : L * 8 + layer * 4 + 4].reshape(4, 1, D)
        x_in = x
        x, x1, acts, gp, qk = forward_layer(layer, x, rows, up_bias, mask.reshape(1, -1), wcol, wdown)
        saved.append((x_in, x1, gp, qk))
        fa.append(acts)

    owner = (f == 0).astype(F32)
    special = x[grid_rows : grid_rows + 2]
    normed_end, scale_end = norm_rows(special)
    feature = jnp.mean(normed_end * vec_all[GLOB + 3] + vec_all[GLOB + 4], 0, keepdims=True).astype(BF)
    logits = nn(feature, class_all) + class_bias
    clip = pair * CPD + half
    flags = lax.dynamic_slice_in_dim(labels, clip, 1, 0).astype(F32)
    weight = lax.dynamic_slice_in_dim(clip_weights, clip, 1, 0).astype(F32)[:, None]
    weight_total = jnp.sum(clip_weights).astype(F32)
    loss_part = owner * jnp.sum(weight * (jax.nn.softplus(logits) - flags * logits))
    dlogits = owner * weight * (jax.nn.sigmoid(logits) - flags) / weight_total
    dlogits_low = dlogits.astype(BF)
    dfinal = jnp.broadcast_to(0.5 * nt(dlogits_low, class_all), (2, D))
    dspecial = norm_back(dfinal * vec_all[GLOB + 3], normed_end, scale_end)
    end_rows = jnp.stack([jnp.sum(dfinal * normed_end, 0), jnp.sum(dfinal, 0)])
    dx = jnp.concatenate(
        [jnp.zeros((grid_rows, D), F32), dspecial, jnp.zeros((TOK - grid_rows - 2, D), F32)], 0
    )
    ba = [None] * L
    row_grads = [None] * L
    up_grads = [None] * L
    for layer in reversed(range(L)):
        rows = vec_all[layer * 8 : layer * 8 + 8]
        x_in, x1, gp, qk = saved[layer]
        dx, ba[layer], row_grads[layer], up = backward_layer(
            layer, dx, x_in, x1, gp, qk, rows, mask.reshape(-1, 1), wcol, wdown
        )
        up_grads[layer] = up.reshape(4, D)
    dgrid = dx[:grid_rows]
    grad_vec = jnp.concatenate(
        row_grads + up_grads + [jnp.sum(dgrid, 0, keepdims=True), dx[grid_rows : grid_rows + 2], end_rows], 0
    )

    vec_high = grad_vec.astype(BF)
    vec_low = (grad_vec - vec_high.astype(F32)).astype(BF)
    left = pad_to(jnp.concatenate([feature, vec_high, vec_low], 0), 0, TOK)
    pick = (
        jnp.arange(D)[None, :] == CLASSES + jnp.arange(VROWS)[:, None]
    ).astype(BF)
    right = pad_to(jnp.concatenate([pad_to(dlogits_low, 1, D), pick, pick], 0), 0, TOK)
    spot = jnp.arange(TOK)
    place_pos = (
        (jnp.arange(NGRID)[None, :] == f * grid_rows + spot[:, None]) & (spot[:, None] < grid_rows)
    ).astype(BF)
    grid_right = jnp.concatenate(
        [place_pos, pad_to(pnorm, 0, TOK), jnp.zeros((TOK, 2 * D - NGRID - PATCH), BF)], 1
    )
    dx_low = jnp.where(spot[:, None] < grid_rows, dx, 0.0).astype(BF)
    misc = jnp.stack(
        [dx_low, grid_right[:, :D], grid_right[:, D:], left, right, jnp.zeros((TOK, D), BF)]
    )
    small = jnp.concatenate([dlogits.reshape(-1), loss_part.reshape(1)])
    small = pad_to(small, 0, 1024).reshape(8, 128)
    if kernels:
        gcol, gdown, small_all, square_all = reduce_grads(times, fa, ba, misc, small)
        small = jnp.sum(small_all, 0).reshape(-1)
        square_total = jnp.sum(square_all)
        gcol = gcol.reshape(2 * L + 1, 4, shard, D).astype(F32)
        grad_wide = gcol[: 2 * L].reshape(L, 2, 4, shard, D).transpose(0, 3, 1, 2, 4).reshape(L, shard, 8 * D)
        grad_down = gdown.reshape(L, FF // times, D).astype(F32)
        grad_embed = jnp.concatenate([gcol[4, 0], gcol[4, 1]], 1)
        grad_cv = gcol[4, 2]
    else:
        ein = functools.partial(jnp.einsum, preferred_element_type=F32)
        wides, downs = [], []
        for l in range(L):
            cols = [tn(fa[l][0], ba[l][i]) for i in range(3)]
            cols += [tn(fa[l][1], ba[l][3])]
            cols += [tn(fa[l][2], ba[l][4 + i]) for i in range(4)]
            wides.append(jnp.concatenate(cols, 1))
            downs.append(jnp.concatenate([tn(fa[l][3 + i], ba[l][8]) for i in range(4)], 0))
        grad_wide = lax.psum_scatter(jnp.stack(wides), "tm", scatter_dimension=1, tiled=True)
        grad_down = lax.psum_scatter(jnp.stack(downs), "tm", scatter_dimension=1, tiled=True)
        grad_embed = lax.psum_scatter(
            jnp.concatenate([tn(misc[0], misc[1]), tn(misc[0], misc[2])], 1), "tm", scatter_dimension=0, tiled=True
        )
        grad_cv = lax.psum_scatter(tn(misc[3], misc[4]), "tm", scatter_dimension=0, tiled=True)
        grad_wide, grad_down, grad_embed, grad_cv = lax.psum(
            (grad_wide, grad_down, grad_embed, grad_cv), "freq"
        )
        squares = sum(jnp.sum(v * v) for v in (grad_wide, grad_down, grad_embed, grad_cv))
        square_total, small = lax.psum(
            (jnp.where(f == 0, squares, 0.0), small.reshape(-1)), ("freq", "tm")
        )
    grad_embed = grad_embed[:, : NGRID + PATCH].T
    grad_class = grad_cv[:, :CLASSES]
    grad_vectors = grad_cv[:, CLASSES : CLASSES + VROWS].T
    grad_bias = small[:CLASSES]
    loss_sum = small[CLASSES]
    grad_norm = jnp.sqrt(square_total + jnp.sum(grad_bias * grad_bias))
    coef = jnp.minimum(1.0, 1.0 / (grad_norm + 1e-06))

    params = (wide_weights, down_weights, embedding, classifier, vectors, class_bias)
    firsts = (wide_first, down_first, embedding_first, classifier_first, vectors_first, bias_first)
    seconds = (wide_second, down_second, embedding_second, classifier_second, vectors_second, bias_second)
    grads = (grad_wide, grad_down, grad_embed, grad_class, grad_vectors, grad_bias)
    news = [adam(w, m, v, g * coef) for w, m, v, g in zip(params, firsts, seconds, grads)]
    masters = [n[0] for n in news]
    return (
        *masters,
        *[n[1] for n in news],
        *[n[2] for n in news],
        *[m.astype(BF) for m in masters[:4]],
        grad_norm,
        loss_sum,
        weight_total,
    )


def solution(mesh):
    split = (
        P(None, "tm", None), P(None, "tm", None), P(None, "tm"), P("tm", None), P(None, "tm"), P(),
    )
    return jax.shard_map(
        local,
        mesh=mesh,
        in_specs=(P("freq", "tm", None), P(), P(), P()) + split * 3,
        out_specs=split * 3 + split[:4] + (P(), P(), P()),
        check_vma=False,
    )
```

time: 3070 us -> 680 us (0.22)
  waiting for transfers between devices: 1950 us -> 0 us
  Pallas kernels: 0 us -> 559 us
  blocking collectives: 529 us -> 0 us
  matrix products: 188 us -> 2.38 us
  other arithmetic: 189 us -> 49.5 us
  local copies, waits for them, and re-layouts: 160 us -> 48.5 us
    reduce_scatter x3 -> x0, waiting for transfers between devices: 926 us -> none  [the longest x1 609 us: local(): lax.psum_scatter(grad_wide, 'tm', scatter_dimension=1, tiled=True)]
    pallas_call x0 -> x6, Pallas kernels: none -> 559 us  [the longest x1 193 us: reduce_grads(): pl.pallas_call(functools.partial(reduce_kernel, times), out_shape=(jax.Sh...]
    ppermute x4 -> x0, waiting for transfers between devices: 450 us -> none  [swapped(): return lax.ppermute(block, axis, route)]
    all_gather x5 -> x0, waiting for transfers between devices: 374 us -> none  [the longest x1 309 us: local(): lax.all_gather(wide_weights.astype(jnp.bfloat16), 'tm', axis=1, tiled=True)]
    unnamed x2 -> x0, blocking collectives: 272 us -> none
    dot_general x41 -> x3, matrix products: 188 us -> 2.38 us  [the longest x1 1.76 us: local(): jnp.einsum('rp,dp->rd', pnorm, embed_all[:, NGRID:NGRID + PATCH], preferr...]
    all_gather x2 -> x0, blocking collectives: 163 us -> none  [the longest x1 112 us: local(): lax.all_gather(classifier.astype(jnp.bfloat16), 'tm', axis=0, tiled=True)]
    psum x1 -> x0, waiting for transfers between devices: 136 us -> none  [local(): lax.psum((grad_wide, grad_down, grad_embed, grad_class, grad_vectors), 'f...]
  transfers between devices with their start and end apart: 15 -> 0, of which waited for: 11 -> 0; matrix products, arithmetic and copies ran while one was open for 7% -> 0% of each run, Pallas kernels for 0% -> 0%
where the time goes in v1:
time: 680 us; the launch traced here: 671 us
  Pallas kernels  559 us (82%)
  other arithmetic  49.5 us (7%)
  local copies, waits for them, and re-layouts  48.5 us (7%)
  between operations  11.4 us (2%)
    pallas_call x1, Pallas kernels, reduce_grads(): pl.pallas_call(functools.partial(reduce_kernel, times), out_shape=(jax.Sh...  193 us
    pallas_call x1, Pallas kernels, gather_weights(): pl.pallas_call(functools.partial(gather_kernel, times), out_shape=(jax.Sh...  174 us
    pallas_call x2, Pallas kernels, backward_layer(): pl.pallas_call(functools.partial(backward_kernel, layer), out_shape=(jax....  113 us
    pallas_call x2, Pallas kernels, forward_layer(): pl.pallas_call(functools.partial(forward_kernel, layer), out_shape=(jax.S...  78.7 us
    convert_element_type x4, other arithmetic, local(): m.astype(BF)  21.6 us
    unnamed x62, local copies, waits for them, and re-layouts  14.6 us

profile of v1, /device:TPU:0, one launch (start us, length us, event | category | flops | bytes accessed | tf_op | source)
XLA Modules:
  0.0 670.5 jit_solution(11493888568034222088)
XLA Ops:
  0.7 0.9 reshape.251
  1.7 0.7 broadcast_compare_fusion
  2.6 1.7 fusion.24
  4.3 0.6 fusion.43
  5.6 1.4 select_maximum_fusion.1
  6.9 1.1 convert_bitcast_fusion.1
  8.0 1.0 convert_element_type.139
  9.4 2.6 convert_element_type.137
  12.1 3.0 reshape.252
  15.0 2.2 copy.97
  17.5 1.4 copy-done.2
  19.0 173.7 %gather_weights.1 = (bf16[5,2,2,4,2,96,768]{6,5,4,3,2,1,0:T(8,128)(2,1)}, bf16[2,4,2,2,192,768]{5,4,3,2,1,0:T(8,128)(2,1)S(1)}, f32[32,8,128]{2,1,0:T(8,128)S(1)}, bf16[160,256]{1,0:T(8,128)(2,1)S(1)}) custom-call(bf16[5,2,2,96,768]{4,3,2,1,0:T(8,128)(2,1)S(1)} %pad_maximum_fusion.ucol, bf16[2,2,192,768]{3,2,1,0:T(8,128)(2,1)S(1)} %bitcast.114, ...), custom_call_target="tpu_custom_call" | custom-call | tf_op jit(solution)/shard_map/gather_weights/pallas_call | solution.py:216
  192.7 3.6 copy-done
  196.3 0.6 fusion.59
  199.8 3.2 slice_bitcast_fusion.2
  203.1 0.7 slice_reduce_fusion.1
  203.8 1.8 fusion.4
  206.0 1.3 copy.102.x_ref
  207.5 0.8 copy.103.rows_ref
  208.5 0.8 copy.104.upb_ref
  209.7 0.7 select_n.88.mask_ref
  210.4 38.4 %forward_layer.2 = (f32[320,768]{1,0:T(8,128)}, f32[320,768]{1,0:T(8,128)}, bf16[7,320,768]{2,1,0:T(8,128)(2,1)}, f32[4,320,768]{2,1,0:T(8,128)}, bf16[3,4,480,128]{3,2,1,0:T(8,128)(2,1)}) custom-call(f32[320,768]{1,0:T(8,128)} %copy.102.x_ref, f32[8,768]{1,0:T(8,128)} %copy.103.rows_ref, f32[4,1,768]{2,1,0:T(1,128)} %copy.104.upb_ref, ...), custom_call_target="tpu_custom_call" | custom-call | tf_op jit(solution)/shard_map/forward_layer/pallas_call | solution.py:366
  248.8 0.7 copy.105.rows_ref
  249.5 0.7 copy.106.upb_ref
  250.3 40.4 %forward_layer.3 = (f32[320,768]{1,0:T(8,128)}, f32[320,768]{1,0:T(8,128)}, bf16[7,320,768]{2,1,0:T(8,128)(2,1)}, f32[4,320,768]{2,1,0:T(8,128)}, bf16[3,4,480,128]{3,2,1,0:T(8,128)(2,1)}) custom-call(f32[320,768]{1,0:T(8,128)} %get-tuple-element.56.x_ref, f32[8,768]{1,0:T(8,128)} %copy.105.rows_ref, f32[4,1,768]{2,1,0:T(1,128)} %copy.106.upb_ref, ...), custom_call_target="tpu_custom_call" | custom-call | tf_op jit(solution)/shard_map/forward_layer/pallas_call | solution.py:366
  290.7 0.9 slice_reduce_fusion.5
  291.5 0.9 multiply_reduce_fusion.2
  292.5 0.8 add_reduce_fusion
  293.6 0.6 dynamic_slice.28
  294.9 0.6 reduce_sum.155
  296.2 1.4 fusion.54
  298.2 0.7 fusion.40.small
  299.2 0.6 fusion.55
  300.7 1.1 maximum_maximum_fusion.1.dout_ref
  301.8 1.4 select_n.94.mask_ref
  303.2 56.0 %backward_layer.2 = (f32[320,768]{1,0:T(8,128)}, bf16[9,320,768]{2,1,0:T(8,128)(2,1)}, f32[8,768]{1,0:T(8,128)}, f32[4,1,768]{2,1,0:T(1,128)}) custom-call(f32[320,768]{1,0:T(8,128)} %maximum_maximum_fusion.1.dout_ref, f32[320,768]{1,0:T(8,128)} %get-tuple-element.56.x_ref, f32[320,768]{1,0:T(8,128)} %get-tuple-element.59.x1_ref, ...), custom_call_target="tpu_custom_call" | custom-call | tf_op jit(solution)/shard_map/backward_layer/pallas_call | solution.py:513
  359.2 56.9 %backward_layer.3 = (f32[320,768]{1,0:T(8,128)}, bf16[9,320,768]{2,1,0:T(8,128)(2,1)}, f32[8,768]{1,0:T(8,128)}, f32[4,1,768]{2,1,0:T(1,128)}) custom-call(f32[320,768]{1,0:T(8,128)} %get-tuple-element.62.dout_ref, f32[320,768]{1,0:T(8,128)} %copy.102.x_ref, f32[320,768]{1,0:T(8,128)} %get-tuple-element.63.x1_ref, f32[4,320,768]{2,1,0:T(8,128)} %get-tuple-element.64.gp_ref, ...), custom_call_target="tpu_custom_call" | custom-call | tf_op jit(solution)/shard_map/backward_layer/pallas_call | solution.py:513
  416.1 0.7 copy.148
  416.8 1.3 slice_reduce_fusion
  418.1 0.7 slice.136
  418.9 0.8 concatenate.50
  419.7 2.1 fusion.16
  422.2 0.8 fusion.22
  423.4 0.8 fusion.21
  424.3 0.8 fusion.20
  425.2 0.8 bitcast_dynamic-update-slice_fusion
  426.0 0.8 broadcast_dynamic-update-slice_fusion.ma
  426.8 193.5 %reduce_grads.1 = (bf16[5,2,2,96,768]{4,3,2,1,0:T(8,128)(2,1)}, bf16[2,2,192,768]{3,2,1,0:T(8,128)(2,1)}, f32[32,8,128]{2,1,0:T(8,128)}, f32[32,8,128]{2,1,0:T(8...) custom-call(bf16[7,320,768]{2,1,0:T(8,128)(2,1)} %get-tuple-element., ...), custom_call_target="tpu_custom_call" | custom-call | tf_op jit(solution)/shard_map/reduce_grads/pallas_call | solution.py:805
  620.3 2.5 convert_element_type.163
  622.9 2.5 copy-done.1
  625.7 0.6 multiply_reduce_fusion.3
  626.3 0.6 reduce_sum.161
  629.2 0.7 convert_element_type.169
  629.9 0.6 multiply_subtract_fusion.5
  630.5 0.6 multiply_subtract_fusion.4
  631.2 0.9 copy.121
  632.0 0.9 copy.122
  632.9 3.0 fusion.45
  636.1 1.4 copy-done.3
  637.6 4.8 fusion.47
  642.8 5.2 copy.113
  648.0 6.2 mul.382
  654.2 13.0 %fusion.49 = (bf16[2,96,6144]{2,1,0:T(8,128)(2,1)}, f32[2,96,6144]{2,1,0:T(8,128)}, f32[2,96,6144]{2,1,0:T(8,128)}, f32[2,96,6144]{2,1,0:T(8,128)}) fusion(f32[2,96,6144]{2,1,0:T(8,128)} %param.26, f32[2,96,6144]{2,1,0:T(8,128)} %mul.382, f32[2,96,6144]{2,1,0:T(8,128)} %param.32, f32[2,96,6144]{2,1,0:T(8,128)} %param.38), kind=kLoop, calls=%fused_computation.146 | loop fusion | flops 17694720 | bytes 35389440 | tf_op jit(solution)/shard_map/convert_element_type | solution.py:1071
  667.3 0.6 slice.145
  (120 shorter events, 6.2 us)
Async XLA Ops:
  0.7 8.3 %copy-start.14 = (f32[29,96]{1,0:T(8,128)S(1)}, f32[29,96]{1,0:T(8,128)}, u32[]{:S(2)}) copy-start(f32[29,96]{1,0:T(8,128)} %param.30) | copy-start | bytes 33412
  17.2 1.7 copy-start.2
  192.7 3.6 copy-start
  250.3 43.3 %copy-start.18 = (f32[527]{0:T(1024)S(1)}, f32[527]{0:T(1024)}, u32[]{:S(2)}) copy-start(f32[527]{0:T(1024)} %param.31) | copy-start | bytes 6328
  250.3 43.3 %copy-start.22 = (s32[8]{0:T(128)S(1)}, s32[8]{0:T(128)}, u32[]{:S(2)}) copy-start(s32[8]{0:T(128)} %param.25) | copy-start | bytes 100
  359.2 59.7 %copy-start.19 = (f32[4,1,768]{2,1,0:T(1,128)S(1)}, f32[4,1,768]{2,1,0:T(1,128)}, u32[]{:S(2)}) copy-start(f32[4,1,768]{2,1,0:T(1,128)} %get-tuple-element.72) | copy-start | bytes 36868
  359.2 59.7 %copy-start.15 = (f32[8,768]{1,0:T(8,128)S(1)}, f32[8,768]{1,0:T(8,128)}, u32[]{:S(2)}) copy-start(f32[8,768]{1,0:T(8,128)} %get-tuple-element.70) | copy-start | bytes 73732
  622.8 2.5 copy-start.1
  622.8 2.8 copy-start.13
  622.9 3.4 copy-start.12
  622.9 5.4 copy-start.10
  622.9 5.6 copy-start.11
  622.9 5.7 copy-start.8
  625.6 4.3 copy-start.20
  625.6 4.3 copy-start.21
  625.6 4.9 copy-start.16
  625.6 4.9 copy-start.17
  628.6 4.2 copy-start.6
  629.1 6.7 %copy-start.9 = (f32[96,527]{1,0:T(8,128)}, f32[96,527]{1,0:T(8,128)S(1)}, u32[]{:S(2)}) copy-start(f32[96,527]{1,0:T(8,128)S(1)} %copy.120) | copy-start | bytes 607108
  632.0 3.9 copy-start.7
  632.9 3.2 copy-start.4
  632.9 3.3 copy-start.5
  635.9 1.7 copy-start.3
  635.9 6.5 slice-start
  637.6 4.8 slice-start.1

commit v2 on v1

v2 whole, which is shorter than its diff:
```python
import functools

import jax
import jax.numpy as jnp
from jax import lax
from jax.experimental import pallas as pl
from jax.experimental.pallas import tpu as pltpu
from jax.sharding import PartitionSpec as P

D = 768
HEADS = 12
HDIM = 64
FF = 3072
L = 2
FROWS = 12
HALF = 52
PATCH = 256
STEP = 5
CPD = 2
NGRID = FROWS * 2 * HALF
CLASSES = 527
VROWS = 29
GLOB = L * 8 + L * (FF // D)

TOK = 320
PER = 3
NF = 4

DECAY_FIRST = 0.5
DECAY_SECOND = 0.5
LEARN_RATE = 0.03
WEIGHT_DECAY = 0.05
EPSILON = 1e-08

MESH = pl.DeviceIdType.MESH
BF = jnp.bfloat16
F32 = jnp.float32
VLIM = 60 * 1024 * 1024
VM = pltpu.VMEM


def nn(a, b):
    return lax.dot_general(a, b, (((1,), (0,)), ((), ())), preferred_element_type=F32)


def nt(a, b):
    return lax.dot_general(a, b, (((1,), (1,)), ((), ())), preferred_element_type=F32)


def tn(a, b):
    return lax.dot_general(a, b, (((0,), (0,)), ((), ())), preferred_element_type=F32)


def norm_rows(x):
    center = jnp.mean(x, -1, keepdims=True)
    shifted = x - center
    scale = lax.rsqrt(jnp.mean(shifted * shifted, -1, keepdims=True) + 1e-06)
    return (shifted * scale, scale)


def norm_back(dnorm, normed, scale):
    return scale * (
        dnorm
        - jnp.mean(dnorm, -1, keepdims=True)
        - normed * jnp.mean(dnorm * normed, -1, keepdims=True)
    )


def vspec():
    return pl.BlockSpec(memory_space=VM)


def aspec():
    return pl.BlockSpec(memory_space=pl.ANY)


def place():
    f, t = lax.axis_index("freq"), lax.axis_index("tm")
    return f, t, f // 2, f % 2, t // 2, t % 2


def remote(src, dst, ssem, rsem, dev):
    return pltpu.make_async_remote_copy(
        src_ref=src, dst_ref=dst, send_sem=ssem, recv_sem=rsem, device_id=dev, device_id_type=MESH
    )


def greet_all(times):
    f, t = lax.axis_index("freq"), lax.axis_index("tm")
    n = NF * times
    me = f * times + t
    barrier = pltpu.get_barrier_semaphore()

    def hello(i, carry):
        other = (me + i) % n
        pl.semaphore_signal(
            barrier, inc=1, device_id=(other // times, other % times), device_id_type=MESH
        )
        return carry

    lax.fori_loop(1, n, hello, 0)
    pl.semaphore_wait(barrier, n - 1)


def spread_small(times, small, gathered, ssem, rsem):
    f, t = lax.axis_index("freq"), lax.axis_index("tm")
    n = NF * times
    me = f * times + t

    def send(i, carry):
        other = (me + i) % n
        remote(
            small, gathered.at[me], ssem, rsem, (other // times, other % times)
        ).start()
        return carry

    lax.fori_loop(1, n, send, 0)
    gathered[me] = small[...]


def wait_small(times, gathered, ssem, rsem):
    n = NF * times
    many = gathered.at[pl.ds(0, n - 1)]
    pltpu.make_async_copy(many, many, rsem).wait()
    pltpu.make_async_copy(many, many, ssem).wait()


QROWS = TOK + TOK // 2
SLOTS = TOK // 2
GRID = FROWS // NF * HALF
EWIDE = 384
EVEC = TOK
ECLS = 352
CMAIN = 512


def greet_clip():
    f, t = lax.axis_index("freq"), lax.axis_index("tm")
    barrier = pltpu.get_barrier_semaphore()
    for i in range(1, NF):
        pl.semaphore_signal(barrier, inc=1, device_id=((f + i) % NF, t), device_id_type=MESH)
    pl.semaphore_wait(barrier, NF - 1)


def pack_half(v):
    return jnp.concatenate([v[: TOK // 2], v[TOK // 2 :]], 1)


def open_half(v):
    return jnp.concatenate([v[:, :HDIM], v[:, HDIM:]], 0)


def exchange_sems():
    dma = pltpu.SemaphoreType.DMA
    return [dma((PER, NF - 1))] * 4


FORWARD_SCRATCH = [
    VM((2, 2, 2, 4, 2, 96, D), BF),
    VM((4, 2, 2, 192, D), BF),
    VM((PER, NF, QROWS, 128), BF),
    VM((PER, NF, TOK // 2, 128), BF),
    VM((NF * TOK, HDIM), BF),
    VM((NF * TOK, HDIM), BF),
    VM((TOK, D), F32),
]


def layer_body(layer, x_ref, vec_ref, mask_ref, outs, scratch, orecv, sems, fetch, tick):
    xo_ref, x1_ref, fa_ref, gp_ref, qk_ref = outs
    wbuf, dbuf, qsend, osend, kall, vall, acc = scratch
    qs, qr, os, orr = sems
    f, t = lax.axis_index("freq"), lax.axis_index("tm")

    def row(i):
        return vec_ref[EVEC + layer * 8 + i : EVEC + layer * 8 + i + 1, :]

    def mat(part, q, cols=slice(None)):
        return wbuf[part, q // 2, q % 2, :, :, :, cols].reshape(D, -1)

    normed, _ = norm_rows(x_ref[...])
    act = (normed * row(0) + row(1)).astype(BF)
    fa_ref[0] = act
    fetch(0)

    def to_clip(j, i):
        other = (f + i) % NF
        return remote(
            qsend.at[j, other], qk_ref.at[j, f], qs.at[j, i - 1], qr.at[j, i - 1], (other, t)
        )

    def back_clip(j, i):
        other = (f + i) % NF
        return remote(
            osend.at[j, other], orecv.at[j, f], os.at[j, i - 1], orr.at[j, i - 1], (other, t)
        )

    for j in range(PER):
        cols = slice(256 * j, 256 * (j + 1))
        query = (nn(act, mat(0, 0, cols)) + row(4)[:, cols]).astype(BF)
        key = nn(act, mat(0, 1, cols)).astype(BF)
        value = (nn(act, mat(0, 2, cols)) + row(5)[:, cols]).astype(BF)
        for h in range(NF):
            part = slice(HDIM * h, HDIM * (h + 1))
            qsend[j, h, :TOK] = jnp.concatenate([query[:, part], key[:, part]], 1)
            qsend[j, h, TOK:] = pack_half(value[:, part])
        for i in range(1, NF):
            to_clip(j, i).start()
        qk_ref[j, f] = qsend[j, f]
    tick()
    mask = mask_ref[...]
    for j in range(PER):
        for i in range(1, NF):
            to_clip(j, i).wait_recv()
        for s in range(NF):
            kall[s * TOK : (s + 1) * TOK] = qk_ref[j, s, :TOK, HDIM:]
            vall[s * TOK : (s + 1) * TOK] = open_half(qk_ref[j, s, TOK:])

        def attend(i, carry):
            s = (f + i) % NF
            halves = []
            for h in range(2):
                lo = h * (TOK // 2)
                q = qk_ref[j, s, lo : lo + TOK // 2, :HDIM]
                scores = nt(q, kall[...]) * (HDIM ** (-0.5)) + mask
                top = jnp.max(scores, -1, keepdims=True)
                expo = jnp.exp(scores - top)
                total = jnp.sum(expo, -1, keepdims=True)
                probs = (expo * (1.0 / total)).astype(BF)
                halves.append(nn(probs, vall[...]).astype(BF))
            osend[j, s] = jnp.concatenate(halves, 1)

            @pl.when(i > 0)
            def _():
                remote(
                    osend.at[j, s], orecv.at[j, f], os.at[j, i - 1], orr.at[j, i - 1], (s, t)
                ).start()

            return carry

        lax.fori_loop(1, NF, attend, 0)
        lax.fori_loop(0, 1, attend, 0)
        orecv[j, f] = osend[j, f]
        tick()
    parts = []
    for j in range(PER):
        for i in range(1, NF):
            back_clip(j, i).wait_recv()
        for h in range(NF):
            parts.append(open_half(orecv[j, h]))
    mixed = jnp.concatenate(parts, 1)
    fa_ref[1] = mixed
    resid = x_ref[...] + nn(mixed, mat(0, 3)) + row(6)
    x1_ref[...] = resid
    normed, _ = norm_rows(resid)
    fa_ref[2] = (normed * row(2) + row(3)).astype(BF)
    acc[...] = resid + row(7)
    fetch(1)
    fetch(2)

    def mlp(k, carry):
        bias = vec_ref[pl.ds(EVEC + L * 8 + layer * 4 + k, 1), :]
        before = nn(fa_ref[2], mat(1, k)) + bias
        lower = 0.5 * (1.0 + lax.erf(before * 0.7071067811865476))
        gp_ref[k] = lower + before * jnp.exp(-0.5 * before * before) * 0.3989422804014327
        hidden = (before * lower).astype(BF)
        fa_ref[3 + k] = hidden
        acc[...] += nn(hidden, dbuf[k].reshape(D, D))
        return carry

    for k in range(0, FF // D, 2):
        lax.fori_loop(k, k + 2, mlp, 0)
        tick()
    xo_ref[...] = acc[...]
    for j in range(PER):
        for i in range(1, NF):
            to_clip(j, i).wait_send()
            back_clip(j, i).wait_send()


def forward_kernel(
    layer, x_ref, vec_ref, mask_ref, wcol, wdown,
    xo_ref, x1_ref, fa_ref, gp_ref, qk_ref,
    wbuf, dbuf, qsend, osend, kall, vall, acc, orecv, wsem, qs, qr, os, orr,
):
    loads = [
        pltpu.make_async_copy(wcol.at[2 * layer], wbuf.at[0], wsem.at[0]),
        pltpu.make_async_copy(wcol.at[2 * layer + 1], wbuf.at[1], wsem.at[1]),
        pltpu.make_async_copy(wdown.at[layer], dbuf, wsem.at[2]),
    ]
    for load in loads:
        load.start()
    greet_clip()
    layer_body(
        layer, x_ref, vec_ref, mask_ref, (xo_ref, x1_ref, fa_ref, gp_ref, qk_ref),
        (wbuf, dbuf, qsend, osend, kall, vall, acc), orecv, (qs, qr, os, orr),
        lambda part: loads[part].wait(), lambda: None,
    )


def forward_layer(layer, x, vec, mask, wcol, wdown):
    return pl.pallas_call(
        functools.partial(forward_kernel, layer),
        out_shape=(
            jax.ShapeDtypeStruct((TOK, D), F32),
            jax.ShapeDtypeStruct((TOK, D), F32),
            jax.ShapeDtypeStruct((7, TOK, D), BF),
            jax.ShapeDtypeStruct((FF // D, TOK, D), F32),
            jax.ShapeDtypeStruct((PER, NF, QROWS, 128), BF),
        ),
        in_specs=[vspec()] * 3 + [aspec()] * 2,
        out_specs=(vspec(),) * 5,
        scratch_shapes=FORWARD_SCRATCH
        + [VM((PER, NF, TOK // 2, 128), BF), pltpu.SemaphoreType.DMA((3,))]
        + exchange_sems(),
        compiler_params=pltpu.CompilerParams(
            collective_id=2 + layer, has_side_effects=True, vmem_limit_bytes=VLIM
        ),
        name="forward_layer",
    )(x, vec, mask, wcol, wdown)


GROUPS = (("c", 0), ("c", 1), ("d", 0), ("c", 2), ("c", 3), ("d", 1))
SUBS = tuple((kind, idx, h) for kind, idx in GROUPS for h in (0, 1))
PATHS = "yzyzyzyyzyzy"
AHEAD = 3


def gather_plan():
    moves = {}
    for s, path in enumerate(PATHS):
        lag = 1 if s < 2 else 2
        times = {"along": s - AHEAD, "first": s}
        times["third"] = s + lag
        if path == "y":
            times["second"] = s + lag
            times["third"] = s + 2 * lag
        times["arrive"] = times["third"] + 1
        for action, when in times.items():
            moves.setdefault(max(when, -1), []).append((s, action))
    plan = [sorted(moves[when]) for when in sorted(moves)]
    ready = {s: n for n, step in enumerate(plan) for s, action in step if action == "arrive"}
    return plan, ready


def gather_steps(count, ucol, udown, ocol, odown, sems):
    zs, zr, own, s1, r1, s2, r2, s3, r3 = sems
    f, t, y, c, g, x = place()
    every = slice(None)

    def source(s):
        kind, idx, h = SUBS[s]
        yy = every if PATHS[s] == "z" else y
        if kind == "c":
            return ucol.at[idx, yy, c, :, pl.ds(h * 384, 384)]
        return udown.at[idx, yy, pl.ds(h * 96, 96), pl.ds(pl.multiple_of(c * 384, 128), 384)]

    def view(s, yy, zz, xx):
        kind, idx, h = SUBS[s]
        if PATHS[s] == "z":
            yy = every
        if kind == "c":
            return ocol.at[idx, yy, c, zz, xx, :, pl.ds(h * 384, 384)]
        return odown.at[
            idx, zz, xx, yy, pl.ds(h * 96, 96), pl.ds(pl.multiple_of(c * 384, 128), 384)
        ]

    def along(s, dz):
        return remote(
            source(s), view(s, y, g, x), zs.at[s, dz - 1], zr.at[s, dz - 1],
            (f, ((g + dz) % count) * 2 + x),
        )

    def keep(s):
        return pltpu.make_async_copy(source(s), view(s, y, g, x), own.at[s])

    def first(s):
        block = view(s, y, every, x)
        return remote(block, block, s1.at[s], r1.at[s], (f, g * 2 + 1 - x))

    def second(s):
        block = view(s, y, every, every)
        return remote(block, block, s2.at[s], r2.at[s], ((1 - y) * 2 + c, t))

    def third(s):
        block = view(s, every, every, every)
        return remote(block, block, s3.at[s], r3.at[s], (y * 2 + 1 - c, t))

    def act(s, action):
        if action == "along":
            keep(s).start()
            for dz in range(1, count):
                along(s, dz).start()
        elif action == "first":
            for dz in range(1, count):
                along(s, dz).wait_recv()
            keep(s).wait()
            first(s).start()
        elif action == "second":
            first(s).wait_recv()
            second(s).start()
        elif action == "third":
            (second if PATHS[s] == "y" else first)(s).wait_recv()
            third(s).start()
        else:
            third(s).wait_recv()

    for step in gather_plan()[0]:
        for s, action in step:
            act(s, action)
        yield
    for s in range(len(SUBS)):
        for dz in range(1, count):
            along(s, dz).wait_send()
        first(s).wait_send()
        if PATHS[s] == "y":
            second(s).wait_send()
        third(s).wait_send()
    yield


def forward_all_kernel(
    times, ucol, udown, uemb, upatch, uclass, stats, pkeep, psend, mask_ref,
    ocol, odown, oclass, vec_out, xs_out, fa_out, gp_out, qk_out, pn_out,
    wbuf, dbuf, qsend, osend, kall, vall, acc, orecv, sall, precv, emb, patches, classes, vec, xs, fa, gp, qk, pn,
    zs, zr, own, s1, r1, s2, r2, s3, r3, es, er, exs, exr, ss, sr, ps, pr, wsem, osem,
    qs0, qr0, os0, or0, qs1, qr1, os1, or1,
):
    f, t, y, c, g, x = place()
    count = times // 2
    over_x = (f, g * 2 + 1 - x)
    greet_all(times)
    spread_small(times, stats, sall, ss, sr)
    swap = remote(psend, precv, ps, pr, over_x)
    swap.start()
    units = ((uemb, emb), (upatch, patches), (uclass, classes))

    def unit_along(n, dz):
        src, dst = units[n]
        return remote(
            src, dst.at[g, x], es.at[n, dz - 1], er.at[n, dz - 1], (f, ((g + dz) % count) * 2 + x)
        )

    def loads(layer, part):
        if part < 2:
            return pltpu.make_async_copy(ocol.at[2 * layer + part], wbuf.at[part], wsem.at[layer, part])
        return pltpu.make_async_copy(odown.at[layer], dbuf, wsem.at[layer, part])

    def unit_over(n):
        block = units[n][1].at[:, x]
        return remote(block, block, exs.at[n], exr.at[n], over_x)

    for n in range(3):
        units[n][1][g, x] = units[n][0][...]
    for n in range(2):
        for dz in range(1, count):
            unit_along(n, dz).start()
    steps = gather_steps(count, ucol, udown, ocol, odown, (zs, zr, own, s1, r1, s2, r2, s3, r3))
    plan, ready = gather_plan()
    last = len(plan) - 1
    done = [-1]

    started, allowed = set(), {(0, part) for part in range(3)}

    def arrived(layer, part):
        group = 3 * layer + part
        return max(ready[2 * group], ready[2 * group + 1])

    def prefetch():
        for layer, part in sorted(allowed - started):
            if done[0] >= arrived(layer, part):
                loads(layer, part).start()
                started.add((layer, part))

    def tick():
        if done[0] < last:
            next(steps)
            done[0] += 1
        prefetch()

    def need(step):
        while done[0] < step:
            tick()

    need(0)
    for n in range(2):
        for dz in range(1, count):
            unit_along(n, dz).wait_recv()
        unit_over(n).start()
    need(1)
    for n in range(2):
        unit_over(n).wait_recv()
    swap.wait_recv()
    wait_small(times, sall, ss, sr)
    sums = jnp.sum(sall[...], 0)
    total, squares, live = sums[0:1, 0:1], sums[0:1, 1:2], sums[0:1, 2:3]
    center = total / live
    mel_scale = lax.rsqrt(squares / live - center * center + 1e-05)
    inside = lax.broadcasted_iota(jnp.int32, (SLOTS, PATCH), 0) < GRID

    def normalized(block):
        return jnp.where(inside, (block[...].astype(F32) - center) * mel_scale, 0.0).astype(BF)

    pn[pl.ds(pl.multiple_of(x * SLOTS, SLOTS), SLOTS)] = normalized(pkeep)
    pn[pl.ds(pl.multiple_of((1 - x) * SLOTS, SLOTS), SLOTS)] = normalized(precv)
    vec[...] = emb[...].reshape(D, EWIDE).astype(F32).T
    patch = patches[...].reshape(D, PATCH)
    bias = vec[EVEC + GLOB : EVEC + GLOB + 1, :]
    spot = lax.broadcasted_iota(jnp.int32, (TOK, D), 0)
    grid_row = jnp.logical_or(spot < GRID, jnp.logical_and(spot >= SLOTS, spot < SLOTS + GRID))
    xs[0] = (nt(pn[...], patch) + vec[:TOK]) + jnp.where(grid_row, bias, 0.0)

    copies = [
        pltpu.make_async_copy(vec, vec_out, osem.at[1]),
        pltpu.make_async_copy(pn, pn_out, osem.at[2]),
    ]
    for copy in copies:
        copy.start()
    sems = ((qs0, qr0, os0, or0), (qs1, qr1, os1, or1))
    for dz in range(1, count):
        unit_along(2, dz).start()
    for layer in range(L):
        if layer == 1:
            for dz in range(1, count):
                unit_along(2, dz).wait_recv()
            unit_over(2).start()

        def fetch(part):
            if part == 1 and layer + 1 < L:
                allowed.add((layer + 1, 0))
            need(arrived(layer, part))
            prefetch()
            loads(layer, part).wait()

        layer_body(
            layer, xs.at[2 * layer], vec, mask_ref,
            (xs.at[2 * layer + 2], xs.at[2 * layer + 1], fa.at[layer], gp.at[layer], qk.at[layer]),
            (wbuf, dbuf, qsend, osend, kall, vall, acc), orecv.at[layer], sems[layer], fetch, tick,
        )
        more = [
            pltpu.make_async_copy(fa.at[layer], fa_out.at[layer], osem.at[3 + 4 * layer]),
            pltpu.make_async_copy(gp.at[layer], gp_out.at[layer], osem.at[4 + 4 * layer]),
            pltpu.make_async_copy(qk.at[layer], qk_out.at[layer], osem.at[5 + 4 * layer]),
        ]
        if layer == 0:
            more.append(pltpu.make_async_copy(xs.at[pl.ds(0, 2)], xs_out.at[pl.ds(0, 2)], osem.at[6]))
        else:
            more.append(pltpu.make_async_copy(xs.at[pl.ds(2, 3)], xs_out.at[pl.ds(2, 3)], osem.at[10]))
        for copy in more:
            copy.start()
        copies += more
        allowed.update((layer + 1, part) for part in (1, 2) if layer + 1 < L)
    need(last)
    next(steps)
    unit_over(2).wait_recv()
    copies.append(pltpu.make_async_copy(classes, oclass, osem.at[0]))
    copies[-1].start()
    for n in range(3):
        for dz in range(1, count):
            unit_along(n, dz).wait_send()
        unit_over(n).wait_send()
    swap.wait_send()
    for copy in copies:
        copy.wait()


def forward_all(times, ucol, udown, uemb, upatch, uclass, stats, pkeep, psend, mask):
    count = times // 2
    total = len(SUBS)
    dma = pltpu.SemaphoreType.DMA
    outs = (
        ((2 * L, 2, 2, count, 2, 96, D), BF),
        ((L, count, 2, 2, 192, D), BF),
        ((count, 2, 96, CMAIN), BF),
        ((EWIDE, D), F32),
        ((2 * L + 1, TOK, D), F32),
        ((L, 7, TOK, D), BF),
        ((L, FF // D, TOK, D), F32),
        ((L, PER, NF, QROWS, 128), BF),
        ((TOK, PATCH), BF),
    )
    return pl.pallas_call(
        functools.partial(forward_all_kernel, times),
        out_shape=tuple(jax.ShapeDtypeStruct(*o) for o in outs),
        in_specs=[vspec()] * 9,
        out_specs=(aspec(),) * len(outs),
        scratch_shapes=FORWARD_SCRATCH
        + [
            VM((L, PER, NF, TOK // 2, 128), BF),
            VM((NF * times, 8, 128), F32),
            VM((SLOTS, PATCH), BF),
            VM((count, 2, 96, EWIDE), BF),
            VM((count, 2, 96, PATCH), BF),
            VM((count, 2, 96, CMAIN), BF),
            VM((EWIDE, D), F32),
            VM((2 * L + 1, TOK, D), F32),
            VM((L, 7, TOK, D), BF),
            VM((L, FF // D, TOK, D), F32),
            VM((L, PER, NF, QROWS, 128), BF),
            VM((TOK, PATCH), BF),
            dma((total, count - 1)), dma((total, count - 1)), dma((total,)),
            dma((total,)), dma((total,)), dma((total,)), dma((total,)), dma((total,)), dma((total,)),
            dma((3, count - 1)), dma((3, count - 1)), dma((3,)), dma((3,)),
            dma, dma, dma, dma, dma((L, 3)), dma((12,)),
        ]
        + exchange_sems() * L,
        compiler_params=pltpu.CompilerParams(
            collective_id=1, has_side_effects=True, vmem_limit_bytes=VLIM
        ),
        name="forward_all",
    )(ucol, udown, uemb, upatch, uclass, stats, pkeep, psend, mask)


BACKWARD_SCRATCH = [
    VM((PER, NF, TOK // 2, 128), BF),
    VM((PER, NF, TOK // 2, 128), BF),
    VM((PER, NF, QROWS, 128), BF),
    VM((PER, NF, QROWS, 128), BF),
    VM((NF * TOK, HDIM), BF),
    VM((NF * TOK, HDIM), BF),
    VM((NF * TOK, HDIM), F32),
    VM((NF * TOK, HDIM), F32),
    VM((NF, TOK, HDIM), BF),
    VM((TOK, D), F32),
]


def backward_body(layer, dcur, er, ba, vec_ref, mask_ref, qk_ref, mats, slope, kept, scratch, sems, at):
    down, up, qkvo = mats
    dsend, drecv, gsend, grecv, kall, vall, dkall, dvall, dqall, acc = scratch
    ds_, dr_, gs_, gr_ = sems
    f, t = lax.axis_index("freq"), lax.axis_index("tm")

    def row(i):
        return vec_ref[EVEC + layer * 8 + i : EVEC + layer * 8 + i + 1, :]

    def note(i, value):
        er[EVEC + i : EVEC + i + 1, :] = jnp.sum(value, 0, keepdims=True)

    ba[8] = dcur[...].astype(BF)
    note(layer * 8 + 7, dcur[...])
    for k in range(FF // D):
        dbefore = nt(ba[8], down(k)) * slope(k)
        note(L * 8 + layer * 4 + k, dbefore)
        ba[4 + k] = dbefore.astype(BF)
        product = nt(ba[4 + k], up(k))
        acc[...] = product if k == 0 else acc[...] + product
        at("mlp%d" % k)
    normed, scale = norm_rows(kept(1))
    dact = acc[...]
    note(layer * 8 + 2, dact * normed)
    note(layer * 8 + 3, dact)
    dcur[...] += norm_back(dact * row(2), normed, scale)
    note(layer * 8 + 6, dcur[...])
    ba[3] = dcur[...].astype(BF)
    at("resid")
    dmixed = nt(ba[3], qkvo(3)).astype(BF)

    def to_clip(j, i):
        other = (f + i) % NF
        return remote(
            dsend.at[j, other], drecv.at[j, f], ds_.at[j, i - 1], dr_.at[j, i - 1], (other, t)
        )

    def back_clip(j, i):
        other = (f + i) % NF
        return remote(
            gsend.at[j, other], grecv.at[j, f], gs_.at[j, i - 1], gr_.at[j, i - 1], (other, t)
        )

    for j in range(PER):
        for h in range(NF):
            lo = 256 * j + HDIM * h
            dsend[j, h] = pack_half(dmixed[:, lo : lo + HDIM])
        for i in range(1, NF):
            to_clip(j, i).start()
        drecv[j, f] = dsend[j, f]
    at("sent")
    mask = mask_ref[...]
    root = HDIM ** (-0.5)
    part = TOK // 2
    for j in range(PER):
        for s in range(NF):
            kall[s * TOK : (s + 1) * TOK] = qk_ref[j, s, :TOK, HDIM:]
            vall[s * TOK : (s + 1) * TOK] = open_half(qk_ref[j, s, TOK:])
        dkall[...] = jnp.zeros_like(dkall)
        dvall[...] = jnp.zeros_like(dvall)
        for i in range(1, NF):
            to_clip(j, i).wait_recv()

        def attend(s, carry):
            q = qk_ref[j, s, :TOK, :HDIM]
            dmix = open_half(drecv[j, s])
            scores = nt(kall[...], q) * root + mask
            top = jnp.max(scores, 0, keepdims=True)
            expo = jnp.exp(scores - top)
            probs = expo * (1.0 / jnp.sum(expo, 0, keepdims=True))
            dprob = nt(vall[...], dmix)
            inner = jnp.sum(probs * dprob, 0, keepdims=True)
            dscore = (probs * (dprob - inner)).astype(BF)
            dvall[...] += nn(probs.astype(BF), dmix)
            dkall[...] += nn(dscore, q)
            dqall[s] = (tn(dscore, kall[...]) * root).astype(BF)
            return carry

        lax.fori_loop(0, NF, attend, 0)
        for s in range(NF):
            span = slice(s * TOK, (s + 1) * TOK)
            gsend[j, s, :TOK] = jnp.concatenate([dqall[s], (dkall[span] * root).astype(BF)], 1)
            gsend[j, s, TOK:] = pack_half(dvall[span].astype(BF))
        for i in range(1, NF):
            back_clip(j, i).start()
        grecv[j, f] = gsend[j, f]
        at("head%d" % j)
    for j in range(PER):
        for i in range(1, NF):
            back_clip(j, i).wait_recv()
        cols = slice(256 * j, 256 * (j + 1))
        ba[0, :, cols] = jnp.concatenate([grecv[j, h, :TOK, :HDIM] for h in range(NF)], 1)
        ba[1, :, cols] = jnp.concatenate([grecv[j, h, :TOK, HDIM:] for h in range(NF)], 1)
        ba[2, :, cols] = jnp.concatenate([open_half(grecv[j, h, TOK:]) for h in range(NF)], 1)
    at("heads")
    note(layer * 8 + 4, ba[0].astype(F32))
    note(layer * 8 + 5, ba[2].astype(F32))
    dact = nt(ba[0], qkvo(0)) + nt(ba[1], qkvo(1)) + nt(ba[2], qkvo(2))
    normed, scale = norm_rows(kept(0))
    note(layer * 8 + 0, dact * normed)
    note(layer * 8 + 1, dact)
    dcur[...] += norm_back(dact * row(0), normed, scale)
    for j in range(PER):
        for i in range(1, NF):
            to_clip(j, i).wait_send()
            back_clip(j, i).wait_send()
    at("done")


def backward_kernel(
    layer, dout_ref, x_ref, x1_ref, gp_ref, qk_ref, vec_ref, mask_ref, wcol, wdown,
    dx_ref, ba_ref, er_ref, wbuf, dbuf, wsem, ds_, dr_, gs_, gr_, *scratch,
):
    loads = [
        pltpu.make_async_copy(wdown.at[layer], dbuf, wsem.at[0]),
        pltpu.make_async_copy(wcol.at[2 * layer + 1], wbuf.at[1], wsem.at[1]),
        pltpu.make_async_copy(wcol.at[2 * layer], wbuf.at[0], wsem.at[2]),
    ]
    for load in loads:
        load.start()
    dx_ref[...] = dout_ref[...]
    er_ref[...] = jnp.zeros_like(er_ref)
    greet_clip()
    for load in loads:
        load.wait()
    backward_body(
        layer, dx_ref, er_ref, ba_ref, vec_ref, mask_ref, qk_ref,
        (lambda k: dbuf[k], lambda k: wbuf[1, k], lambda k: wbuf[0, k]),
        lambda k: gp_ref[k], lambda i: x1_ref[...] if i else x_ref[...],
        scratch, (ds_, dr_, gs_, gr_), lambda point: None,
    )


def backward_layer(layer, dout, x, x1, gp, qk, vec, mask, wcol, wdown):
    return pl.pallas_call(
        functools.partial(backward_kernel, layer),
        out_shape=(
            jax.ShapeDtypeStruct((TOK, D), F32),
            jax.ShapeDtypeStruct((9, TOK, D), BF),
            jax.ShapeDtypeStruct((EWIDE, D), F32),
        ),
        in_specs=[vspec()] * 7 + [aspec()] * 2,
        out_specs=(vspec(),) * 3,
        scratch_shapes=[VM((2, 4, D, D), BF), VM((4, D, D), BF), pltpu.SemaphoreType.DMA((3,))]
        + exchange_sems()
        + BACKWARD_SCRATCH,
        compiler_params=pltpu.CompilerParams(
            collective_id=2 + L + layer, has_side_effects=True, vmem_limit_bytes=VLIM
        ),
        name="backward_layer",
    )(dout, x, x1, gp, qk, vec, mask, wcol, wdown)


RGROUPS = (("d", 1), ("u", 1), ("q", 1), ("d", 0), ("u", 0), ("q", 0))
RFIRST = ("xx", "yx", "xx", "xx", "yx", "xx")
SLOTS_R = 2
PWIDE = (CMAIN, EWIDE + PATCH)
STAGES = 5


def backward_all_kernel(
    times, dout_in, xs_in, gp_in, qk_in, fa_in, vec_ref, mask_ref, pn_ref, head_ref, end_ref, small, wcol, wdown,
    gcol, gdown, gpart, small_all, square_all, rfa,
    *refs,
):
    (
        wbuf, gp, xb, dcur, er, qk, ba, lbuf, rd, ru, rq, full, low, recv1, mid_own, mid_low, recv2,
        zlow, zown, zrecv, psend0, psend1, pown0, pown1, pxr0, pxr1, pzs0, pzs1, pzr0, pzr1, sq,
        wsem, gsem, xsem, qsem, ls, fas, far, bs, br, s1, r1, s2, r2, zs, zr, fs, fr, ks, kr,
        ss, sr, qs, qr, p1, p1r, p2, p2r, p3, p3r, p4, p4r, credit,
        ds_, dr_, gs_, gr_,
    ) = refs[: -len(BACKWARD_SCRATCH)]
    scratch = refs[-len(BACKWARD_SCRATCH) :]
    f, t, y, c, g, x = place()
    count = times // 2
    over_x = (f, g * 2 + 1 - x)
    over_y = ((1 - y) * 2 + c, t)
    over_c = (y * 2 + 1 - c, t)
    total = len(RGROUPS)
    other_core = 1 - c

    def half_cols(core):
        return pl.ds(pl.multiple_of(core * 384, 128), 384)

    def weight(layer, which):
        src = (wdown.at[layer], wcol.at[2 * layer + 1], wcol.at[2 * layer])[which]
        return pltpu.make_async_copy(src, wbuf.at[weight_slot(layer, which)], wsem.at[layer, which])

    def weight_slot(layer, which):
        return (which % 2 + (L - 1 - layer)) % 2

    def slope_load(layer, k):
        return pltpu.make_async_copy(gp_in.at[layer, k], gp.at[k % 2], gsem.at[layer, k])

    def kept_load(layer, i):
        return pltpu.make_async_copy(xs_in.at[2 * layer + i], xb, xsem.at[layer, i])

    def heads_load(layer):
        return pltpu.make_async_copy(qk_in.at[layer], qk, qsem.at[layer])

    first_load = pltpu.make_async_copy(dout_in, dcur, qsem.at[L])
    first_load.start()
    for which in range(2):
        weight(L - 1, which).start()
    for k in range(2):
        slope_load(L - 1, k).start()
    kept_load(L - 1, 1).start()
    heads_load(L - 1).start()
    greet_all(times)
    spread_small(times, small, small_all, ss, sr)

    def forward_swap(layer, n):
        span = pl.ds(3, 4) if n == 0 else pl.ds(0, 3)
        return remote(
            fa_in.at[layer, span], rfa.at[layer, span], fas.at[layer, n], far.at[layer, n], over_c
        )

    for layer in reversed(range(L)):
        for n in range(2):
            forward_swap(layer, n).start()

    def swap(gi, n):
        kind, l = RGROUPS[gi]
        if kind == "d":
            src, dst = ba.at[8, :, half_cols(other_core)], rd.at[l]
        elif kind == "u":
            src, dst = ba.at[4 + 2 * n + other_core], ru.at[l, n]
        else:
            src, dst = ba.at[2 * n + other_core], rq.at[l, n]
        return remote(src, dst, bs.at[gi, n], br.at[gi, n], over_c)

    def swaps(gi):
        return range(1 if RGROUPS[gi][0] == "d" else 2)

    def left_loads(gi):
        kind, l = RGROUPS[gi]
        out = []
        blocks = {"d": (3, 4, 5, 6), "u": (2,), "q": (0, c)}[kind]
        for n, block in enumerate(blocks):
            for m, src in enumerate((fa_in, rfa)):
                out.append(
                    pltpu.make_async_copy(
                        src.at[l, block], lbuf.at[n, pl.ds(m * TOK, TOK)], ls.at[n, m]
                    )
                )
        return out

    def product(left, own, other, cols):
        return tn(lbuf[left, :TOK], own(cols)) + tn(lbuf[left, TOK:], other(cols))

    def store(gi, h, role, xx, where, value):
        if RFIRST[gi][h] == "y":
            keep, index = role == 0, xx
        else:
            keep, index = x == xx, role

        def save_full():
            full[(h, index) + where] = value

        def save_low():
            low[(h, index) + where] = value.astype(BF)

        if isinstance(keep, bool):
            (save_full if keep else save_low)()
        else:
            pl.when(keep)(save_full)
            pl.when(jnp.logical_not(keep))(save_low)

    def compute(gi):
        kind, l = RGROUPS[gi]
        if kind == "d":

            def one(z, carry):
                prod = product(
                    z, lambda _: ba[8, :, half_cols(c)], lambda _: rd[l], None
                ).reshape(2, 2, 2, 96, 384)
                for xx in range(2):
                    for yy in range(2):
                        for h in range(2):
                            store(gi, h, (yy + y) % 2, xx, (z,), prod[xx, yy, h])
                return carry

            lax.fori_loop(0, count, one, 0)
            return
        recv = ru if kind == "u" else rq
        base = 4 if kind == "u" else 0
        for role in range(2):
            yy = y if role == 0 else 1 - y
            left = 0 if kind == "u" else yy
            for h in range(2):
                cols = slice(h * 384, (h + 1) * 384)
                prod = product(
                    left, lambda cols: ba[base + 2 * yy + c, :, cols], lambda cols: recv[l, yy, :, cols], cols
                ).reshape(count, 2, 96, 384)
                for xx in range(2):
                    store(gi, h, role, xx, (), prod[:, xx])

    def step1(gi, h):
        return remote(
            low.at[h], recv1.at[gi % SLOTS_R, h], s1.at[gi, h], r1.at[gi, h],
            over_y if RFIRST[gi][h] == "y" else over_x,
        )

    def step2(gi, h):
        return remote(
            mid_low.at[h], recv2.at[gi % SLOTS_R, h], s2.at[gi, h], r2.at[gi, h],
            over_x if RFIRST[gi][h] == "y" else over_y,
        )

    def along(gi, dz):
        return remote(
            zlow.at[(g + dz) % count], zrecv.at[gi % SLOTS_R, dz - 1], zs.at[gi, dz - 1], zr.at[gi, dz - 1],
            (f, ((g + dz) % count) * 2 + x),
        )

    def result(gi, yy):
        kind, l = RGROUPS[gi]
        if kind == "d":
            return gdown.at[l, yy, :, half_cols(c)]
        return gcol.at[2 * l + (1 if kind == "u" else 0), yy, c]

    def spread_y(gi):
        block = result(gi, y)
        return remote(block, block, fs.at[gi], fr.at[gi], over_y)

    def spread_c(gi):
        block = result(gi, slice(None))
        return remote(block, block, ks.at[gi], kr.at[gi], over_c)

    def advance(gi, stage):
        slot = gi % SLOTS_R
        if stage == 1:
            for h in range(2):
                step1(gi, h).wait_recv()
                step1(gi, h).wait_send()
                keep, send = (x, 1 - x) if RFIRST[gi][h] == "y" else (0, 1)
                mid_low[h] = (full[h, send] + recv1[slot, h, send].astype(F32)).astype(BF)
                step2(gi, h).start()
                mid_own[h] = full[h, keep] + recv1[slot, h, keep].astype(F32)
        elif stage == 2:
            for h in range(2):
                step2(gi, h).wait_recv()
                step2(gi, h).wait_send()
                summed = mid_own[h] + recv2[slot, h].astype(F32)
                zlow[:, h] = summed.astype(BF)
                mid_own[h] = summed
            if gi >= SLOTS_R:
                for dz in range(1, count):
                    pl.semaphore_wait(credit.at[1 + dz], 1)
            for dz in range(1, count):
                along(gi, dz).start()
            for h in range(2):
                zown[h] = mid_own[h, g]
            if gi + SLOTS_R < total:
                pl.semaphore_signal(credit.at[0], inc=1, device_id=over_x, device_id_type=MESH)
                pl.semaphore_signal(credit.at[1], inc=1, device_id=over_y, device_id_type=MESH)
        elif stage == 3:
            for dz in range(1, count):
                along(gi, dz).wait_recv()
                along(gi, dz).wait_send()
            for h in range(2):
                value = zown[h]
                for dz in range(1, count):
                    value = value + zrecv[slot, dz - 1, h].astype(F32)
                sq[...] += jnp.sum((value * value).reshape(12, 8, 3, 128), (0, 2))
                kind, l = RGROUPS[gi]
                if kind == "d":
                    gdown[l, y, h * 96 : (h + 1) * 96, half_cols(c)] = value.astype(BF)
                else:
                    idx = 2 * l + (1 if kind == "u" else 0)
                    gcol[idx, y, c, :, h * 384 : (h + 1) * 384] = value.astype(BF)
            if gi + SLOTS_R < total:
                for dz in range(1, count):
                    pl.semaphore_signal(
                        credit.at[1 + dz], inc=1, device_id=(f, ((g + count - dz) % count) * 2 + x), device_id_type=MESH
                    )
            spread_y(gi).start()
        elif stage == 4:
            spread_y(gi).wait_recv()
            spread_c(gi).start()
        else:
            spread_c(gi).wait_recv()

    psends, powns, pxrs, pzss, pzrs = (psend0, psend1), (pown0, pown1), (pxr0, pxr1), (pzs0, pzs1), (pzr0, pzr1)
    pspans = (slice(0, CMAIN), slice(CMAIN, CMAIN + PWIDE[1]))

    def part_over(n):
        return remote(psends[n], pxrs[n], p1.at[n], p1r.at[n], over_x)

    def part_along(n, dz):
        return remote(
            pzss[n].at[(g + dz) % count], pzrs[n].at[dz - 1], p2.at[n, dz - 1], p2r.at[n, dz - 1],
            (f, ((g + dz) % count) * 2 + x),
        )

    def part_y(n):
        block = gpart.at[n, y, c]
        return remote(block, block, p3.at[n], p3r.at[n], over_y)

    def part_c(n):
        block = gpart.at[n, :, c]
        return remote(block, block, p4.at[n], p4r.at[n], over_c)

    def part_compute(n):
        pieces = []
        if n == 0:
            pieces.append((0, tn(head_ref[0], head_ref[1, :, :CMAIN])))
        else:
            pieces.append((0, er[...].T))
            pieces.append((EWIDE, tn(dcur[...].astype(BF), pn_ref[...])))
        for lo, piece in pieces:
            piece = piece.reshape(count, 2, 96, -1)
            span = slice(lo, lo + piece.shape[-1])
            for xx in range(2):

                @pl.when(x == xx)
                def _():
                    powns[n][:, :, span] = piece[:, xx]
                    psends[n][:, :, span] = piece[:, 1 - xx].astype(BF)

        part_over(n).start()

    def part_advance(n, stage):
        if stage == 1:
            part_over(n).wait_recv()
            summed = powns[n][...] + pxrs[n][...].astype(F32)
            powns[n][...] = summed
            pzss[n][...] = summed.astype(BF)
            for dz in range(1, count):
                part_along(n, dz).start()
        elif stage == 2:
            value = powns[n][g]
            for dz in range(1, count):
                part_along(n, dz).wait_recv()
                value = value + pzrs[n][dz - 1].astype(F32)
            gpart[n, y, c, :, : PWIDE[n]] = value.astype(BF)
            part_y(n).start()
            if n == 1:
                lane = lax.broadcasted_iota(jnp.int32, (96, EWIDE), 1)
                inside = jnp.logical_and(lane % SLOTS < GRID, lane < TOK)
                own = jnp.where(inside, value[:, :EWIDE], 0.0)
                sq[...] += jnp.sum((own * own).reshape(12, 8, 3, 128), (0, 2))
        elif stage == 3:
            part_y(n).wait_recv()
            part_c(n).start()
        else:
            part_c(n).wait_recv()
            value = gpart[n, 0, 0].astype(F32) + gpart[n, 0, 1].astype(F32)
            value = value + gpart[n, 1, 0].astype(F32) + gpart[n, 1, 1].astype(F32)
            value = value[:, : PWIDE[n]]
            if n == 1:
                lane = lax.broadcasted_iota(jnp.int32, value.shape, 1)
                value = jnp.where(lane >= EVEC, value, 0.0)
            value = jnp.where(f == 0, value * value, 0.0)
            sq[...] += jnp.sum(value.reshape(12, 8, PWIDE[n] // 128, 128), (0, 2))

    under_way = []

    def tick():
        for entry in list(under_way):
            entry[2] += 1
            (advance if entry[0] == "group" else part_advance)(entry[1], entry[2])
            if entry[2] == (STAGES if entry[0] == "group" else STAGES - 1):
                under_way.remove(entry)

    def stage_of(kind, n):
        for entry in under_way:
            if entry[0] == kind and entry[1] == n:
                return entry[2]
        return STAGES

    def launch(gi):
        while gi > 0 and stage_of("group", gi - 1) < 1:
            tick()
        l = RGROUPS[gi][1]
        for n in swaps(gi):
            swap(gi, n).wait_recv()
        for copy in left_loads(gi):
            copy.wait()
        if gi >= SLOTS_R:
            while stage_of("group", gi - SLOTS_R) < 2:
                tick()
        compute(gi)
        for n in swaps(gi):
            swap(gi, n).wait_send()
        if gi >= SLOTS_R:
            pl.semaphore_wait(credit.at[0], 1)
            pl.semaphore_wait(credit.at[1], 1)
        for h in range(2):
            step1(gi, h).start()
        under_way.append(["group", gi, 0])
        if gi + 1 < total:
            prepare(gi + 1)

    waited = set()

    def prepare(gi):
        kind, l = RGROUPS[gi]
        for n in ((0,) if kind == "d" else (1,)):
            if (l, n) not in waited:
                waited.add((l, n))
                forward_swap(l, n).wait_recv()
        for copy in left_loads(gi):
            copy.start()

    def launch_part(n):
        part_compute(n)
        under_way.append(["part", n, 0])

    sq[...] = jnp.zeros_like(sq)
    er[...] = jnp.zeros_like(er)
    er[EVEC + GLOB + 3 : EVEC + GLOB + 5, :] = end_ref[...]
    er[ECLS:, :] = tn(head_ref[1, :, CMAIN : CMAIN + EWIDE - ECLS], head_ref[0])
    launch_part(0)
    prepare(0)
    first_load.wait()
    loaded = set()

    for layer in reversed(range(L)):
        base = 3 * (L - 1 - layer)

        def mat(which):
            def read(k):
                if (layer, which) not in loaded:
                    loaded.add((layer, which))
                    weight(layer, which).wait()
                return wbuf[weight_slot(layer, which), k]

            return read

        def slope(k):
            slope_load(layer, k).wait()
            return gp[k % 2]

        def kept(i):
            kept_load(layer, i).wait()
            return xb[...]

        def at(point):
            if point.startswith("mlp"):
                k = int(point[3:])
                if k + 2 < FF // D:
                    slope_load(layer, k + 2).start()
                elif layer > 0:
                    slope_load(layer - 1, k - 2).start()
                if k == 0:
                    swap(base, 0).start()
                if k == 3:
                    for n in swaps(base + 1):
                        swap(base + 1, n).start()
                    weight(layer, 2).start()
                    if layer > 0:
                        weight(layer - 1, 0).start()
                if k % 2:
                    tick()
            elif point == "resid":
                kept_load(layer, 0).start()
                if layer == L - 1:
                    heads_load(layer).wait()
            elif point == "sent":
                if layer < L - 1:
                    heads_load(layer).wait()
                launch(base)
            elif point == "head0":
                tick()
            elif point == "head1":
                launch(base + 1)
            elif point == "head2":
                tick()
                if layer > 0:
                    heads_load(layer - 1).start()
            elif point == "heads":
                for n in swaps(base + 2):
                    swap(base + 2, n).start()
                tick()
            elif point == "done":
                if layer > 0:
                    weight(layer - 1, 1).start()
                    kept_load(layer - 1, 1).start()
                    launch(base + 2)

        backward_body(
            layer, dcur, er, ba, vec_ref, mask_ref, qk, (mat(0), mat(1), mat(2)), slope, kept, scratch,
            (ds_.at[layer], dr_.at[layer], gs_.at[layer], gr_.at[layer]), at,
        )
    dgrid = dcur[...]
    spot = lax.broadcasted_iota(jnp.int32, (TOK, D), 0)
    er[:TOK, :] = dgrid
    inside = jnp.where(spot % SLOTS < GRID, dgrid, 0.0)
    er[EVEC + GLOB : EVEC + GLOB + 1, :] = jnp.sum(inside, 0, keepdims=True)
    er[EVEC + GLOB + 1 : EVEC + GLOB + 3, :] = dgrid[GRID : GRID + 2, :]
    launch_part(1)
    launch(total - 1)
    shared = False
    while under_way:
        tick()
        if not shared and stage_of("group", total - 1) >= 3 and stage_of("part", 1) >= STAGES - 1:
            shared = True
            n = NF * times
            me = f * times + t

            def send(i, carry):
                other = (me + i) % n
                remote(sq, square_all.at[me], qs, qr, (other // times, other % times)).start()
                return carry

            lax.fori_loop(1, n, send, 0)
            square_all[me] = sq[...]
    for layer in range(L):
        for n in range(2):
            forward_swap(layer, n).wait_send()
    for gi in range(total):
        spread_y(gi).wait_send()
        spread_c(gi).wait_send()
    for n in range(2):
        part_over(n).wait_send()
        for dz in range(1, count):
            part_along(n, dz).wait_send()
        part_y(n).wait_send()
        part_c(n).wait_send()
    wait_small(times, small_all, ss, sr)
    wait_small(times, square_all, qs, qr)


def backward_all(times, dout, xs, gp, qk, fa, vec, mask, pnorm, head, end_rows, small, wcol, wdown):
    count = times // 2
    n = NF * times
    total = len(RGROUPS)
    dma = pltpu.SemaphoreType.DMA
    most = max(PWIDE)
    return pl.pallas_call(
        functools.partial(backward_all_kernel, times),
        out_shape=(
            jax.ShapeDtypeStruct((2 * L, 2, 2, 96, D), BF),
            jax.ShapeDtypeStruct((L, 2, 192, D), BF),
            jax.ShapeDtypeStruct((2, 2, 2, 96, most), BF),
            jax.ShapeDtypeStruct((n, 8, 128), F32),
            jax.ShapeDtypeStruct((n, 8, 128), F32),
            jax.ShapeDtypeStruct(fa.shape, BF),
        ),
        in_specs=[aspec()] * 5 + [vspec()] * 6 + [aspec()] * 2,
        out_specs=(vspec(),) * 5 + (aspec(),),
        scratch_shapes=[
            VM((2, 4, D, D), BF),
            VM((2, TOK, D), F32),
            VM((TOK, D), F32),
            VM((TOK, D), F32),
            VM((EWIDE, D), F32),
            VM((PER, NF, QROWS, 128), BF),
            VM((9, TOK, D), BF),
            VM((4, 2 * TOK, D), BF),
            VM((L, TOK, 384), BF),
            VM((L, 2, TOK, D), BF),
            VM((L, 2, TOK, D), BF),
            VM((2, 2, count, 96, 384), F32),
            VM((2, 2, count, 96, 384), BF),
            VM((SLOTS_R, 2, 2, count, 96, 384), BF),
            VM((2, count, 96, 384), F32),
            VM((2, count, 96, 384), BF),
            VM((SLOTS_R, 2, count, 96, 384), BF),
            VM((count, 2, 96, 384), BF),
            VM((2, 96, 384), F32),
            VM((SLOTS_R, count - 1, 2, 96, 384), BF),
            *[VM((count, 96, w), BF) for w in PWIDE],
            *[VM((count, 96, w), F32) for w in PWIDE],
            *[VM((count, 96, w), BF) for w in PWIDE],
            *[VM((count, 96, w), BF) for w in PWIDE],
            *[VM((count - 1, 96, w), BF) for w in PWIDE],
            VM((8, 128), F32),
            dma((L, 3)), dma((L, 4)), dma((L, 2)), dma((L + 1,)), dma((4, 2)),
            dma((L, 2)), dma((L, 2)), dma((total, 2)), dma((total, 2)),
            dma((total, 2)), dma((total, 2)), dma((total, 2)), dma((total, 2)),
            dma((total, count - 1)), dma((total, count - 1)),
            dma((total,)), dma((total,)), dma((total,)), dma((total,)),
            dma, dma, dma, dma,
            dma((2,)), dma((2,)), dma((2, count - 1)), dma((2, count - 1)), dma((2,)), dma((2,)), dma((2,)), dma((2,)),
            pltpu.SemaphoreType.REGULAR((count + 1,)),
            *[dma((L, PER, NF - 1))] * 4,
        ]
        + BACKWARD_SCRATCH,
        compiler_params=pltpu.CompilerParams(
            collective_id=2 + 2 * L, has_side_effects=True, vmem_limit_bytes=63 * 1024 * 1024
        ),
        name="backward_all",
    )(dout, xs, gp, qk, fa, vec, mask, pnorm, head, end_rows, small, wcol, wdown)[:5]


def adam(weight, first, second, grad):
    first = DECAY_FIRST * first + (1.0 - DECAY_FIRST) * grad
    second = DECAY_SECOND * second + (1.0 - DECAY_SECOND) * grad * grad
    fix_one = 1.0 - DECAY_FIRST**STEP
    fix_two = 1.0 - DECAY_SECOND**STEP
    weight = weight - LEARN_RATE * (
        first / fix_one / (jnp.sqrt(second / fix_two) + EPSILON) + WEIGHT_DECAY * weight
    )
    return (weight, first, second)


def pad_to(v, axis, size):
    pads = [(0, 0)] * v.ndim
    pads[axis] = (0, size - v.shape[axis])
    return jnp.pad(v, pads)


def embed_units(embedding, classifier, vectors, f):
    width = embedding.shape[1]
    blocks = embedding[:NGRID].reshape(NF, FROWS // NF, 2, HALF, width)
    block = lax.dynamic_index_in_dim(blocks, f, 0, keepdims=False).transpose(1, 0, 2, 3)
    block = block.reshape(2, GRID, width)
    tokens = jnp.where(f == 0, vectors[GLOB + 1 : GLOB + 3], 0.0)
    tokens = jnp.stack([tokens, jnp.zeros_like(tokens)])
    block = jnp.concatenate([block, tokens, jnp.zeros((2, SLOTS - GRID - 2, width), F32)], 1)
    rest = classifier[:, CMAIN:].T
    unit = jnp.concatenate(
        [
            block.reshape(TOK, width), vectors, jnp.zeros((ECLS - EVEC - VROWS, width), F32),
            pad_to(rest, 0, EWIDE - ECLS),
        ],
        0,
    )
    return unit.T.astype(BF), embedding[NGRID:].T.astype(BF), classifier[:, :CMAIN].astype(BF)


def local(
    patches, column_mask, labels, clip_weights, wide_weights, down_weights, embedding, classifier,
    vectors, class_bias, wide_first, down_first, embedding_first, classifier_first, vectors_first,
    bias_first, wide_second, down_second, embedding_second, classifier_second, vectors_second,
    bias_second,
):
    times = lax.axis_size("tm")
    f, t = lax.axis_index("freq"), lax.axis_index("tm")
    half = t % 2
    pair = t // 2
    rows_dev = FROWS // NF
    kernels = D // times == 96
    shard = D // times
    columns = column_mask.reshape(times, CPD, HALF) > 0
    mine_columns = lax.dynamic_index_in_dim(columns, t, 0, keepdims=False)
    raw = patches.reshape(rows_dev, CPD, HALF, PATCH)

    pixels = raw.astype(F32)
    live = mine_columns.astype(F32)[None, :, :, None]
    sums = jnp.stack(
        [
            jnp.sum(pixels * live),
            jnp.sum(pixels * pixels * live),
            jnp.sum(live) * (rows_dev * PATCH),
        ]
    )
    keep_block, give_block = (
        pad_to(lax.dynamic_index_in_dim(raw, i, 1, keepdims=False).reshape(GRID, PATCH), 0, SLOTS)
        for i in (half, 1 - half)
    )

    wide_low = wide_weights.astype(BF)
    down_low = down_weights.astype(BF)
    unit_embed, unit_patch, unit_class = embed_units(embedding, classifier, vectors, f)

    clip_columns = lax.dynamic_slice(columns, (pair * 2, half, 0), (2, 1, HALF)).reshape(2, HALF)
    slots = jnp.concatenate(
        [
            jnp.broadcast_to(jnp.tile(clip_columns, (1, rows_dev)), (NF, 2, GRID)),
            jnp.broadcast_to(
                ((jnp.arange(NF)[:, None] == 0) & (jnp.arange(2)[None, :] == 0))[:, :, None], (NF, 2, 2)
            ),
            jnp.zeros((NF, 2, SLOTS - GRID - 2), bool),
        ],
        2,
    ).reshape(NF * TOK)
    mask = jnp.where(slots, 0.0, -1e30).astype(F32)

    if kernels:
        units = wide_low.reshape(L, shard, 2, 4, D).transpose(0, 2, 3, 1, 4)
        wcol, wdown, class_main, vec, xs, fa, gp, qk, pnorm = forward_all(
            times, units.reshape(2 * L, 2, 2, shard, D), down_low.reshape(L, 2, 192, D), unit_embed, unit_patch, unit_class,
            jnp.broadcast_to(pad_to(sums, 0, 128), (8, 128)), keep_block, give_block, mask.reshape(1, -1),
        )
        class_main = class_main.reshape(D, CMAIN)
    else:
        wide_all = lax.all_gather(wide_low, "tm", axis=1, tiled=True)
        wcol = wide_all.reshape(L, D, 2, 4, D).transpose(0, 2, 3, 1, 4)
        wcol = wcol.reshape(2 * L, 2, 2, 4, 2, 96, D)
        wdown = lax.all_gather(down_low, "tm", axis=1, tiled=True).reshape(L, 4, 2, 2, 192, D)
        vec = lax.all_gather(unit_embed, "tm", axis=0, tiled=True).T.astype(F32)
        patch = lax.all_gather(unit_patch, "tm", axis=0, tiled=True)
        class_main = lax.all_gather(unit_class, "tm", axis=0, tiled=True)
        sums = lax.psum(sums, ("freq", "tm"))
        take_block = lax.ppermute(
            give_block, "tm", [(i, i + 1 - 2 * (i % 2)) for i in range(times)]
        )
        pixels = jnp.concatenate(
            [jnp.where(half == 0, keep_block, take_block), jnp.where(half == 0, take_block, keep_block)], 0
        )
        center = sums[0] / sums[2]
        mel_scale = lax.rsqrt(sums[1] / sums[2] - center * center + 1e-05)
        inside = (jnp.arange(TOK) % SLOTS < GRID)[:, None]
        pnorm = jnp.where(inside, (pixels.astype(F32) - center) * mel_scale, 0.0).astype(BF)
        x = nt(pnorm, patch) + vec[:TOK] + jnp.where(inside, vec[EVEC + GLOB], 0.0)
        xs, fa, gp, qk = [x], [], [], []
        for layer in range(L):
            x, x1, acts, slopes, heads = forward_layer(layer, x, vec, mask.reshape(1, -1), wcol, wdown)
            xs += [x1, x]
            fa.append(acts)
            gp.append(slopes)
            qk.append(heads)
    wcol = wcol.reshape(2 * L, 4, D, D)
    wdown = wdown.reshape(L, 4, D, D)
    vec_all = vec[EVEC : EVEC + VROWS]
    class_all = jnp.concatenate([class_main, vec[ECLS : ECLS + CLASSES - CMAIN].T.astype(BF)], 1)

    owner = (f == 0).astype(F32)
    special = xs[2 * L][GRID : GRID + 2]
    normed_end, scale_end = norm_rows(special)
    feature = jnp.mean(normed_end * vec_all[GLOB + 3] + vec_all[GLOB + 4], 0, keepdims=True).astype(BF)
    logits = nn(feature, class_all) + class_bias
    clip = pair * CPD + half
    flags = lax.dynamic_slice_in_dim(labels, clip, 1, 0).astype(F32)
    weight = lax.dynamic_slice_in_dim(clip_weights, clip, 1, 0).astype(F32)[:, None]
    weight_total = jnp.sum(clip_weights).astype(F32)
    loss_part = owner * jnp.sum(weight * (jax.nn.softplus(logits) - flags * logits))
    dlogits = owner * weight * (jax.nn.sigmoid(logits) - flags) / weight_total
    dlogits_low = dlogits.astype(BF)
    dfinal = jnp.broadcast_to(0.5 * nt(dlogits_low, class_all), (2, D))
    dspecial = norm_back(dfinal * vec_all[GLOB + 3], normed_end, scale_end)
    end_rows = jnp.stack([jnp.sum(dfinal * normed_end, 0), jnp.sum(dfinal, 0)])
    dx = jnp.concatenate(
        [jnp.zeros((GRID, D), F32), dspecial, jnp.zeros((TOK - GRID - 2, D), F32)], 0
    )
    small = jnp.concatenate([dlogits.reshape(-1), loss_part.reshape(1)])
    small = pad_to(small, 0, 1024).reshape(8, 128)
    if kernels:
        head = jnp.stack([pad_to(feature, 0, 16), pad_to(pad_to(dlogits_low, 1, D), 0, 16)])
        gcol, gdown, gpart, small_all, square_all = backward_all(
            times, dx, xs, gp, qk, fa, vec, mask.reshape(-1, 1), pnorm, head, end_rows, small, wcol, wdown
        )
        small = jnp.sum(small_all, 0).reshape(-1)
        square_total = jnp.sum(square_all)
        gcol = gcol.astype(F32)
        grad_wide = gcol.reshape(L, 2, 4, shard, D).transpose(0, 3, 1, 2, 4).reshape(L, shard, 8 * D)
        grad_down = gdown.reshape(L, FF // times, D).astype(F32)
        gpart = gpart.astype(F32).reshape(2, NF, shard, -1)
        grad_pos = gpart[1, :, :, :TOK].reshape(NF, shard, 2, SLOTS)[:, :, :, :GRID]
        grad_pos = grad_pos.reshape(NF, shard, 2, rows_dev, HALF).transpose(0, 3, 2, 4, 1).reshape(NGRID, shard)
        summed = jnp.sum(gpart, 1)
        grad_embed = jnp.concatenate([grad_pos, summed[1, :, EWIDE : EWIDE + PATCH].T], 0)
        grad_class = jnp.concatenate(
            [summed[0, :, :CMAIN], summed[1, :, ECLS : ECLS + CLASSES - CMAIN]], 1
        )
        grad_vectors = summed[1, :, EVEC : EVEC + VROWS].T
    else:
        ba = [None] * L
        er = jnp.zeros((EWIDE, D), F32)
        for layer in reversed(range(L)):
            dx, ba[layer], rows = backward_layer(
                layer, dx, xs[2 * layer], xs[2 * layer + 1], gp[layer], qk[layer], vec, mask.reshape(-1, 1), wcol, wdown
            )
            er = er + rows
        dgrid = jnp.where(inside, dx, 0.0)
        grad_vectors = er[EVEC : EVEC + GLOB]
        grad_vectors = jnp.concatenate(
            [grad_vectors, jnp.sum(dgrid, 0, keepdims=True), dx[GRID : GRID + 2], end_rows], 0
        )
        wides, downs = [], []
        for l in range(L):
            cols = [tn(fa[l][0], ba[l][i]) for i in range(3)]
            cols += [tn(fa[l][1], ba[l][3])]
            cols += [tn(fa[l][2], ba[l][4 + i]) for i in range(4)]
            wides.append(jnp.concatenate(cols, 1))
            downs.append(jnp.concatenate([tn(fa[l][3 + i], ba[l][8]) for i in range(4)], 0))
        dpos = dgrid.reshape(2, SLOTS, D)[:, :GRID].reshape(2, rows_dev, HALF, D)
        dpos = dpos.transpose(1, 0, 2, 3).reshape(rows_dev * 2 * HALF, D)
        dpos = lax.dynamic_update_slice(jnp.zeros((NGRID, D), F32), dpos, (f * rows_dev * 2 * HALF, 0))
        dembed = jnp.concatenate([dpos, tn(pnorm, dgrid.astype(BF))], 0)
        grads = (
            lax.psum_scatter(jnp.stack(wides), "tm", scatter_dimension=1, tiled=True),
            lax.psum_scatter(jnp.stack(downs), "tm", scatter_dimension=1, tiled=True),
            lax.psum_scatter(dembed, "tm", scatter_dimension=1, tiled=True),
            lax.psum_scatter(tn(feature, dlogits_low), "tm", scatter_dimension=0, tiled=True),
            lax.psum_scatter(grad_vectors, "tm", scatter_dimension=1, tiled=True),
        )
        grads = lax.psum(grads, "freq")
        grad_wide, grad_down, grad_embed, grad_class, grad_vectors = grads
        squares = sum(jnp.sum(v * v) for v in grads)
        square_total, small = lax.psum(
            (jnp.where(f == 0, squares, 0.0), small.reshape(-1)), ("freq", "tm")
        )
    grad_bias = small[:CLASSES]
    loss_sum = small[CLASSES]
    grad_norm = jnp.sqrt(square_total + jnp.sum(grad_bias * grad_bias))
    coef = jnp.minimum(1.0, 1.0 / (grad_norm + 1e-06))

    params = (wide_weights, down_weights, embedding, classifier, vectors, class_bias)
    firsts = (wide_first, down_first, embedding_first, classifier_first, vectors_first, bias_first)
    seconds = (wide_second, down_second, embedding_second, classifier_second, vectors_second, bias_second)
    grads = (grad_wide, grad_down, grad_embed, grad_class, grad_vectors, grad_bias)
    news = [adam(w, m, v, g * coef) for w, m, v, g in zip(params, firsts, seconds, grads)]
    masters = [n[0] for n in news]
    return (
        *masters,
        *[n[1] for n in news],
        *[n[2] for n in news],
        *[m.astype(BF) for m in masters[:4]],
        grad_norm,
        loss_sum,
        weight_total,
    )


def solution(mesh):
    split = (
        P(None, "tm", None), P(None, "tm", None), P(None, "tm"), P("tm", None), P(None, "tm"), P(),
    )
    return jax.shard_map(
        local,
        mesh=mesh,
        in_specs=(P("freq", "tm", None), P(), P(), P()) + split * 3,
        out_specs=split * 3 + split[:4] + (P(), P(), P()),
        check_vma=False,
    )
```

time: 680 us -> 604 us (0.89)
  Pallas kernels: 559 us -> 501 us
  local copies, waits for them, and re-layouts: 48.5 us -> 38 us
    pallas_call x6 -> x2, Pallas kernels: 559 us -> 501 us  [the longest x1 288 us: backward_all(): pl.pallas_call(functools.partial(backward_all_kernel, times), out_shape=(...]
    unnamed x62 -> x41, local copies, waits for them, and re-layouts: 14.6 us -> 1.18 us
where the time goes in v2:
time: 604 us; the launch traced here: 600 us
  Pallas kernels  501 us (83%)
  other arithmetic  49.9 us (8%)
  local copies, waits for them, and re-layouts  38 us (6%)
  between operations  8.24 us (1%)
    pallas_call x1, Pallas kernels, backward_all(): pl.pallas_call(functools.partial(backward_all_kernel, times), out_shape=(...  288 us
    pallas_call x1, Pallas kernels, forward_all(): pl.pallas_call(functools.partial(forward_all_kernel, times), out_shape=tu...  213 us
    convert_element_type x4, other arithmetic, local(): m.astype(BF)  21.2 us

profile of v2, /device:TPU:0, one launch (start us, length us, event | category | flops | bytes accessed | tf_op | source)
XLA Modules:
  0.0 600.3 jit_solution(11320892928150656274)
XLA Ops:
  0.7 1.3 reduce_sum.145
  2.7 1.2 dynamic_slice.29
  4.6 0.7 fusion.21
  5.7 0.7 broadcast_compare_fusion
  6.6 0.6 fusion.25
  8.1 1.7 fusion.4
  9.8 1.4 select_maximum_fusion.1
  11.2 0.6 broadcast_in_dim.57.stats
  11.8 0.7 select_n.83.mask_ref
  12.5 0.7 convert.39
  13.3 1.6 fusion.14.upatch
  15.0 1.0 convert.40
  15.9 0.6 slice.84.uclass
  16.6 1.1 reshape.274
  17.7 0.6 pad.36.psend
  18.4 0.6 pad.35.pkeep
  19.0 0.7 slice.64
  19.8 1.2 copy.151
  20.9 0.8 reshape.271
  21.8 0.9 fusion.9
  22.7 0.2 fusion.11
  23.1 0.7 fusion.13.uemb
  23.8 1.3 select_n.88.mask_ref
  25.1 1.1 convert_element_type.100
  26.3 2.6 convert_element_type.99
  28.9 3.2 reshape.268
  32.1 3.6 copy.150
  35.6 213.1 %forward_all.1 = (bf16[4,2,2,4,2,96,768]{6,5,4,3,2,1,0:T(8,128)(2,1)}, bf16[2,4,2,2,192,768]{5,4,3,2,1,0:T(8,128)(2,1)}, bf16[4,2,96,512]{3,2,1,0:T(8,128)(2,1)}...) custom-call(bf16[4,2,2,96,768]{4,3,2,1,0:T(8,128)(2,1)} %bitcast.91,, ...), custom_call_target="tpu_custom_call" | custom-call | tf_op jit(solution)/shard_map/forward_all/pallas_call | solution.py:582
  248.7 0.9 slice_reduce_fusion
  249.6 0.9 multiply_reduce_fusion.2
  250.5 0.8 slice_reduce_fusion.1
  251.4 0.8 add_reduce_fusion
  252.2 0.8 fusion.15
  253.1 0.2 copy.157
  253.2 1.4 convolution_reduce_fusion
  254.7 1.4 fusion.37
  256.7 1.5 fusion.41
  258.2 0.7 fusion.19.small
  258.9 0.6 fusion.38
  260.1 0.1 multiply_reduce_fusion
  260.3 0.6 pad_maximum_fusion.4.end_ref
  261.0 0.6 pad_maximum_fusion.3.head_ref
  261.6 1.1 maximum_maximum_fusion.dout_in
  262.7 288.2 %backward_all.1 = (bf16[4,2,2,96,768]{4,3,2,1,0:T(8,128)(2,1)}, bf16[2,2,192,768]{3,2,1,0:T(8,128)(2,1)}, bf16[2,2,2,96,640]{4,3,2,1,0:T(8,128)(2,1)}, f32[32,8,...) custom-call(f32[320,768]{1,0:T(8,128)} %maximum_maximum_fusion.dout_in, ...), custom_call_target="tpu_custom_call" | custom-call | tf_op jit(solution)/shard_map/backward_all/pallas_call | solution.py:1258
  550.9 1.6 reduce_sum.150
  552.6 0.9 reduce_sum.151
  553.5 0.6 slice.81
  554.1 0.6 multiply_reduce_fusion.3
  556.1 0.6 multiply_subtract_fusion.5
  556.7 1.4 convert_reduce_fusion
  558.3 0.6 multiply_subtract_fusion.4
  559.1 0.3 copy.168
  559.4 0.5 copy.161
  559.9 1.0 copy.165
  560.8 1.3 reshape.295
  562.2 2.1 fusion.27
  564.3 1.6 convert_multiply_fusion.1
  565.9 1.7 fusion.29
  567.6 0.7 copy-done.4
  568.4 0.5 convert_multiply_fusion
  568.9 5.2 copy.159
  574.1 6.3 %mul.361 = f32[2,96,6144]{2,1,0:T(8,128)} reshape(f32[2,96,2,4,768]{4,3,2,1,0:T(4,128)} %copy.159) | data formatting | bytes 9437184 | tf_op jit(solution)/shard_map/mul | solution.py:1523
  580.4 7.9 %fusion.31 = (bf16[2,384,768]{2,1,0:T(8,128)(2,1)}, f32[2,384,768]{2,1,0:T(8,128)}, f32[2,384,768]{2,1,0:T(8,128)}, f32[2,384,768]{2,1,0:T(8,128)}) fusion(f32[2,384,768]{2,1,0:T(8,128)S(1)} %copy-done.2, f32[2,2,192,768]{3,2,1,0:T(8,128)} %convert_multiply_fusion.1, f32[2,384,768]{2,1,0:T(8,128)} %param.33, f32[2,384,768]{2,1,0:T(8,128)} %param.39), kind=kLoop, calls=%fused_computation.107 | loop fusion | flops 8847360 | bytes 17694720 | tf_op jit(solution)/shard_map/convert_element_type | solution.py:1529
  588.3 9.5 %fusion.33 = (bf16[2,96,6144]{2,1,0:T(8,128)(2,1)}, f32[2,96,6144]{2,1,0:T(8,128)}, f32[2,96,6144]{2,1,0:T(8,128)}, f32[2,96,6144]{2,1,0:T(8,128)}) fusion(f32[2,96,6144]{2,1,0:T(8,128)S(1)} %bitcast.88, f32[2,96,6144]{2,1,0:T(8,128)S(1)} %copy-done, f32[2,96,6144]{2,1,0:T(8,128)} %param.32, f32[2,96,6144]{2,1,0:T(8,128)} %param.38), kind=kLoop, calls=%fused_computation.108 | loop fusion | flops 17694720 | bytes 35389440 | tf_op jit(solution)/shard_map/convert_element_type | solution.py:1529
  (88 shorter events, 1.8 us)
Async XLA Ops:
  0.7 18.4 %copy-start.5 = (f32[1504,96]{0,1:T(8,128)S(1)}, f32[1504,96]{0,1:T(8,128)}, u32[]{:S(2)}) copy-start(f32[1504,96]{0,1:T(8,128)} %param.28) | copy-start | bytes 1732612
  16.6 8.6 %copy-start.1 = (f32[2,384,768]{2,1,0:T(8,128)S(1)}, f32[2,384,768]{2,1,0:T(8,128)}, u32[]{:S(2)}) copy-start(f32[2,384,768]{2,1,0:T(8,128)} %param.27) | copy-start | bytes 7077892
  35.6 219.0 %copy-start.14 = (f32[527]{0:T(1024)S(1)}, f32[527]{0:T(1024)}, u32[]{:S(2)}) copy-start(f32[527]{0:T(1024)} %param.31) | copy-start | bytes 6328
  262.7 293.4 %copy-start.15 = (f32[527]{0:T(1024)S(1)}, f32[527]{0:T(1024)}, u32[]{:S(2)}) copy-start(f32[527]{0:T(1024)} %param.37) | copy-start | bytes 6328
  262.7 293.4 %copy-start.16 = (f32[527]{0:T(1024)S(1)}, f32[527]{0:T(1024)}, u32[]{:S(2)}) copy-start(f32[527]{0:T(1024)} %param.43) | copy-start | bytes 6328
  262.7 295.6 %copy-start.11 = (f32[29,96]{1,0:T(8,128)S(1)}, f32[29,96]{1,0:T(8,128)}, u32[]{:S(2)}) copy-start(f32[29,96]{1,0:T(8,128)} %param.30) | copy-start | bytes 33412
  262.7 295.6 %copy-start.12 = (f32[29,96]{1,0:T(8,128)S(1)}, f32[29,96]{1,0:T(8,128)}, u32[]{:S(2)}) copy-start(f32[29,96]{1,0:T(8,128)} %param.36) | copy-start | bytes 33412
  262.7 295.6 %copy-start.13 = (f32[29,96]{1,0:T(8,128)S(1)}, f32[29,96]{1,0:T(8,128)}, u32[]{:S(2)}) copy-start(f32[29,96]{1,0:T(8,128)} %param.42) | copy-start | bytes 33412
  550.9 8.1 %copy-start.3 = (bf16[2,2,2,96,640]{4,3,2,1,0:T(8,128)(2,1)S(1)}, bf16[2,2,2,96,640]{4,3,2,1,0:T(8,128)(2,1)}, u32[]{:S(2)}) copy-start(bf16[2,2,2,96,640]{4,3,2,1,0:T(8,128)(2,1)} %get-tuple-element.52) | copy-start | bytes 2949124
  559.3 2.8 copy-start.7
  559.4 2.8 copy-start.10
  562.2 2.2 copy-start.6
  562.2 3.8 copy-start.8
  562.2 3.7 copy-start.9
  565.9 2.4 copy-start.4
  574.1 6.4 %copy-start.2 = (f32[2,384,768]{2,1,0:T(8,128)S(1)}, f32[2,384,768]{2,1,0:T(8,128)}, u32[]{:S(2)}) copy-start(f32[2,384,768]{2,1,0:T(8,128)} %param.27) | copy-start | bytes 7077892
  574.1 14.2 %slice-start = ((s8[4718592]{0:T(1024)(128)(4,1)}), s8[524288]{0:T(1024)(128)(4,1)S(1)}, s32[]{:S(2)}) async-start(s8[4718592]{0:T(1024)(128)(4,1)} %bitcast.87), calls=%async_computation | async-start | bytes 1048576
  580.4 7.9 %slice-start.1 = ((s8[4718592]{0:T(1024)(128)(4,1)}), s8[4194304]{0:T(1024)(128)(4,1)S(1)}, s32[]{:S(2)}) async-start(s8[4718592]{0:T(1024)(128)(4,1)} %bitcast.87), calls=%async_computation.1 | async-start | bytes 8388608
  580.4 7.9 %copy-start = (f32[2,96,6144]{2,1,0:T(8,128)S(1)}, f32[2,96,6144]{2,1,0:T(8,128)}, u32[]{:S(2)}) copy-start(f32[2,96,6144]{2,1,0:T(8,128)} %mul.361) | copy-start | bytes 14155780

commit v3 on v2

--- a/solution.py
+++ b/solution.py
@@ -150,6 +150,12 @@
     return jnp.concatenate([v[:, :HDIM], v[:, HDIM:]], 0)
 
 
+def with_mask(block):
+    lane = lax.broadcasted_iota(jnp.int32, block.shape, 1)
+    query = jnp.where(lane < HDIM, block.astype(F32) * (HDIM ** (-0.5)), 0.0)
+    return jnp.where(lane == HDIM, 1.0, query).astype(BF)
+
+
 def exchange_sems():
     dma = pltpu.SemaphoreType.DMA
     return [dma((PER, NF - 1))] * 4
@@ -160,13 +166,13 @@
     VM((4, 2, 2, 192, D), BF),
     VM((PER, NF, QROWS, 128), BF),
     VM((PER, NF, TOK // 2, 128), BF),
-    VM((NF * TOK, HDIM), BF),
+    VM((NF * TOK, 128), BF),
     VM((NF * TOK, HDIM), BF),
     VM((TOK, D), F32),
 ]
 
 
-def layer_body(layer, x_ref, vec_ref, mask_ref, outs, scratch, orecv, sems, fetch, tick):
+def layer_body(layer, x_ref, vec_ref, outs, scratch, orecv, sems, fetch, tick):
     xo_ref, x1_ref, fa_ref, gp_ref, qk_ref = outs
     wbuf, dbuf, qsend, osend, kall, vall, acc = scratch
     qs, qr, os, orr = sems
@@ -208,12 +214,11 @@
             to_clip(j, i).start()
         qk_ref[j, f] = qsend[j, f]
     tick()
-    mask = mask_ref[...]
     for j in range(PER):
         for i in range(1, NF):
             to_clip(j, i).wait_recv()
         for s in range(NF):
-            kall[s * TOK : (s + 1) * TOK] = qk_ref[j, s, :TOK, HDIM:]
+            kall[s * TOK : (s + 1) * TOK, :HDIM] = qk_ref[j, s, :TOK, HDIM:]
             vall[s * TOK : (s + 1) * TOK] = open_half(qk_ref[j, s, TOK:])
 
         def attend(i, carry):
@@ -221,8 +226,7 @@
             halves = []
             for h in range(2):
                 lo = h * (TOK // 2)
-                q = qk_ref[j, s, lo : lo + TOK // 2, :HDIM]
-                scores = nt(q, kall[...]) * (HDIM ** (-0.5)) + mask
+                scores = nt(with_mask(qk_ref[j, s, lo : lo + TOK // 2]), kall[...])
                 top = jnp.max(scores, -1, keepdims=True)
                 expo = jnp.exp(scores - top)
                 total = jnp.sum(expo, -1, keepdims=True)
@@ -278,8 +282,17 @@
             back_clip(j, i).wait_send()
 
 
+def load_mask(mask, kall):
+    def body(sem):
+        copy = pltpu.make_async_copy(mask, kall, sem)
+        copy.start()
+        copy.wait()
+
+    pl.run_scoped(body, pltpu.SemaphoreType.DMA)
+
+
 def forward_kernel(
-    layer, x_ref, vec_ref, mask_ref, wcol, wdown,
+    layer, x_ref, vec_ref, mask, wcol, wdown,
     xo_ref, x1_ref, fa_ref, gp_ref, qk_ref,
     wbuf, dbuf, qsend, osend, kall, vall, acc, orecv, wsem, qs, qr, os, orr,
 ):
@@ -290,9 +303,10 @@
     ]
     for load in loads:
         load.start()
+    load_mask(mask, kall)
     greet_clip()
     layer_body(
-        layer, x_ref, vec_ref, mask_ref, (xo_ref, x1_ref, fa_ref, gp_ref, qk_ref),
+        layer, x_ref, vec_ref, (xo_ref, x1_ref, fa_ref, gp_ref, qk_ref),
         (wbuf, dbuf, qsend, osend, kall, vall, acc), orecv, (qs, qr, os, orr),
         lambda part: loads[part].wait(), lambda: None,
     )
@@ -308,7 +322,7 @@
             jax.ShapeDtypeStruct((FF // D, TOK, D), F32),
             jax.ShapeDtypeStruct((PER, NF, QROWS, 128), BF),
         ),
-        in_specs=[vspec()] * 3 + [aspec()] * 2,
+        in_specs=[vspec()] * 2 + [aspec()] * 3,
         out_specs=(vspec(),) * 5,
         scratch_shapes=FORWARD_SCRATCH
         + [VM((PER, NF, TOK // 2, 128), BF), pltpu.SemaphoreType.DMA((3,))]
@@ -343,7 +357,7 @@
     return plan, ready
 
 
-def gather_steps(count, ucol, udown, ocol, odown, sems):
+def gather_steps(count, ucol, udown, ocol, odown, sems, prepare):
     zs, zr, own, s1, r1, s2, r2, s3, r3 = sems
     f, t, y, c, g, x = place()
     every = slice(None)
@@ -388,6 +402,7 @@
 
     def act(s, action):
         if action == "along":
+            prepare(s // 2)
             keep(s).start()
             for dz in range(1, count):
                 along(s, dz).start()
@@ -419,20 +434,92 @@
     yield
 
 
+def loss_part(owner, clip, x_ref, vec, classes, labels, clip_weights, class_bias, dout, head, end_rows, small):
+    owner = jnp.where(owner, 1.0, 0.0)
+    normed, scale = norm_rows(x_ref[GRID : GRID + 2, :])
+    gain = vec[EVEC + GLOB + 3 : EVEC + GLOB + 4, :]
+    final = normed * gain + vec[EVEC + GLOB + 4 : EVEC + GLOB + 5, :]
+    feature = jnp.mean(final, 0, keepdims=True).astype(BF)
+    first_row = lax.broadcasted_iota(jnp.int32, (16, D), 0) == 0
+    feature = jnp.where(first_row, jnp.broadcast_to(feature.astype(F32), (16, D)), 0.0).astype(BF)
+    head[0] = feature
+    main = classes[...].reshape(D, CMAIN)
+    tail = vec[ECLS:EWIDE, :].astype(BF)
+    logits = jnp.concatenate([nn(feature, main), nt(feature, tail), jnp.zeros((16, 224), F32)], 1)[0:1]
+    logits = logits + class_bias[...]
+    flags = labels[pl.ds(clip, 1), :].astype(F32)
+    weights = clip_weights[...].astype(F32)
+    weight = jnp.sum(
+        jnp.where(lax.broadcasted_iota(jnp.int32, weights.shape, 1) == clip, weights, 0.0), keepdims=True
+    )
+    total = jnp.sum(weights, keepdims=True)
+    lane = lax.broadcasted_iota(jnp.int32, (1, D), 1)
+    inside = lane < CLASSES
+    soft = jnp.maximum(logits, 0.0) + jnp.log1p(jnp.exp(-jnp.abs(logits)))
+    loss = jnp.sum(jnp.where(inside, soft - flags * logits, 0.0), keepdims=True) * weight * owner
+    slope = 1.0 / (1.0 + jnp.exp(-logits))
+    grads = jnp.where(inside, owner * weight * (slope - flags) / total, 0.0)
+    for i in range(8):
+        small[i : i + 1, :] = jnp.zeros((1, 128), F32) if i > 5 else (
+            grads[:, 128 * i : 128 * (i + 1)]
+            + (jnp.where(lane[:, 128 * i : 128 * (i + 1)] == CLASSES, loss, 0.0))
+        )
+    grads = jnp.where(first_row, jnp.broadcast_to(grads, (16, D)), 0.0).astype(BF)
+    head[1] = grads
+    dfinal = 0.5 * (nt(grads[:, :CMAIN], main) + nn(grads[:, CMAIN : CMAIN + EWIDE - ECLS], tail))[0:1]
+    end_rows[0:1, :] = jnp.sum(dfinal * normed, 0, keepdims=True)
+    end_rows[1:2, :] = 2.0 * dfinal
+    special = norm_back(jnp.broadcast_to(dfinal * gain, normed.shape), normed, scale)
+    dout[...] = jnp.zeros_like(dout)
+    dout[GRID : GRID + 2, :] = special
+
+
 def forward_all_kernel(
-    times, ucol, udown, uemb, upatch, uclass, stats, pkeep, psend, mask_ref,
-    ocol, odown, oclass, vec_out, xs_out, fa_out, gp_out, qk_out, pn_out,
+    times, wide, down, uemb, upatch, uclass, live, pkeep, psend, labels, clip_weights, class_bias, mask,
+    ocol, odown, vec_out, xs_out, fa_out, gp_out, qk_out, pn_out, dout_out, head, end_rows, small,
     wbuf, dbuf, qsend, osend, kall, vall, acc, orecv, sall, precv, emb, patches, classes, vec, xs, fa, gp, qk, pn,
     zs, zr, own, s1, r1, s2, r2, s3, r3, es, er, exs, exr, ss, sr, ps, pr, wsem, osem,
-    qs0, qr0, os0, or0, qs1, qr1, os1, or1,
+    qs0, qr0, os0, or0, qs1, qr1, os1, or1, ucol, udown, cols_wide, cols_down, stats, dout, psem,
 ):
     f, t, y, c, g, x = place()
     count = times // 2
     over_x = (f, g * 2 + 1 - x)
+
+    def fetch_master(group):
+        kind, idx = GROUPS[group]
+        if kind == "c":
+            src = wide.at[idx // 2, :, pl.ds(idx % 2 * 4 * D, 4 * D)]
+            return pltpu.make_async_copy(src, cols_wide.at[idx], psem.at[group])
+        return pltpu.make_async_copy(down.at[idx], cols_down.at[idx], psem.at[group])
+
+    prepared = set()
+
+    def prepare(group):
+        if group in prepared:
+            return
+        prepared.add(group)
+        fetch_master(group).wait()
+        kind, idx = GROUPS[group]
+        for q in range(4):
+            if kind == "c":
+                ucol[idx, q // 2, q % 2] = cols_wide[idx, :, q * D : (q + 1) * D].astype(BF)
+            else:
+                udown[idx, q // 2, q % 2 * 96 : q % 2 * 96 + 96] = cols_down[idx, q * 96 : (q + 1) * 96].astype(BF)
+
+    for group in range(len(GROUPS)):
+        fetch_master(group).start()
+    row = lax.broadcasted_iota(jnp.int32, (8, 128), 1)
+    stats[...] = jnp.zeros_like(stats)
+    for n, block in enumerate((pkeep, psend)):
+        pixel, alive = block[...].astype(F32), live[n]
+        masked = pixel * alive
+        for lane, value in enumerate((masked, masked * pixel, alive * float(PATCH))):
+            stats[...] += jnp.where(row == lane, jnp.sum(value, keepdims=True), 0.0)
     greet_all(times)
     spread_small(times, stats, sall, ss, sr)
     swap = remote(psend, precv, ps, pr, over_x)
     swap.start()
+    load_mask(mask, kall)
     units = ((uemb, emb), (upatch, patches), (uclass, classes))
 
     def unit_along(n, dz):
@@ -455,7 +542,7 @@
     for n in range(2):
         for dz in range(1, count):
             unit_along(n, dz).start()
-    steps = gather_steps(count, ucol, udown, ocol, odown, (zs, zr, own, s1, r1, s2, r2, s3, r3))
+    steps = gather_steps(count, ucol, udown, ocol, odown, (zs, zr, own, s1, r1, s2, r2, s3, r3), prepare)
     plan, ready = gather_plan()
     last = len(plan) - 1
     done = [-1]
@@ -533,7 +620,7 @@
             loads(layer, part).wait()
 
         layer_body(
-            layer, xs.at[2 * layer], vec, mask_ref,
+            layer, xs.at[2 * layer], vec,
             (xs.at[2 * layer + 2], xs.at[2 * layer + 1], fa.at[layer], gp.at[layer], qk.at[layer]),
             (wbuf, dbuf, qsend, osend, kall, vall, acc), orecv.at[layer], sems[layer], fetch, tick,
         )
@@ -550,11 +637,14 @@
             copy.start()
         copies += more
         allowed.update((layer + 1, part) for part in (1, 2) if layer + 1 < L)
+    unit_over(2).wait_recv()
+    loss_part(
+        f == 0, g * 2 + x, xs.at[2 * L], vec, classes, labels, clip_weights, class_bias, dout, head, end_rows, small
+    )
+    copies.append(pltpu.make_async_copy(dout, dout_out, osem.at[0]))
+    copies[-1].start()
     need(last)
     next(steps)
-    unit_over(2).wait_recv()
-    copies.append(pltpu.make_async_copy(classes, oclass, osem.at[0]))
-    copies[-1].start()
     for n in range(3):
         for dz in range(1, count):
             unit_along(n, dz).wait_send()
@@ -564,26 +654,29 @@
         copy.wait()
 
 
-def forward_all(times, ucol, udown, uemb, upatch, uclass, stats, pkeep, psend, mask):
+def forward_all(times, wide, down, uemb, upatch, uclass, live, pkeep, psend, labels, clip_weights, class_bias, mask):
     count = times // 2
     total = len(SUBS)
     dma = pltpu.SemaphoreType.DMA
     outs = (
         ((2 * L, 2, 2, count, 2, 96, D), BF),
         ((L, count, 2, 2, 192, D), BF),
-        ((count, 2, 96, CMAIN), BF),
         ((EWIDE, D), F32),
         ((2 * L + 1, TOK, D), F32),
         ((L, 7, TOK, D), BF),
         ((L, FF // D, TOK, D), F32),
         ((L, PER, NF, QROWS, 128), BF),
         ((TOK, PATCH), BF),
+        ((TOK, D), F32),
+        ((2, 16, D), BF),
+        ((2, D), F32),
+        ((8, 128), F32),
     )
     return pl.pallas_call(
         functools.partial(forward_all_kernel, times),
         out_shape=tuple(jax.ShapeDtypeStruct(*o) for o in outs),
-        in_specs=[vspec()] * 9,
-        out_specs=(aspec(),) * len(outs),
+        in_specs=[aspec()] * 2 + [vspec()] * 9 + [aspec()],
+        out_specs=(aspec(),) * (len(outs) - 3) + (vspec(),) * 3,
         scratch_shapes=FORWARD_SCRATCH
         + [
             VM((L, PER, NF, TOK // 2, 128), BF),
@@ -603,12 +696,21 @@
             dma((3, count - 1)), dma((3, count - 1)), dma((3,)), dma((3,)),
             dma, dma, dma, dma, dma((L, 3)), dma((12,)),
         ]
-        + exchange_sems() * L,
+        + exchange_sems() * L
+        + [
+            VM((2 * L, 2, 2, 96, D), BF),
+            VM((L, 2, 192, D), BF),
+            VM((2 * L, 96, 4 * D), F32),
+            VM((L, 4 * 96, D), F32),
+            VM((8, 128), F32),
+            VM((TOK, D), F32),
+            dma((len(GROUPS),)),
+        ],
         compiler_params=pltpu.CompilerParams(
             collective_id=1, has_side_effects=True, vmem_limit_bytes=VLIM
         ),
         name="forward_all",
-    )(ucol, udown, uemb, upatch, uclass, stats, pkeep, psend, mask)
+    )(wide, down, uemb, upatch, uclass, live, pkeep, psend, labels, clip_weights, class_bias, mask)
 
 
 BACKWARD_SCRATCH = [
@@ -616,7 +718,7 @@
     VM((PER, NF, TOK // 2, 128), BF),
     VM((PER, NF, QROWS, 128), BF),
     VM((PER, NF, QROWS, 128), BF),
-    VM((NF * TOK, HDIM), BF),
+    VM((NF * TOK, 128), BF),
     VM((NF * TOK, HDIM), BF),
     VM((NF * TOK, HDIM), F32),
     VM((NF * TOK, HDIM), F32),
@@ -625,7 +727,7 @@
 ]
 
 
-def backward_body(layer, dcur, er, ba, vec_ref, mask_ref, qk_ref, mats, slope, kept, scratch, sems, at):
+def backward_body(layer, dcur, er, ba, vec_ref, qk_ref, mats, slope, kept, scratch, sems, at):
     down, up, qkvo = mats
     dsend, drecv, gsend, grecv, kall, vall, dkall, dvall, dqall, acc = scratch
     ds_, dr_, gs_, gr_ = sems
@@ -676,12 +778,10 @@
             to_clip(j, i).start()
         drecv[j, f] = dsend[j, f]
     at("sent")
-    mask = mask_ref[...]
     root = HDIM ** (-0.5)
-    part = TOK // 2
     for j in range(PER):
         for s in range(NF):
-            kall[s * TOK : (s + 1) * TOK] = qk_ref[j, s, :TOK, HDIM:]
+            kall[s * TOK : (s + 1) * TOK, :HDIM] = qk_ref[j, s, :TOK, HDIM:]
             vall[s * TOK : (s + 1) * TOK] = open_half(qk_ref[j, s, TOK:])
         dkall[...] = jnp.zeros_like(dkall)
         dvall[...] = jnp.zeros_like(dvall)
@@ -689,9 +789,9 @@
             to_clip(j, i).wait_recv()
 
         def attend(s, carry):
-            q = qk_ref[j, s, :TOK, :HDIM]
+            q = with_mask(qk_ref[j, s, :TOK])
             dmix = open_half(drecv[j, s])
-            scores = nt(kall[...], q) * root + mask
+            scores = nt(kall[...], q)
             top = jnp.max(scores, 0, keepdims=True)
             expo = jnp.exp(scores - top)
             probs = expo * (1.0 / jnp.sum(expo, 0, keepdims=True))
@@ -699,14 +799,14 @@
             inner = jnp.sum(probs * dprob, 0, keepdims=True)
             dscore = (probs * (dprob - inner)).astype(BF)
             dvall[...] += nn(probs.astype(BF), dmix)
-            dkall[...] += nn(dscore, q)
-            dqall[s] = (tn(dscore, kall[...]) * root).astype(BF)
+            dkall[...] += nn(dscore, q[:, :HDIM])
+            dqall[s] = (tn(dscore, kall[:, :HDIM]) * root).astype(BF)
             return carry
 
         lax.fori_loop(0, NF, attend, 0)
         for s in range(NF):
             span = slice(s * TOK, (s + 1) * TOK)
-            gsend[j, s, :TOK] = jnp.concatenate([dqall[s], (dkall[span] * root).astype(BF)], 1)
+            gsend[j, s, :TOK] = jnp.concatenate([dqall[s], dkall[span].astype(BF)], 1)
             gsend[j, s, TOK:] = pack_half(dvall[span].astype(BF))
         for i in range(1, NF):
             back_clip(j, i).start()
@@ -735,7 +835,7 @@
 
 
 def backward_kernel(
-    layer, dout_ref, x_ref, x1_ref, gp_ref, qk_ref, vec_ref, mask_ref, wcol, wdown,
+    layer, dout_ref, x_ref, x1_ref, gp_ref, qk_ref, vec_ref, mask, wcol, wdown,
     dx_ref, ba_ref, er_ref, wbuf, dbuf, wsem, ds_, dr_, gs_, gr_, *scratch,
 ):
     loads = [
@@ -747,11 +847,12 @@
         load.start()
     dx_ref[...] = dout_ref[...]
     er_ref[...] = jnp.zeros_like(er_ref)
+    load_mask(mask, scratch[4])
     greet_clip()
     for load in loads:
         load.wait()
     backward_body(
-        layer, dx_ref, er_ref, ba_ref, vec_ref, mask_ref, qk_ref,
+        layer, dx_ref, er_ref, ba_ref, vec_ref, qk_ref,
         (lambda k: dbuf[k], lambda k: wbuf[1, k], lambda k: wbuf[0, k]),
         lambda k: gp_ref[k], lambda i: x1_ref[...] if i else x_ref[...],
         scratch, (ds_, dr_, gs_, gr_), lambda point: None,
@@ -766,7 +867,7 @@
             jax.ShapeDtypeStruct((9, TOK, D), BF),
             jax.ShapeDtypeStruct((EWIDE, D), F32),
         ),
-        in_specs=[vspec()] * 7 + [aspec()] * 2,
+        in_specs=[vspec()] * 6 + [aspec()] * 3,
         out_specs=(vspec(),) * 3,
         scratch_shapes=[VM((2, 4, D, D), BF), VM((4, D, D), BF), pltpu.SemaphoreType.DMA((3,))]
         + exchange_sems()
@@ -779,23 +880,24 @@
 
 
 RGROUPS = (("d", 1), ("u", 1), ("q", 1), ("d", 0), ("u", 0), ("q", 0))
-RFIRST = ("xx", "yx", "xx", "xx", "yx", "xx")
+RFIRST = ("xx", "yx", "xx", "yx", "yx", "xx")
 SLOTS_R = 2
+BUFS = 2
 PWIDE = (CMAIN, EWIDE + PATCH)
 STAGES = 5
 
 
 def backward_all_kernel(
-    times, dout_in, xs_in, gp_in, qk_in, fa_in, vec_ref, mask_ref, pn_ref, head_ref, end_ref, small, wcol, wdown,
-    gcol, gdown, gpart, small_all, square_all, rfa,
+    times, dout_in, xs_in, gp_in, qk_in, fa_in, vec_ref, mask, pn_ref, head_ref, end_ref, small, wcol, wdown,
+    gcol, gdown, gpart, scalars, rfa,
     *refs,
 ):
     (
         wbuf, gp, xb, dcur, er, qk, ba, lbuf, rd, ru, rq, full, low, recv1, mid_own, mid_low, recv2,
-        zlow, zown, zrecv, psend0, psend1, pown0, pown1, pxr0, pxr1, pzs0, pzs1, pzr0, pzr1, sq,
+        zlow, zown, zrecv, psend, pown, pxr0, pxr1, pzr0, pzr1, sq,
         wsem, gsem, xsem, qsem, ls, fas, far, bs, br, s1, r1, s2, r2, zs, zr, fs, fr, ks, kr,
         ss, sr, qs, qr, p1, p1r, p2, p2r, p3, p3r, p4, p4r, credit,
-        ds_, dr_, gs_, gr_,
+        ds_, dr_, gs_, gr_, small_all, square_all,
     ) = refs[: -len(BACKWARD_SCRATCH)]
     scratch = refs[-len(BACKWARD_SCRATCH) :]
     f, t, y, c, g, x = place()
@@ -882,10 +984,10 @@
             keep, index = x == xx, role
 
         def save_full():
-            full[(h, index) + where] = value
+            full[(gi % BUFS, h, index) + where] = value
 
         def save_low():
-            low[(h, index) + where] = value.astype(BF)
+            low[(gi % BUFS, h, index) + where] = value.astype(BF)
 
         if isinstance(keep, bool):
             (save_full if keep else save_low)()
@@ -893,7 +995,7 @@
             pl.when(keep)(save_full)
             pl.when(jnp.logical_not(keep))(save_low)
 
-    def compute(gi):
+    def compute(gi, h):
         kind, l = RGROUPS[gi]
         if kind == "d":
 
@@ -903,28 +1005,28 @@
                 ).reshape(2, 2, 2, 96, 384)
                 for xx in range(2):
                     for yy in range(2):
-                        for h in range(2):
-                            store(gi, h, (yy + y) % 2, xx, (z,), prod[xx, yy, h])
+                        for hh in range(2):
+                            store(gi, hh, (yy + y) % 2, xx, (z,), prod[xx, yy, hh])
                 return carry
 
-            lax.fori_loop(0, count, one, 0)
+            if h == 0:
+                lax.fori_loop(0, count, one, 0)
             return
         recv = ru if kind == "u" else rq
         base = 4 if kind == "u" else 0
         for role in range(2):
             yy = y if role == 0 else 1 - y
             left = 0 if kind == "u" else yy
-            for h in range(2):
-                cols = slice(h * 384, (h + 1) * 384)
-                prod = product(
-                    left, lambda cols: ba[base + 2 * yy + c, :, cols], lambda cols: recv[l, yy, :, cols], cols
-                ).reshape(count, 2, 96, 384)
-                for xx in range(2):
-                    store(gi, h, role, xx, (), prod[:, xx])
+            prod = product(
+                left, lambda cols: ba[base + 2 * yy + c, :, cols], lambda cols: recv[l, yy, :, cols],
+                slice(h * 384, (h + 1) * 384),
+            ).reshape(count, 2, 96, 384)
+            for xx in range(2):
+                store(gi, h, role, xx, (), prod[:, xx])
 
     def step1(gi, h):
         return remote(
-            low.at[h], recv1.at[gi % SLOTS_R, h], s1.at[gi, h], r1.at[gi, h],
+            low.at[gi % BUFS, h], recv1.at[gi % SLOTS_R, h], s1.at[gi, h], r1.at[gi, h],
             over_y if RFIRST[gi][h] == "y" else over_x,
         )
 
@@ -934,89 +1036,85 @@
             over_x if RFIRST[gi][h] == "y" else over_y,
         )
 
-    def along(gi, dz):
+    def along(gi, h, dz):
         return remote(
-            zlow.at[(g + dz) % count], zrecv.at[gi % SLOTS_R, dz - 1], zs.at[gi, dz - 1], zr.at[gi, dz - 1],
-            (f, ((g + dz) % count) * 2 + x),
-        )
-
-    def result(gi, yy):
+            zlow.at[h, (g + dz) % count], zrecv.at[gi % SLOTS_R, h, dz - 1],
+            zs.at[gi, h, dz - 1], zr.at[gi, h, dz - 1], (f, ((g + dz) % count) * 2 + x),
+        )
+
+    def result(gi, h, yy):
         kind, l = RGROUPS[gi]
         if kind == "d":
-            return gdown.at[l, yy, :, half_cols(c)]
-        return gcol.at[2 * l + (1 if kind == "u" else 0), yy, c]
-
-    def spread_y(gi):
-        block = result(gi, y)
-        return remote(block, block, fs.at[gi], fr.at[gi], over_y)
-
-    def spread_c(gi):
-        block = result(gi, slice(None))
-        return remote(block, block, ks.at[gi], kr.at[gi], over_c)
-
-    def advance(gi, stage):
-        slot = gi % SLOTS_R
+            return gdown.at[l, yy, pl.ds(h * 96, 96), half_cols(c)]
+        return gcol.at[2 * l + (1 if kind == "u" else 0), yy, c, :, pl.ds(h * 384, 384)]
+
+    def spread_y(gi, h):
+        block = result(gi, h, y)
+        return remote(block, block, fs.at[gi, h], fr.at[gi, h], over_y)
+
+    def spread_c(gi, h):
+        block = result(gi, h, slice(None))
+        return remote(block, block, ks.at[gi, h], kr.at[gi, h], over_c)
+
+    def advance(gi, h, stage):
+        slot, buf = gi % SLOTS_R, gi % BUFS
         if stage == 1:
-            for h in range(2):
-                step1(gi, h).wait_recv()
-                step1(gi, h).wait_send()
-                keep, send = (x, 1 - x) if RFIRST[gi][h] == "y" else (0, 1)
-                mid_low[h] = (full[h, send] + recv1[slot, h, send].astype(F32)).astype(BF)
-                step2(gi, h).start()
-                mid_own[h] = full[h, keep] + recv1[slot, h, keep].astype(F32)
+            step1(gi, h).wait_recv()
+            step1(gi, h).wait_send()
+            keep, send = (x, 1 - x) if RFIRST[gi][h] == "y" else (0, 1)
+            mid_low[h] = (full[buf, h, send] + recv1[slot, h, send].astype(F32)).astype(BF)
+            step2(gi, h).start()
+            mid_own[h] = full[buf, h, keep] + recv1[slot, h, keep].astype(F32)
         elif stage == 2:
-            for h in range(2):
-                step2(gi, h).wait_recv()
-                step2(gi, h).wait_send()
-                summed = mid_own[h] + recv2[slot, h].astype(F32)
-                zlow[:, h] = summed.astype(BF)
-                mid_own[h] = summed
-            if gi >= SLOTS_R:
-                for dz in range(1, count):
+            step2(gi, h).wait_recv()
+            step2(gi, h).wait_send()
+            summed = mid_own[h] + recv2[slot, h].astype(F32)
+            zlow[h] = summed.astype(BF)
+            mid_own[h] = summed
+            for dz in range(1, count):
+                if gi >= SLOTS_R:
                     pl.semaphore_wait(credit.at[1 + dz], 1)
-            for dz in range(1, count):
-                along(gi, dz).start()
-            for h in range(2):
-                zown[h] = mid_own[h, g]
+                along(gi, h, dz).start()
+            zown[h] = mid_own[h, g]
             if gi + SLOTS_R < total:
                 pl.semaphore_signal(credit.at[0], inc=1, device_id=over_x, device_id_type=MESH)
                 pl.semaphore_signal(credit.at[1], inc=1, device_id=over_y, device_id_type=MESH)
         elif stage == 3:
+            value = zown[h]
             for dz in range(1, count):
-                along(gi, dz).wait_recv()
-                along(gi, dz).wait_send()
-            for h in range(2):
-                value = zown[h]
-                for dz in range(1, count):
-                    value = value + zrecv[slot, dz - 1, h].astype(F32)
-                sq[...] += jnp.sum((value * value).reshape(12, 8, 3, 128), (0, 2))
-                kind, l = RGROUPS[gi]
-                if kind == "d":
-                    gdown[l, y, h * 96 : (h + 1) * 96, half_cols(c)] = value.astype(BF)
-                else:
-                    idx = 2 * l + (1 if kind == "u" else 0)
-                    gcol[idx, y, c, :, h * 384 : (h + 1) * 384] = value.astype(BF)
+                along(gi, h, dz).wait_recv()
+                along(gi, h, dz).wait_send()
+                value = value + zrecv[slot, h, dz - 1].astype(F32)
+            sq[...] += jnp.sum((value * value).reshape(12, 8, 3, 128), (0, 2))
+            kind, l = RGROUPS[gi]
+            if kind == "d":
+                gdown[l, y, h * 96 : (h + 1) * 96, half_cols(c)] = value.astype(BF)
+            else:
+                idx = 2 * l + (1 if kind == "u" else 0)
+                gcol[idx, y, c, :, h * 384 : (h + 1) * 384] = value.astype(BF)
             if gi + SLOTS_R < total:
                 for dz in range(1, count):
+                    back = (f, ((g + count - dz) % count) * 2 + x)
                     pl.semaphore_signal(
-                        credit.at[1 + dz], inc=1, device_id=(f, ((g + count - dz) % count) * 2 + x), device_id_type=MESH
+                        credit.at[1 + dz], inc=1, device_id=back, device_id_type=MESH
                     )
-            spread_y(gi).start()
+            spread_y(gi, h).start()
         elif stage == 4:
-            spread_y(gi).wait_recv()
-            spread_c(gi).start()
+            spread_y(gi, h).wait_recv()
+            spread_c(gi, h).start()
         else:
-            spread_c(gi).wait_recv()
-
-    psends, powns, pxrs, pzss, pzrs = (psend0, psend1), (pown0, pown1), (pxr0, pxr1), (pzs0, pzs1), (pzr0, pzr1)
-    pspans = (slice(0, CMAIN), slice(CMAIN, CMAIN + PWIDE[1]))
+            spread_c(gi, h).wait_recv()
+
+    pxrs, pzrs = (pxr0, pxr1), (pzr0, pzr1)
+    psends = [psend.at[:, :, pl.ds(0, w)] for w in PWIDE]
+    powns = [pown.at[:, :, pl.ds(0, w)] for w in PWIDE]
 
     def part_over(n):
         return remote(psends[n], pxrs[n], p1.at[n], p1r.at[n], over_x)
 
     def part_along(n, dz):
         return remote(
-            pzss[n].at[(g + dz) % count], pzrs[n].at[dz - 1], p2.at[n, dz - 1], p2r.at[n, dz - 1],
+            psends[n].at[(g + dz) % count], pzrs[n].at[dz - 1], p2.at[n, dz - 1], p2r.at[n, dz - 1],
             (f, ((g + dz) % count) * 2 + x),
         )
 
@@ -1052,13 +1150,15 @@
             part_over(n).wait_recv()
             summed = powns[n][...] + pxrs[n][...].astype(F32)
             powns[n][...] = summed
-            pzss[n][...] = summed.astype(BF)
+            part_over(n).wait_send()
+            psends[n][...] = summed.astype(BF)
             for dz in range(1, count):
                 part_along(n, dz).start()
         elif stage == 2:
             value = powns[n][g]
             for dz in range(1, count):
                 part_along(n, dz).wait_recv()
+                part_along(n, dz).wait_send()
                 value = value + pzrs[n][dz - 1].astype(F32)
             gpart[n, y, c, :, : PWIDE[n]] = value.astype(BF)
             part_y(n).start()
@@ -1085,37 +1185,42 @@
 
     def tick():
         for entry in list(under_way):
-            entry[2] += 1
-            (advance if entry[0] == "group" else part_advance)(entry[1], entry[2])
-            if entry[2] == (STAGES if entry[0] == "group" else STAGES - 1):
+            after = entry[3] + 1
+            if entry[0] == "group" and after < 3 and stage_of("group", entry[1] - 1, entry[2]) <= after:
+                continue
+            entry[3] = after
+            if entry[0] == "part":
+                part_advance(entry[1], entry[3])
+            else:
+                advance(entry[1], entry[2], entry[3])
+            if entry[3] == (STAGES if entry[0] == "group" else STAGES - 1):
                 under_way.remove(entry)
 
-    def stage_of(kind, n):
+    def stage_of(kind, n, h=0):
         for entry in under_way:
-            if entry[0] == kind and entry[1] == n:
-                return entry[2]
+            if entry[:3] == [kind, n, h]:
+                return entry[3]
         return STAGES
 
     def launch(gi):
-        while gi > 0 and stage_of("group", gi - 1) < 1:
-            tick()
-        l = RGROUPS[gi][1]
         for n in swaps(gi):
             swap(gi, n).wait_recv()
         for copy in left_loads(gi):
             copy.wait()
-        if gi >= SLOTS_R:
-            while stage_of("group", gi - SLOTS_R) < 2:
+        for h in range(2):
+            hs = range(2) if RGROUPS[gi][0] == "d" else (h,)
+            while any(gi >= BUFS and stage_of("group", gi - BUFS, i) < 1 for i in hs):
                 tick()
-        compute(gi)
+            while gi >= SLOTS_R and stage_of("group", gi - SLOTS_R, h) < 2:
+                tick()
+            compute(gi, h)
+            if gi >= SLOTS_R:
+                pl.semaphore_wait(credit.at[0], 1)
+                pl.semaphore_wait(credit.at[1], 1)
+            step1(gi, h).start()
+            under_way.append(["group", gi, h, 0])
         for n in swaps(gi):
             swap(gi, n).wait_send()
-        if gi >= SLOTS_R:
-            pl.semaphore_wait(credit.at[0], 1)
-            pl.semaphore_wait(credit.at[1], 1)
-        for h in range(2):
-            step1(gi, h).start()
-        under_way.append(["group", gi, 0])
         if gi + 1 < total:
             prepare(gi + 1)
 
@@ -1132,8 +1237,9 @@
 
     def launch_part(n):
         part_compute(n)
-        under_way.append(["part", n, 0])
-
+        under_way.append(["part", n, 0, 0])
+
+    load_mask(mask, scratch[4])
     sq[...] = jnp.zeros_like(sq)
     er[...] = jnp.zeros_like(er)
     er[EVEC + GLOB + 3 : EVEC + GLOB + 5, :] = end_ref[...]
@@ -1189,9 +1295,9 @@
                     heads_load(layer).wait()
                 launch(base)
             elif point == "head0":
+                launch(base + 1)
+            elif point == "head1":
                 tick()
-            elif point == "head1":
-                launch(base + 1)
             elif point == "head2":
                 tick()
                 if layer > 0:
@@ -1207,7 +1313,7 @@
                     launch(base + 2)
 
         backward_body(
-            layer, dcur, er, ba, vec_ref, mask_ref, qk, (mat(0), mat(1), mat(2)), slope, kept, scratch,
+            layer, dcur, er, ba, vec_ref, qk, (mat(0), mat(1), mat(2)), slope, kept, scratch,
             (ds_.at[layer], dr_.at[layer], gs_.at[layer], gr_.at[layer]), at,
         )
     dgrid = dcur[...]
@@ -1221,7 +1327,7 @@
     shared = False
     while under_way:
         tick()
-        if not shared and stage_of("group", total - 1) >= 3 and stage_of("part", 1) >= STAGES - 1:
+        if not shared and stage_of("group", total - 1, 1) >= 3 and stage_of("part", 1) >= STAGES - 1:
             shared = True
             n = NF * times
             me = f * times + t
@@ -1237,16 +1343,21 @@
         for n in range(2):
             forward_swap(layer, n).wait_send()
     for gi in range(total):
-        spread_y(gi).wait_send()
-        spread_c(gi).wait_send()
+        for h in range(2):
+            spread_y(gi, h).wait_send()
+            spread_c(gi, h).wait_send()
     for n in range(2):
-        part_over(n).wait_send()
-        for dz in range(1, count):
-            part_along(n, dz).wait_send()
         part_y(n).wait_send()
         part_c(n).wait_send()
     wait_small(times, small_all, ss, sr)
     wait_small(times, square_all, qs, qr)
+    summed = jnp.sum(small_all[...], 0)
+    spot = lax.broadcasted_iota(jnp.int32, (8, 128), 0) * 128 + lax.broadcasted_iota(jnp.int32, (8, 128), 1)
+    bias = jnp.where(spot < CLASSES, summed, 0.0)
+    norm = jnp.sqrt(jnp.sum(jnp.sum(square_all[...], 0) + bias * bias, keepdims=True))
+    scalars[0] = summed
+    scalars[1] = jnp.broadcast_to(norm, (8, 128))
+    scalars[2] = jnp.broadcast_to(jnp.minimum(1.0, 1.0 / (norm + 1e-06)), (8, 128))
 
 
 def backward_all(times, dout, xs, gp, qk, fa, vec, mask, pnorm, head, end_rows, small, wcol, wdown):
@@ -1261,12 +1372,11 @@
             jax.ShapeDtypeStruct((2 * L, 2, 2, 96, D), BF),
             jax.ShapeDtypeStruct((L, 2, 192, D), BF),
             jax.ShapeDtypeStruct((2, 2, 2, 96, most), BF),
-            jax.ShapeDtypeStruct((n, 8, 128), F32),
-            jax.ShapeDtypeStruct((n, 8, 128), F32),
+            jax.ShapeDtypeStruct((3, 8, 128), F32),
             jax.ShapeDtypeStruct(fa.shape, BF),
         ),
-        in_specs=[aspec()] * 5 + [vspec()] * 6 + [aspec()] * 2,
-        out_specs=(vspec(),) * 5 + (aspec(),),
+        in_specs=[aspec()] * 5 + [vspec()] + [aspec()] + [vspec()] * 4 + [aspec()] * 2,
+        out_specs=(vspec(),) * 4 + (aspec(),),
         scratch_shapes=[
             VM((2, 4, D, D), BF),
             VM((2, TOK, D), F32),
@@ -1279,37 +1389,38 @@
             VM((L, TOK, 384), BF),
             VM((L, 2, TOK, D), BF),
             VM((L, 2, TOK, D), BF),
-            VM((2, 2, count, 96, 384), F32),
-            VM((2, 2, count, 96, 384), BF),
+            VM((BUFS, 2, 2, count, 96, 384), F32),
+            VM((BUFS, 2, 2, count, 96, 384), BF),
             VM((SLOTS_R, 2, 2, count, 96, 384), BF),
             VM((2, count, 96, 384), F32),
             VM((2, count, 96, 384), BF),
             VM((SLOTS_R, 2, count, 96, 384), BF),
-            VM((count, 2, 96, 384), BF),
+            VM((2, count, 96, 384), BF),
             VM((2, 96, 384), F32),
-            VM((SLOTS_R, count - 1, 2, 96, 384), BF),
-            *[VM((count, 96, w), BF) for w in PWIDE],
-            *[VM((count, 96, w), F32) for w in PWIDE],
-            *[VM((count, 96, w), BF) for w in PWIDE],
+            VM((SLOTS_R, 2, count - 1, 96, 384), BF),
+            VM((count, 96, most), BF),
+            VM((count, 96, most), F32),
             *[VM((count, 96, w), BF) for w in PWIDE],
             *[VM((count - 1, 96, w), BF) for w in PWIDE],
             VM((8, 128), F32),
             dma((L, 3)), dma((L, 4)), dma((L, 2)), dma((L + 1,)), dma((4, 2)),
             dma((L, 2)), dma((L, 2)), dma((total, 2)), dma((total, 2)),
             dma((total, 2)), dma((total, 2)), dma((total, 2)), dma((total, 2)),
-            dma((total, count - 1)), dma((total, count - 1)),
-            dma((total,)), dma((total,)), dma((total,)), dma((total,)),
+            dma((total, 2, count - 1)), dma((total, 2, count - 1)),
+            dma((total, 2)), dma((total, 2)), dma((total, 2)), dma((total, 2)),
             dma, dma, dma, dma,
             dma((2,)), dma((2,)), dma((2, count - 1)), dma((2, count - 1)), dma((2,)), dma((2,)), dma((2,)), dma((2,)),
             pltpu.SemaphoreType.REGULAR((count + 1,)),
             *[dma((L, PER, NF - 1))] * 4,
+            VM((n, 8, 128), F32),
+            VM((n, 8, 128), F32),
         ]
         + BACKWARD_SCRATCH,
         compiler_params=pltpu.CompilerParams(
-            collective_id=2 + 2 * L, has_side_effects=True, vmem_limit_bytes=63 * 1024 * 1024
+            collective_id=2 + 2 * L, has_side_effects=True, vmem_limit_bytes=65400 * 1024
         ),
         name="backward_all",
-    )(dout, xs, gp, qk, fa, vec, mask, pnorm, head, end_rows, small, wcol, wdown)[:5]
+    )(dout, xs, gp, qk, fa, vec, mask, pnorm, head, end_rows, small, wcol, wdown)[:4]
 
 
 def adam(weight, first, second, grad):
@@ -1317,10 +1428,91 @@
     second = DECAY_SECOND * second + (1.0 - DECAY_SECOND) * grad * grad
     fix_one = 1.0 - DECAY_FIRST**STEP
     fix_two = 1.0 - DECAY_SECOND**STEP
-    weight = weight - LEARN_RATE * (
-        first / fix_one / (jnp.sqrt(second / fix_two) + EPSILON) + WEIGHT_DECAY * weight
+    scaled = jnp.sqrt(second * (1.0 / fix_two)) + EPSILON
+    weight = weight * (1.0 - LEARN_RATE * WEIGHT_DECAY) - (LEARN_RATE / fix_one) * first / scaled
+    return (weight, first, second)
+
+
+PIECES = 2
+WIDE_STEPS = L * 8 // PIECES
+DOWN_STEPS = L * 4 // PIECES
+
+
+def update_kernel(*refs):
+    scalars, gcol, gdown, gpart = refs[:4]
+    ins, outs, gemb = refs[4:19], refs[19:38], refs[38]
+    step = pl.program_id(0)
+    coef = scalars[2, 0:1, 0:1]
+
+    def apply(which, grad, at=...):
+        new = adam(*(ins[which + 5 * i][at] for i in range(3)), grad * coef)
+        for i in range(3):
+            outs[which + 5 * i][at] = new[i]
+        if which < 4:
+            outs[15 + which][at] = new[0].astype(BF)
+
+    @pl.when(step < WIDE_STEPS)
+    def _():
+        for p in range(PIECES):
+            apply(0, gcol[0, p].astype(F32), (0, slice(None), slice(p * D, (p + 1) * D)))
+
+    @pl.when(step >= WIDE_STEPS)
+    def _():
+        apply(1, gdown[0].astype(F32), (0,))
+
+    @pl.when(step == 0)
+    def _():
+        main = sum(gpart[0, i, :, :CMAIN].astype(F32) for i in range(NF))
+        rest = sum(gpart[1, i, :, EVEC:].astype(F32) for i in range(NF))
+        per = FROWS // NF
+        for i in range(NF):
+            block = gpart[1, i].astype(F32)
+            for h in range(2):
+                for r in range(per):
+                    to = (i * per + r) * 2 * HALF + h * HALF
+                    gemb[:, to : to + HALF] = block[:, h * SLOTS + r * HALF : h * SLOTS + (r + 1) * HALF]
+        gemb[:, NGRID:] = rest[:, EWIDE - EVEC :]
+        apply(2, gemb[...])
+        tail = rest[:, ECLS - EVEC : ECLS - EVEC + CLASSES - CMAIN]
+        apply(3, jnp.concatenate([main, tail], 1))
+        turned = rest[:, : 128].T
+        apply(4, turned[:VROWS])
+
+
+def update(scalars, gcol, gdown, gpart, params, firsts, seconds):
+    shard = gcol.shape[2]
+    per_wide, per_down = 8 // PIECES, 4 // PIECES
+
+    def wide(step):
+        step = jnp.minimum(step, WIDE_STEPS - 1)
+        return (step // per_wide, 0, step % per_wide)
+
+    def wide_grad(step):
+        step = jnp.minimum(step, WIDE_STEPS - 1)
+        return (step // per_wide, step % per_wide, 0, 0)
+
+    def down(step):
+        step = jnp.maximum(step - WIDE_STEPS, 0)
+        return (step // per_down, step % per_down, 0)
+
+    params, firsts, seconds = (
+        [v[0], v[1], v[2].T, v[3], v[4]] for v in (params, firsts, seconds)
     )
-    return (weight, first, second)
+    down_block = pl.BlockSpec((1, PIECES * shard, D), down)
+    specs = [pl.BlockSpec((1, shard, PIECES * D), wide), down_block] + [vspec()] * 3
+    shapes = [jax.ShapeDtypeStruct(v.shape, F32) for v in params] * 3
+    shapes += [jax.ShapeDtypeStruct(v.shape, BF) for v in params[:4]]
+    news = pl.pallas_call(
+        update_kernel,
+        grid=(WIDE_STEPS + DOWN_STEPS,),
+        out_shape=shapes,
+        in_specs=[vspec(), pl.BlockSpec((1, PIECES, shard, D), wide_grad), down_block, vspec()] + specs * 3,
+        out_specs=specs * 3 + specs[:4],
+        scratch_shapes=[VM((shard, NGRID + PATCH), F32)],
+        compiler_params=pltpu.CompilerParams(vmem_limit_bytes=48 * 1024 * 1024),
+        name="update",
+    )(scalars, gcol, gdown, gpart, *params, *firsts, *seconds)
+    return [v.T if i % 5 == 2 else v for i, v in enumerate(news)]
 
 
 def pad_to(v, axis, size):
@@ -1365,22 +1557,13 @@
     mine_columns = lax.dynamic_index_in_dim(columns, t, 0, keepdims=False)
     raw = patches.reshape(rows_dev, CPD, HALF, PATCH)
 
-    pixels = raw.astype(F32)
-    live = mine_columns.astype(F32)[None, :, :, None]
-    sums = jnp.stack(
-        [
-            jnp.sum(pixels * live),
-            jnp.sum(pixels * pixels * live),
-            jnp.sum(live) * (rows_dev * PATCH),
-        ]
-    )
     keep_block, give_block = (
         pad_to(lax.dynamic_index_in_dim(raw, i, 1, keepdims=False).reshape(GRID, PATCH), 0, SLOTS)
         for i in (half, 1 - half)
     )
 
-    wide_low = wide_weights.astype(BF)
-    down_low = down_weights.astype(BF)
+    live = jnp.stack([pad_to(jnp.tile(mine_columns[i], rows_dev), 0, SLOTS) for i in range(2)])
+    live = jnp.where(half == 0, live, live[::-1]).astype(F32)[:, :, None]
     unit_embed, unit_patch, unit_class = embed_units(embedding, classifier, vectors, f)
 
     clip_columns = lax.dynamic_slice(columns, (pair * 2, half, 0), (2, 1, HALF)).reshape(2, HALF)
@@ -1394,23 +1577,27 @@
         ],
         2,
     ).reshape(NF * TOK)
-    mask = jnp.where(slots, 0.0, -1e30).astype(F32)
-
+    mask = jnp.where(slots[:, None] | (jnp.arange(128) != HDIM)[None, :], 0.0, -1e30).astype(BF)
+
+    weight_total = jnp.sum(clip_weights).astype(F32)
     if kernels:
-        units = wide_low.reshape(L, shard, 2, 4, D).transpose(0, 2, 3, 1, 4)
-        wcol, wdown, class_main, vec, xs, fa, gp, qk, pnorm = forward_all(
-            times, units.reshape(2 * L, 2, 2, shard, D), down_low.reshape(L, 2, 192, D), unit_embed, unit_patch, unit_class,
-            jnp.broadcast_to(pad_to(sums, 0, 128), (8, 128)), keep_block, give_block, mask.reshape(1, -1),
-        )
-        class_main = class_main.reshape(D, CMAIN)
+        wcol, wdown, vec, xs, fa, gp, qk, pnorm, dx, head, end_rows, small = forward_all(
+            times, wide_weights, down_weights, unit_embed, unit_patch, unit_class, live, keep_block, give_block,
+            pad_to(labels, 1, D), clip_weights[None], pad_to(class_bias[None], 1, D), mask,
+        )
     else:
-        wide_all = lax.all_gather(wide_low, "tm", axis=1, tiled=True)
+        wide_all = lax.all_gather(wide_weights.astype(BF), "tm", axis=1, tiled=True)
         wcol = wide_all.reshape(L, D, 2, 4, D).transpose(0, 2, 3, 1, 4)
         wcol = wcol.reshape(2 * L, 2, 2, 4, 2, 96, D)
-        wdown = lax.all_gather(down_low, "tm", axis=1, tiled=True).reshape(L, 4, 2, 2, 192, D)
+        wdown = lax.all_gather(down_weights.astype(BF), "tm", axis=1, tiled=True)
+        wdown = wdown.reshape(L, 4, 2, 2, 192, D)
         vec = lax.all_gather(unit_embed, "tm", axis=0, tiled=True).T.astype(F32)
         patch = lax.all_gather(unit_patch, "tm", axis=0, tiled=True)
         class_main = lax.all_gather(unit_class, "tm", axis=0, tiled=True)
+        pixels = jnp.stack([keep_block, give_block]).astype(F32)
+        sums = jnp.stack(
+            [jnp.sum(pixels * live), jnp.sum(pixels * pixels * live), jnp.sum(live) * PATCH]
+        )
         sums = lax.psum(sums, ("freq", "tm"))
         take_block = lax.ppermute(
             give_block, "tm", [(i, i + 1 - 2 * (i % 2)) for i in range(times)]
@@ -1425,61 +1612,60 @@
         x = nt(pnorm, patch) + vec[:TOK] + jnp.where(inside, vec[EVEC + GLOB], 0.0)
         xs, fa, gp, qk = [x], [], [], []
         for layer in range(L):
-            x, x1, acts, slopes, heads = forward_layer(layer, x, vec, mask.reshape(1, -1), wcol, wdown)
+            x, x1, acts, slopes, heads = forward_layer(layer, x, vec, mask, wcol, wdown)
             xs += [x1, x]
             fa.append(acts)
             gp.append(slopes)
             qk.append(heads)
     wcol = wcol.reshape(2 * L, 4, D, D)
     wdown = wdown.reshape(L, 4, D, D)
-    vec_all = vec[EVEC : EVEC + VROWS]
-    class_all = jnp.concatenate([class_main, vec[ECLS : ECLS + CLASSES - CMAIN].T.astype(BF)], 1)
-
-    owner = (f == 0).astype(F32)
-    special = xs[2 * L][GRID : GRID + 2]
-    normed_end, scale_end = norm_rows(special)
-    feature = jnp.mean(normed_end * vec_all[GLOB + 3] + vec_all[GLOB + 4], 0, keepdims=True).astype(BF)
-    logits = nn(feature, class_all) + class_bias
-    clip = pair * CPD + half
-    flags = lax.dynamic_slice_in_dim(labels, clip, 1, 0).astype(F32)
-    weight = lax.dynamic_slice_in_dim(clip_weights, clip, 1, 0).astype(F32)[:, None]
-    weight_total = jnp.sum(clip_weights).astype(F32)
-    loss_part = owner * jnp.sum(weight * (jax.nn.softplus(logits) - flags * logits))
-    dlogits = owner * weight * (jax.nn.sigmoid(logits) - flags) / weight_total
-    dlogits_low = dlogits.astype(BF)
-    dfinal = jnp.broadcast_to(0.5 * nt(dlogits_low, class_all), (2, D))
-    dspecial = norm_back(dfinal * vec_all[GLOB + 3], normed_end, scale_end)
-    end_rows = jnp.stack([jnp.sum(dfinal * normed_end, 0), jnp.sum(dfinal, 0)])
-    dx = jnp.concatenate(
-        [jnp.zeros((GRID, D), F32), dspecial, jnp.zeros((TOK - GRID - 2, D), F32)], 0
-    )
-    small = jnp.concatenate([dlogits.reshape(-1), loss_part.reshape(1)])
-    small = pad_to(small, 0, 1024).reshape(8, 128)
+    if not kernels:
+        vec_all = vec[EVEC : EVEC + VROWS]
+        class_all = jnp.concatenate([class_main, vec[ECLS : ECLS + CLASSES - CMAIN].T.astype(BF)], 1)
+
+        owner = (f == 0).astype(F32)
+        special = xs[2 * L][GRID : GRID + 2]
+        normed_end, scale_end = norm_rows(special)
+        feature = jnp.mean(normed_end * vec_all[GLOB + 3] + vec_all[GLOB + 4], 0, keepdims=True).astype(BF)
+        logits = nn(feature, class_all) + class_bias
+        clip = pair * CPD + half
+        flags = lax.dynamic_slice_in_dim(labels, clip, 1, 0).astype(F32)
+        weight = lax.dynamic_slice_in_dim(clip_weights, clip, 1, 0).astype(F32)[:, None]
+        loss_part = owner * jnp.sum(weight * (jax.nn.softplus(logits) - flags * logits))
+        dlogits = owner * weight * (jax.nn.sigmoid(logits) - flags) / weight_total
+        dlogits_low = dlogits.astype(BF)
+        dfinal = jnp.broadcast_to(0.5 * nt(dlogits_low, class_all), (2, D))
+        dspecial = norm_back(dfinal * vec_all[GLOB + 3], normed_end, scale_end)
+        end_rows = jnp.stack([jnp.sum(dfinal * normed_end, 0), jnp.sum(dfinal, 0)])
+        dx = jnp.concatenate(
+            [jnp.zeros((GRID, D), F32), dspecial, jnp.zeros((TOK - GRID - 2, D), F32)], 0
+        )
+        small = jnp.concatenate([dlogits.reshape(-1), loss_part.reshape(1)])
+        small = pad_to(small, 0, 1024).reshape(8, 128)
     if kernels:
-        head = jnp.stack([pad_to(feature, 0, 16), pad_to(pad_to(dlogits_low, 1, D), 0, 16)])
-        gcol, gdown, gpart, small_all, square_all = backward_all(
-            times, dx, xs, gp, qk, fa, vec, mask.reshape(-1, 1), pnorm, head, end_rows, small, wcol, wdown
-        )
-        small = jnp.sum(small_all, 0).reshape(-1)
-        square_total = jnp.sum(square_all)
-        gcol = gcol.astype(F32)
-        grad_wide = gcol.reshape(L, 2, 4, shard, D).transpose(0, 3, 1, 2, 4).reshape(L, shard, 8 * D)
-        grad_down = gdown.reshape(L, FF // times, D).astype(F32)
-        gpart = gpart.astype(F32).reshape(2, NF, shard, -1)
-        grad_pos = gpart[1, :, :, :TOK].reshape(NF, shard, 2, SLOTS)[:, :, :, :GRID]
-        grad_pos = grad_pos.reshape(NF, shard, 2, rows_dev, HALF).transpose(0, 3, 2, 4, 1).reshape(NGRID, shard)
-        summed = jnp.sum(gpart, 1)
-        grad_embed = jnp.concatenate([grad_pos, summed[1, :, EWIDE : EWIDE + PATCH].T], 0)
-        grad_class = jnp.concatenate(
-            [summed[0, :, :CMAIN], summed[1, :, ECLS : ECLS + CLASSES - CMAIN]], 1
-        )
-        grad_vectors = summed[1, :, EVEC : EVEC + VROWS].T
+        gcol, gdown, gpart, scalars = backward_all(
+            times, dx, xs, gp, qk, fa, vec, mask, pnorm, head, end_rows, small, wcol, wdown
+        )
+        small = scalars[0].reshape(-1)
+        grad_norm, coef = scalars[1, 0, 0], scalars[2, 0, 0]
+        params = (wide_weights, down_weights, embedding, classifier, vectors)
+        firsts = (wide_first, down_first, embedding_first, classifier_first, vectors_first)
+        seconds = (wide_second, down_second, embedding_second, classifier_second, vectors_second)
+        news = update(
+            scalars, gcol.reshape(L, 8, shard, D), gdown.reshape(L, FF // times, D),
+            gpart.reshape(2, NF, shard, -1), params, firsts, seconds,
+        )
+        bias = adam(class_bias, bias_first, bias_second, small[:CLASSES] * coef)
+        return (
+            *news[:5], bias[0], *news[5:10], bias[1], *news[10:15], bias[2], *news[15:],
+            grad_norm, small[CLASSES], weight_total,
+        )
     else:
         ba = [None] * L
         er = jnp.zeros((EWIDE, D), F32)
         for layer in reversed(range(L)):
             dx, ba[layer], rows = backward_layer(
-                layer, dx, xs[2 * layer], xs[2 * layer + 1], gp[layer], qk[layer], vec, mask.reshape(-1, 1), wcol, wdown
+                layer, dx, xs[2 * layer], xs[2 * layer + 1], gp[layer], qk[layer], vec, mask, wcol, wdown
             )
             er = er + rows
         dgrid = jnp.where(inside, dx, 0.0)

time: 604 us -> 552 us (0.914)
  other arithmetic: 49.9 us -> 5.46 us
  local copies, waits for them, and re-layouts: 38 us -> 21 us
  Pallas kernels: 501 us -> 514 us
    pallas_call x0 -> x1, Pallas kernels: none -> 25.3 us  [update(): pl.pallas_call(update_kernel, grid=(WIDE_STEPS + DOWN_STEPS,), out_shape=...]
    convert_element_type x8 -> x1, other arithmetic: 25 us -> 0.97 us  [local(): jnp.where(slots[:, None] | (jnp.arange(128) != HDIM)[None, :], 0.0, -1e+30)]
    mul x2 -> x0, local copies, waits for them, and re-layouts: 11.6 us -> none  [local(): g * coef]
    pallas_call x1, Pallas kernels: 288 us -> 277 us  [backward_all(): pl.pallas_call(functools.partial(backward_all_kernel, times), out_shape=(...]
    reduce_sum x11 -> x0, other arithmetic: 10.2 us -> none  [the longest x1 1.68 us: local(): jnp.sum(pixels * live)]
    reshape x4 -> x0, local copies, waits for them, and re-layouts: 9 us -> none  [the longest x2 6.72 us: local(): units = wide_low.reshape(L, shard, 2, 4, D).transpose(0, 2, 3, 1, 4)]
    unnamed x41 -> x37, local copies, waits for them, and re-layouts: 1.18 us -> 9.26 us
where the time goes in v3:
time: 552 us; the launch traced here: 543 us
  Pallas kernels  514 us (93%)
  local copies, waits for them, and re-layouts  21 us (4%)
    pallas_call x1, Pallas kernels, backward_all(): pl.pallas_call(functools.partial(backward_all_kernel, times), out_shape=(...  277 us
    pallas_call x1, Pallas kernels, forward_all(): pl.pallas_call(functools.partial(forward_all_kernel, times), out_shape=tu...  211 us
    pallas_call x1, Pallas kernels, update(): pl.pallas_call(update_kernel, grid=(WIDE_STEPS + DOWN_STEPS,), out_shape=...  25.3 us

profile of v3, /device:TPU:0, one launch (start us, length us, event | category | flops | bytes accessed | tf_op | source)
XLA Modules:
  0.0 543.3 jit_solution(1652173738121105661)
XLA Ops:
  0.7 0.0 copy-start.9
  0.7 0.0 copy-start.2
  0.7 0.0 copy-start.13
  0.7 0.0 copy-start.14
  0.7 1.0 reshape.143
  1.8 0.6 pad.32.pkeep
  2.5 0.6 pad.33.psend
  3.1 0.7 broadcast_compare_fusion
  3.8 0.1 gt.11
  3.9 0.1 tile.38
  4.1 0.1 broadcast_and_fusion
  4.1 0.1 broadcast_in_dim.49
  4.2 0.1 pad.38.clone
  4.3 0.1 add_add_fusion
  4.4 0.1 or.19
  4.5 1.0 select_convert_fusion.mask
  5.5 0.1 tile.32
  5.6 0.1 tile.35
  5.7 0.1 rev.3
  5.8 0.8 copy.71.live
  6.6 1.1 slice.41
  7.7 0.2 copy.65
  7.9 0.1 reshape.140
  8.0 0.1 copy.66
  8.1 0.7 fusion.9
  8.8 0.1 pad.47.clone
  8.9 0.2 fusion.3
  9.2 0.1 copy.69
  9.3 0.0 copy-done.2
  9.3 0.0 copy-done.9
  9.3 0.1 copy.70
  9.5 0.1 pad.43.clone
  9.5 0.7 fusion.5.uemb
  10.3 0.6 slice.55.uclass
  10.9 1.6 fusion.6.upatch
  12.5 0.0 copy-done.13
  12.5 0.6 pad.34.labels
  13.1 0.0 copy-done.14
  13.2 0.6 pad.35.class_bias
  13.7 211.4 %forward_all.1 = (bf16[4,2,2,4,2,96,768]{6,5,4,3,2,1,0:T(8,128)(2,1)}, bf16[2,4,2,2,192,768]{5,4,3,2,1,0:T(8,128)(2,1)}, f32[384,768]{1,0:T(8,128)}, f32[5,320,7...) custom-call(f32[2,96,6144]{2,1,0:T(8,128)} %refs_4_.1, ...), custom_call_target="tpu_custom_call" | custom-call | tf_op jit(solution)/shard_map/forward_all/pallas_call | solution.py:675
  225.1 0.0 copy-start.15
  225.1 0.0 copy-start.16
  225.2 0.0 copy-start.11
  225.2 0.0 copy-start.12
  225.2 276.9 %backward_all.1 = (bf16[4,2,2,96,768]{4,3,2,1,0:T(8,128)(2,1)}, bf16[2,2,192,768]{3,2,1,0:T(8,128)(2,1)}, bf16[2,2,2,96,640]{4,3,2,1,0:T(8,128)(2,1)}, f32[3,8,128]{2,1,0:T(8,128)}, bf16[2,7,320,768]{3,2,1,0:T(8,128)(2,1)}) custom-call(f32[320,768]{1,0:T(8,128)} %get-tuple-element.60.dout_in, f32[5,320,768]{2,1,0:T(8,128)} %get-tuple-element.61.xs_in, ...), custom_call_target="tpu_custom_call" | custom-call | tf_op jit(solution)/shard_map/backward_all/pallas_call | solution.py:1369
  502.1 0.7 slice_bitcast_fusion.1
  502.8 1.2 fusion.11
  504.0 0.0 copy-done.15
  504.0 0.0 copy-done.16
  504.0 1.3 divide_subtract_fusion
  505.3 0.0 copy-done.11
  505.3 0.0 copy-done.12
  505.3 1.1 copy-done
  506.4 1.3 copy-done.1
  507.6 0.9 copy-done.3
  508.6 1.2 copy-done.4
  509.8 1.1 copy-done.5
  510.8 1.1 copy-done.6
  511.9 0.9 copy-done.7
  512.9 0.9 copy-done.8
  513.8 0.7 copy-done.10
  514.5 25.3 %update.1 = (f32[2,96,6144]{2,1,0:T(8,128)}, f32[2,384,768]{2,1,0:T(8,128)}, f32[96,1504]{1,0:T(8,128)}, f32[96,527]{1,0:T(8,128)}, f32[29,96]{1,0:T(8,128)}, /*...) custom-call(f32[3,8,128]{2,1,0:T(8,128)S(1)} %copy-done.10, ...), custom_call_target="tpu_custom_call" | custom-call | tf_op jit(solution)/shard_map/update/pallas_call | solution.py:1505
  539.8 0.6 slice.52
  540.4 0.7 reduce_sum.9
  (41 shorter events, 0.3 us)
Async XLA Ops:
  0.7 8.7 %copy-start.9 = (f32[29,96]{1,0:T(8,128)S(1)}, f32[29,96]{1,0:T(8,128)}, u32[]{:S(2)}) copy-start(f32[29,96]{1,0:T(8,128)} %refs_8_.1) | copy-start | bytes 33412
  0.7 8.6 %copy-start.2 = (f32[96,527]{1,0:T(8,128)S(1)}, f32[96,527]{1,0:T(8,128)}, u32[]{:S(2)}) copy-start(f32[96,527]{1,0:T(8,128)} %refs_7_.1) | copy-start | bytes 607108
  0.7 11.8 %copy-start.13 = (s32[8,527]{1,0:T(8,128)S(1)}, s32[8,527]{1,0:T(8,128)}, u32[]{:S(2)}) copy-start(s32[8,527]{1,0:T(8,128)} %param.24) | copy-start | bytes 50596
  0.7 12.4 %copy-start.14 = (f32[527]{0:T(1024)S(1)}, f32[527]{0:T(1024)}, u32[]{:S(2)}) copy-start(f32[527]{0:T(1024)} %param.31) | copy-start | bytes 6328
  225.1 278.9 %copy-start.15 = (f32[527]{0:T(1024)S(1)}, f32[527]{0:T(1024)}, u32[]{:S(2)}) copy-start(f32[527]{0:T(1024)} %param.37) | copy-start | bytes 6328
  225.1 278.9 %copy-start.16 = (f32[527]{0:T(1024)S(1)}, f32[527]{0:T(1024)}, u32[]{:S(2)}) copy-start(f32[527]{0:T(1024)} %param.43) | copy-start | bytes 6328
  225.2 280.1 %copy-start.11 = (f32[29,96]{1,0:T(8,128)S(1)}, f32[29,96]{1,0:T(8,128)}, u32[]{:S(2)}) copy-start(f32[29,96]{1,0:T(8,128)} %refs_13_.1) | copy-start | bytes 33412
  225.2 280.1 %copy-start.12 = (f32[29,96]{1,0:T(8,128)S(1)}, f32[29,96]{1,0:T(8,128)}, u32[]{:S(2)}) copy-start(f32[29,96]{1,0:T(8,128)} %refs_18_.1) | copy-start | bytes 33412
  505.3 1.1 copy-start
  506.4 1.3 copy-start.1
  507.6 0.9 copy-start.3
  508.6 1.2 copy-start.4
  509.8 1.1 copy-start.5
  510.8 1.1 copy-start.6
  511.9 0.9 copy-start.7
  512.8 0.9 copy-start.8
  513.8 0.7 copy-start.10
  514.5 25.9 %copy-start.17 = (s32[8]{0:T(128)S(1)}, s32[8]{0:T(128)}, u32[]{:S(2)}) copy-start(s32[8]{0:T(128)} %param.25) | copy-start | bytes 100

commit v4 on v3

--- a/solution.py
+++ b/solution.py
@@ -788,7 +788,7 @@
         for i in range(1, NF):
             to_clip(j, i).wait_recv()
 
-        def attend(s, carry):
+        def attend(s):
             q = with_mask(qk_ref[j, s, :TOK])
             dmix = open_half(drecv[j, s])
             scores = nt(kall[...], q)
@@ -801,9 +801,11 @@
             dvall[...] += nn(probs.astype(BF), dmix)
             dkall[...] += nn(dscore, q[:, :HDIM])
             dqall[s] = (tn(dscore, kall[:, :HDIM]) * root).astype(BF)
-            return carry
-
-        lax.fori_loop(0, NF, attend, 0)
+
+        for s in range(NF):
+            attend(s)
+            if s < NF - 1:
+                at("head%d%d" % (j, s))
         for s in range(NF):
             span = slice(s * TOK, (s + 1) * TOK)
             gsend[j, s, :TOK] = jnp.concatenate([dqall[s], dkall[span].astype(BF)], 1)
@@ -811,7 +813,7 @@
         for i in range(1, NF):
             back_clip(j, i).start()
         grecv[j, f] = gsend[j, f]
-        at("head%d" % j)
+        at("head%d%d" % (j, NF - 1))
     for j in range(PER):
         for i in range(1, NF):
             back_clip(j, i).wait_recv()
@@ -880,9 +882,38 @@
 
 
 RGROUPS = (("d", 1), ("u", 1), ("q", 1), ("d", 0), ("u", 0), ("q", 0))
-RFIRST = ("xx", "yx", "xx", "yx", "yx", "xx")
+ROUTES = ("zz", "xz", "zy", "yz", "xz", "yy")
+ORDER = {
+    (1, "mlp1"): (0,),
+    (1, "mlp3"): (200,),
+    (1, "head00"): (1,),
+    (1, "head01"): (200, 100,),
+    (1, "head03"): (200,),
+    (1, "head10"): (10, 200,),
+    (1, "head13"): (101,),
+    (1, "head20"): (100,),
+    (1, "head22"): (11,),
+    (1, "head23"): (100,),
+    (1, "heads"): (100, 101, 110,),
+    (1, "done"): (100, 101, 20, 111, 21,),
+    (0, "mlp0"): (110,),
+    (0, "mlp1"): (101,),
+    (0, "mlp2"): (101,),
+    (0, "sent"): (111,),
+    (0, "head00"): (110, 120, 121, 30, 111, 31, 110,),
+    (0, "head02"): (110,),
+    (0, "head03"): (121,),
+    (0, "head12"): (120,),
+    (0, "head13"): (130,),
+    (0, "head20"): (111,),
+    (0, "head21"): (121, 131, 111,),
+    (0, "head23"): (120, 40, 130,),
+    (0, "heads"): (120, 121, 131, 41, 140, 120,),
+    (0, "done"): (121, 130, 131, 50,),
+    "end": (140, 130, 131, 130, 131, 141, 51, 140, 150, 210, 141, 150, 151, 140, 210, 141, 140, 210, 151, 141, 150, 210, 141, 150, 150, 151, 151, 151,),
+}
 SLOTS_R = 2
-BUFS = 2
+BUFS = 1
 PWIDE = (CMAIN, EWIDE + PATCH)
 STAGES = 5
 
@@ -978,7 +1009,7 @@
         return tn(lbuf[left, :TOK], own(cols)) + tn(lbuf[left, TOK:], other(cols))
 
     def store(gi, h, role, xx, where, value):
-        if RFIRST[gi][h] == "y":
+        if ROUTES[gi][h] == "y":
             keep, index = role == 0, xx
         else:
             keep, index = x == xx, role
@@ -1027,20 +1058,28 @@
     def step1(gi, h):
         return remote(
             low.at[gi % BUFS, h], recv1.at[gi % SLOTS_R, h], s1.at[gi, h], r1.at[gi, h],
-            over_y if RFIRST[gi][h] == "y" else over_x,
+            over_y if ROUTES[gi][h] == "y" else over_x,
         )
 
     def step2(gi, h):
+        if ROUTES[gi][h] == "z":
+            src, dst = zlow.at[h, 0], recv2.at[gi % SLOTS_R, h, count - 1]
+        else:
+            src, dst = mid_low.at[h], recv2.at[gi % SLOTS_R, h]
         return remote(
-            mid_low.at[h], recv2.at[gi % SLOTS_R, h], s2.at[gi, h], r2.at[gi, h],
-            over_x if RFIRST[gi][h] == "y" else over_y,
-        )
-
-    def along(gi, h, dz):
-        return remote(
-            zlow.at[h, (g + dz) % count], zrecv.at[gi % SLOTS_R, h, dz - 1],
-            zs.at[gi, h, dz - 1], zr.at[gi, h, dz - 1], (f, ((g + dz) % count) * 2 + x),
-        )
+            src, dst, s2.at[gi, h], r2.at[gi, h], over_x if ROUTES[gi][h] == "y" else over_y
+        )
+
+    def along(gi, h, dz, role=0):
+        to = (g + dz) % count
+        slot = gi % SLOTS_R
+        if ROUTES[gi][h] != "z":
+            src, dst = zlow.at[h, to], zrecv.at[slot, h, dz - 1]
+        elif role == 0:
+            src, dst = mid_low.at[h, to], zrecv.at[slot, h, dz - 1]
+        else:
+            src, dst = zlow.at[h, to], recv2.at[slot, h, dz - 1]
+        return remote(src, dst, zs.at[gi, h, role, dz - 1], zr.at[gi, h, role, dz - 1], (f, to * 2 + x))
 
     def result(gi, h, yy):
         kind, l = RGROUPS[gi]
@@ -1056,35 +1095,69 @@
         block = result(gi, h, slice(None))
         return remote(block, block, ks.at[gi, h], kr.at[gi, h], over_c)
 
+    def wait_along(gi, h):
+        for role in range(2 if ROUTES[gi][h] == "z" else 1):
+            for dz in range(1, count):
+                along(gi, h, dz, role).wait_recv()
+                along(gi, h, dz, role).wait_send()
+
+    def start_along(gi, h):
+        for dz in range(1, count):
+            if gi >= SLOTS_R:
+                pl.semaphore_wait(credit.at[1 + dz], 1)
+            for role in range(2 if ROUTES[gi][h] == "z" else 1):
+                along(gi, h, dz, role).start()
+
     def advance(gi, h, stage):
         slot, buf = gi % SLOTS_R, gi % BUFS
+        twice = ROUTES[gi][h] == "z"
         if stage == 1:
             step1(gi, h).wait_recv()
             step1(gi, h).wait_send()
-            keep, send = (x, 1 - x) if RFIRST[gi][h] == "y" else (0, 1)
+            if twice:
+                summed = full[buf, h, 0] + recv1[slot, h, 0].astype(F32)
+                mid_low[h] = summed.astype(BF)
+                mid_own[h] = summed
+                summed = full[buf, h, 1] + recv1[slot, h, 1].astype(F32)
+                zlow[h] = summed.astype(BF)
+                start_along(gi, h)
+                full[buf, h, 1] = summed
+                zown[h] = full[buf, h, 1, g]
+                return
+            keep, send = (x, 1 - x) if ROUTES[gi][h] == "y" else (0, 1)
             mid_low[h] = (full[buf, h, send] + recv1[slot, h, send].astype(F32)).astype(BF)
             step2(gi, h).start()
             mid_own[h] = full[buf, h, keep] + recv1[slot, h, keep].astype(F32)
         elif stage == 2:
+            if twice:
+                wait_along(gi, h)
+                value = zown[h]
+                for dz in range(1, count):
+                    value = value + recv2[slot, h, dz - 1].astype(F32)
+                zlow[h, 0] = value.astype(BF)
+                step2(gi, h).start()
+                value = mid_own[h, g]
+                for dz in range(1, count):
+                    value = value + zrecv[slot, h, dz - 1].astype(F32)
+                zown[h] = value
+                return
             step2(gi, h).wait_recv()
             step2(gi, h).wait_send()
             summed = mid_own[h] + recv2[slot, h].astype(F32)
             zlow[h] = summed.astype(BF)
+            start_along(gi, h)
             mid_own[h] = summed
-            for dz in range(1, count):
-                if gi >= SLOTS_R:
-                    pl.semaphore_wait(credit.at[1 + dz], 1)
-                along(gi, h, dz).start()
             zown[h] = mid_own[h, g]
-            if gi + SLOTS_R < total:
-                pl.semaphore_signal(credit.at[0], inc=1, device_id=over_x, device_id_type=MESH)
-                pl.semaphore_signal(credit.at[1], inc=1, device_id=over_y, device_id_type=MESH)
         elif stage == 3:
             value = zown[h]
-            for dz in range(1, count):
-                along(gi, h, dz).wait_recv()
-                along(gi, h, dz).wait_send()
-                value = value + zrecv[slot, h, dz - 1].astype(F32)
+            if twice:
+                step2(gi, h).wait_recv()
+                step2(gi, h).wait_send()
+                value = value + recv2[slot, h, count - 1].astype(F32)
+            else:
+                wait_along(gi, h)
+                for dz in range(1, count):
+                    value = value + zrecv[slot, h, dz - 1].astype(F32)
             sq[...] += jnp.sum((value * value).reshape(12, 8, 3, 128), (0, 2))
             kind, l = RGROUPS[gi]
             if kind == "d":
@@ -1092,13 +1165,15 @@
             else:
                 idx = 2 * l + (1 if kind == "u" else 0)
                 gcol[idx, y, c, :, h * 384 : (h + 1) * 384] = value.astype(BF)
+            spread_y(gi, h).start()
             if gi + SLOTS_R < total:
+                pl.semaphore_signal(credit.at[0], inc=1, device_id=over_x, device_id_type=MESH)
+                pl.semaphore_signal(credit.at[1], inc=1, device_id=over_y, device_id_type=MESH)
                 for dz in range(1, count):
                     back = (f, ((g + count - dz) % count) * 2 + x)
                     pl.semaphore_signal(
                         credit.at[1 + dz], inc=1, device_id=back, device_id_type=MESH
                     )
-            spread_y(gi, h).start()
         elif stage == 4:
             spread_y(gi, h).wait_recv()
             spread_c(gi, h).start()
@@ -1181,48 +1256,36 @@
             value = jnp.where(f == 0, value * value, 0.0)
             sq[...] += jnp.sum(value.reshape(12, 8, PWIDE[n] // 128, 128), (0, 2))
 
-    under_way = []
-
-    def tick():
-        for entry in list(under_way):
-            after = entry[3] + 1
-            if entry[0] == "group" and after < 3 and stage_of("group", entry[1] - 1, entry[2]) <= after:
-                continue
-            entry[3] = after
-            if entry[0] == "part":
-                part_advance(entry[1], entry[3])
-            else:
-                advance(entry[1], entry[2], entry[3])
-            if entry[3] == (STAGES if entry[0] == "group" else STAGES - 1):
-                under_way.remove(entry)
-
-    def stage_of(kind, n, h=0):
-        for entry in under_way:
-            if entry[:3] == [kind, n, h]:
-                return entry[3]
-        return STAGES
-
-    def launch(gi):
-        for n in swaps(gi):
-            swap(gi, n).wait_recv()
-        for copy in left_loads(gi):
-            copy.wait()
-        for h in range(2):
-            hs = range(2) if RGROUPS[gi][0] == "d" else (h,)
-            while any(gi >= BUFS and stage_of("group", gi - BUFS, i) < 1 for i in hs):
-                tick()
-            while gi >= SLOTS_R and stage_of("group", gi - SLOTS_R, h) < 2:
-                tick()
-            compute(gi, h)
-            if gi >= SLOTS_R:
-                pl.semaphore_wait(credit.at[0], 1)
-                pl.semaphore_wait(credit.at[1], 1)
-            step1(gi, h).start()
-            under_way.append(["group", gi, h, 0])
-        for n in swaps(gi):
-            swap(gi, n).wait_send()
-        if gi + 1 < total:
-            prepare(gi + 1)
+    stages = {}
+
+    def launch(gi, h):
+        if h == 0:
+            for n in swaps(gi):
+                swap(gi, n).wait_recv()
+            for copy in left_loads(gi):
+                copy.wait()
+        compute(gi, h)
+        if gi >= SLOTS_R:
+            pl.semaphore_wait(credit.at[0], 1)
+            pl.semaphore_wait(credit.at[1], 1)
+        step1(gi, h).start()
+        stages[gi, h] = 0
+        if h == 1:
+            for n in swaps(gi):
+                swap(gi, n).wait_send()
+            if gi + 1 < total:
+                prepare(gi + 1)
+
+    def perform(op):
+        what, gi, h = op // 100, op // 10 % 10, op % 10
+        if what == 0:
+            launch(gi, h)
+            return
+        stages[gi, h if what == 1 else 2] += 1
+        if what == 1:
+            advance(gi, h, stages[gi, h])
+        else:
+            part_advance(gi, stages[gi, 2])
 
     waited = set()
 
@@ -1237,7 +1300,7 @@
 
     def launch_part(n):
         part_compute(n)
-        under_way.append(["part", n, 0, 0])
+        stages[n, 2] = 0
 
     load_mask(mask, scratch[4])
     sq[...] = jnp.zeros_like(sq)
@@ -1284,8 +1347,6 @@
                     weight(layer, 2).start()
                     if layer > 0:
                         weight(layer - 1, 0).start()
-                if k % 2:
-                    tick()
             elif point == "resid":
                 kept_load(layer, 0).start()
                 if layer == L - 1:
@@ -1293,24 +1354,18 @@
             elif point == "sent":
                 if layer < L - 1:
                     heads_load(layer).wait()
-                launch(base)
-            elif point == "head0":
-                launch(base + 1)
-            elif point == "head1":
-                tick()
-            elif point == "head2":
-                tick()
+            elif point == "head%d%d" % (PER - 1, NF - 1):
                 if layer > 0:
                     heads_load(layer - 1).start()
             elif point == "heads":
                 for n in swaps(base + 2):
                     swap(base + 2, n).start()
-                tick()
             elif point == "done":
                 if layer > 0:
                     weight(layer - 1, 1).start()
                     kept_load(layer - 1, 1).start()
-                    launch(base + 2)
+            for op in ORDER.get((layer, point), ()):
+                perform(op)
 
         backward_body(
             layer, dcur, er, ba, vec_ref, qk, (mat(0), mat(1), mat(2)), slope, kept, scratch,
@@ -1323,11 +1378,11 @@
     er[EVEC + GLOB : EVEC + GLOB + 1, :] = jnp.sum(inside, 0, keepdims=True)
     er[EVEC + GLOB + 1 : EVEC + GLOB + 3, :] = dgrid[GRID : GRID + 2, :]
     launch_part(1)
-    launch(total - 1)
     shared = False
-    while under_way:
-        tick()
-        if not shared and stage_of("group", total - 1, 1) >= 3 and stage_of("part", 1) >= STAGES - 1:
+    for op in ORDER["end"]:
+        perform(op)
+        summed = all(stages.get((gi, h), 0) >= 3 for gi in range(total) for h in range(2))
+        if not shared and summed and stages[0, 2] == stages[1, 2] == STAGES - 1:
             shared = True
             n = NF * times
             me = f * times + t
@@ -1339,6 +1394,8 @@
 
             lax.fori_loop(1, n, send, 0)
             square_all[me] = sq[...]
+    if not shared or any(stages[gi, h] < STAGES for gi in range(total) for h in range(2)):
+        raise ValueError("incomplete order")
     for layer in range(L):
         for n in range(2):
             forward_swap(layer, n).wait_send()
@@ -1406,7 +1463,7 @@
             dma((L, 3)), dma((L, 4)), dma((L, 2)), dma((L + 1,)), dma((4, 2)),
             dma((L, 2)), dma((L, 2)), dma((total, 2)), dma((total, 2)),
             dma((total, 2)), dma((total, 2)), dma((total, 2)), dma((total, 2)),
-            dma((total, 2, count - 1)), dma((total, 2, count - 1)),
+            dma((total, 2, 2, count - 1)), dma((total, 2, 2, count - 1)),
             dma((total, 2)), dma((total, 2)), dma((total, 2)), dma((total, 2)),
             dma, dma, dma, dma,
             dma((2,)), dma((2,)), dma((2, count - 1)), dma((2, count - 1)), dma((2,)), dma((2,)), dma((2,)), dma((2,)),

time: 552 us -> 498 us (0.902)
  Pallas kernels: 514 us -> 460 us
    pallas_call x1, Pallas kernels: 277 us -> 223 us  [backward_all(): pl.pallas_call(functools.partial(backward_all_kernel, times), out_shape=(...]
where the time goes in v4:
time: 498 us; the launch traced here: 489 us
  Pallas kernels  460 us (92%)
  local copies, waits for them, and re-layouts  21 us (4%)
  other arithmetic  5.46 us (1%)
    pallas_call x1, Pallas kernels, backward_all(): pl.pallas_call(functools.partial(backward_all_kernel, times), out_shape=(...  223 us
    pallas_call x1, Pallas kernels, forward_all(): pl.pallas_call(functools.partial(forward_all_kernel, times), out_shape=tu...  211 us
    pallas_call x1, Pallas kernels, update(): pl.pallas_call(update_kernel, grid=(WIDE_STEPS + DOWN_STEPS,), out_shape=...  25.3 us

profile of v4, /device:TPU:0, one launch (start us, length us, event | category | flops | bytes accessed | tf_op | source)
XLA Modules:
  0.0 489.2 jit_solution(16044406590217696367)
XLA Ops:
  0.7 0.0 copy-start.9
  0.7 0.0 copy-start.2
  0.7 0.0 copy-start.13
  0.7 0.0 copy-start.14
  0.7 1.0 reshape.143
  1.8 0.6 pad.32.pkeep
  2.5 0.6 pad.33.psend
  3.1 0.7 broadcast_compare_fusion
  3.8 0.1 gt.11
  3.9 0.1 tile.38
  4.1 0.1 broadcast_and_fusion
  4.1 0.1 broadcast_in_dim.49
  4.2 0.1 pad.38.clone
  4.3 0.1 add_add_fusion
  4.4 0.1 or.19
  4.5 1.0 select_convert_fusion.mask
  5.5 0.1 tile.32
  5.6 0.1 tile.35
  5.7 0.1 rev.3
  5.8 0.8 copy.71.live
  6.6 1.1 slice.41
  7.7 0.2 copy.65
  7.9 0.1 reshape.140
  8.0 0.1 copy.66
  8.1 0.7 fusion.9
  8.8 0.1 pad.47.clone
  8.9 0.2 fusion.3
  9.2 0.1 copy.69
  9.3 0.0 copy-done.2
  9.3 0.0 copy-done.9
  9.3 0.1 copy.70
  9.5 0.1 pad.43.clone
  9.5 0.7 fusion.5.uemb
  10.3 0.6 slice.55.uclass
  10.9 1.6 fusion.6.upatch
  12.5 0.0 copy-done.13
  12.5 0.6 pad.34.labels
  13.1 0.0 copy-done.14
  13.2 0.6 pad.35.class_bias
  13.7 211.4 %forward_all.1 = (bf16[4,2,2,4,2,96,768]{6,5,4,3,2,1,0:T(8,128)(2,1)}, bf16[2,4,2,2,192,768]{5,4,3,2,1,0:T(8,128)(2,1)}, f32[384,768]{1,0:T(8,128)}, f32[5,320,7...) custom-call(f32[2,96,6144]{2,1,0:T(8,128)} %refs_4_.1, ...), custom_call_target="tpu_custom_call" | custom-call | tf_op jit(solution)/shard_map/forward_all/pallas_call | solution.py:675
  225.2 0.0 copy-start.15
  225.2 0.0 copy-start.16
  225.2 0.0 copy-start.11
  225.2 0.0 copy-start.12
  225.2 222.8 %backward_all.1 = (bf16[4,2,2,96,768]{4,3,2,1,0:T(8,128)(2,1)}, bf16[2,2,192,768]{3,2,1,0:T(8,128)(2,1)}, bf16[2,2,2,96,640]{4,3,2,1,0:T(8,128)(2,1)}, f32[3,8,128]{2,1,0:T(8,128)}, bf16[2,7,320,768]{3,2,1,0:T(8,128)(2,1)}) custom-call(f32[320,768]{1,0:T(8,128)} %get-tuple-element.60.dout_in, f32[5,320,768]{2,1,0:T(8,128)} %get-tuple-element.61.xs_in, ...), custom_call_target="tpu_custom_call" | custom-call | tf_op jit(solution)/shard_map/backward_all/pallas_call | solution.py:1426
  448.0 0.7 slice_bitcast_fusion.1
  448.7 1.2 fusion.11
  449.9 0.0 copy-done.15
  449.9 0.0 copy-done.16
  449.9 1.3 divide_subtract_fusion
  451.2 0.0 copy-done.11
  451.2 1.1 copy-done
  452.3 1.3 copy-done.1
  453.5 0.9 copy-done.3
  454.5 1.2 copy-done.4
  455.7 1.1 copy-done.5
  456.7 1.1 copy-done.6
  457.8 0.9 copy-done.7
  458.8 0.9 copy-done.8
  459.7 0.7 copy-done.10
  460.4 25.3 %update.1 = (f32[2,96,6144]{2,1,0:T(8,128)}, f32[2,384,768]{2,1,0:T(8,128)}, f32[96,1504]{1,0:T(8,128)}, f32[96,527]{1,0:T(8,128)}, f32[29,96]{1,0:T(8,128)}, /*...) custom-call(f32[3,8,128]{2,1,0:T(8,128)S(1)} %copy-done.10, ...), custom_call_target="tpu_custom_call" | custom-call | tf_op jit(solution)/shard_map/update/pallas_call | solution.py:1562
  485.7 0.6 slice.52
  486.3 0.0 copy-done.17
  486.3 0.7 reduce_sum.9
  (41 shorter events, 0.3 us)
Async XLA Ops:
  0.7 8.7 %copy-start.9 = (f32[29,96]{1,0:T(8,128)S(1)}, f32[29,96]{1,0:T(8,128)}, u32[]{:S(2)}) copy-start(f32[29,96]{1,0:T(8,128)} %refs_8_.1) | copy-start | bytes 33412
  0.7 8.6 %copy-start.2 = (f32[96,527]{1,0:T(8,128)S(1)}, f32[96,527]{1,0:T(8,128)}, u32[]{:S(2)}) copy-start(f32[96,527]{1,0:T(8,128)} %refs_7_.1) | copy-start | bytes 607108
  0.7 11.8 %copy-start.13 = (s32[8,527]{1,0:T(8,128)S(1)}, s32[8,527]{1,0:T(8,128)}, u32[]{:S(2)}) copy-start(s32[8,527]{1,0:T(8,128)} %param.24) | copy-start | bytes 50596
  0.7 12.4 %copy-start.14 = (f32[527]{0:T(1024)S(1)}, f32[527]{0:T(1024)}, u32[]{:S(2)}) copy-start(f32[527]{0:T(1024)} %param.31) | copy-start | bytes 6328
  225.2 224.8 %copy-start.15 = (f32[527]{0:T(1024)S(1)}, f32[527]{0:T(1024)}, u32[]{:S(2)}) copy-start(f32[527]{0:T(1024)} %param.37) | copy-start | bytes 6328
  225.2 224.8 %copy-start.16 = (f32[527]{0:T(1024)S(1)}, f32[527]{0:T(1024)}, u32[]{:S(2)}) copy-start(f32[527]{0:T(1024)} %param.43) | copy-start | bytes 6328
  225.2 226.0 %copy-start.11 = (f32[29,96]{1,0:T(8,128)S(1)}, f32[29,96]{1,0:T(8,128)}, u32[]{:S(2)}) copy-start(f32[29,96]{1,0:T(8,128)} %refs_13_.1) | copy-start | bytes 33412
  225.2 226.0 %copy-start.12 = (f32[29,96]{1,0:T(8,128)S(1)}, f32[29,96]{1,0:T(8,128)}, u32[]{:S(2)}) copy-start(f32[29,96]{1,0:T(8,128)} %refs_18_.1) | copy-start | bytes 33412
  451.2 1.1 copy-start
  452.3 1.3 copy-start.1
  453.5 0.9 copy-start.3
  454.5 1.2 copy-start.4
  455.7 1.1 copy-start.5
  456.7 1.1 copy-start.6
  457.8 0.9 copy-start.7
  458.8 0.9 copy-start.8
  459.7 0.7 copy-start.10
  460.4 25.9 %copy-start.17 = (s32[8]{0:T(128)S(1)}, s32[8]{0:T(128)}, u32[]{:S(2)}) copy-start(s32[8]{0:T(128)} %param.25) | copy-start | bytes 100
